TPU v7x, 512 devices: a whole 4x4x16 slice. The times are simulated.
512 devices in a mesh: blk: 16 (over z_hi, x, core), grp: 32 (over y, z_lo).
Axes of the slice: x: 4, y: 4, z: 16 (z_hi: 2, z_lo: 8; z = z_hi * 8 + z_lo), core: 2. Of those that a mesh axis runs over, the one named last changes fastest.
Arguments:
- picture_vectors: bfloat16 [98304, 640], P(('blk', 'grp')), may hold values from -0.23925781 to 0.23925781
- caption_vectors: bfloat16 [98304, 640], P(('blk', 'grp')), may hold values from -0.23925781 to 0.23925781
- picture_match_label: int32 [98304], P(('blk', 'grp')), may hold values from 0 to 255
- caption_match_label: int32 [98304], P(('blk', 'grp')), may hold values from 0 to 255
- inverse_softness: float32 [1], replicated, may hold values from 6 to 16
- score_offset: float32 [1], replicated, may hold values from -3 to -1
Outputs:
- image_grad: bfloat16 [98304, 640], P(('blk', 'grp'))
- text_grad: float32 [98304, 640], P(('blk', 'grp'))
Inputs may be any that keep to these rules, and one draw needn't show every extreme that they name: `picture_match_label`: pair ids; an image and a text form a positive pair when their ids are equal. `caption_match_label`: pair ids, as for the images.
All inputs are finite; a program needn't handle non-finite values.
Results may differ from a plain program's by a relative error of at most 0.0034.
Values may be sent and summed in bfloat16 or wider, within the bound.
No kernel may reach another device: no remote copies, remote signals or barrier semaphores. Data moves between devices by JAX's collectives and lax.ppermute only.
A program may use at most 64 MiB of HBM per device.

v0:
```python
import jax
import jax.numpy as jnp
from jax import lax
from jax.sharding import PartitionSpec as P


def shifted(block, axis, distance):
    devices = range(lax.axis_size(axis))
    route = [((i - distance) % len(devices), i) for i in devices]
    return lax.ppermute(block, axis, route)


def pair_weights(left_rows, left_pair_index, right_rows, right_ids, score_factor, logit_bias):
    scores = (
        jnp.dot(left_rows, right_rows.T, preferred_element_type=jnp.float32) * score_factor
        + logit_bias
    )
    positive = (left_pair_index[:, None] == right_ids[None, :]).astype(jnp.float32)
    return ((jax.nn.sigmoid(scores) - positive) / 8.0).astype(jnp.bfloat16)


def fold_rows(received, piece):
    return lax.dot_general(
        received, piece, (((0,), (0,)), ((), ())), preferred_element_type=jnp.float32
    )


def body(
    picture_vectors,
    caption_vectors,
    picture_match_label,
    caption_match_label,
    inverse_softness,
    score_offset,
):
    score_factor = inverse_softness[0]
    logit_bias = score_offset[0]
    moved_texts, moved_tids = shifted((caption_vectors, caption_match_label), "blk", 1)
    block_texts, block_tids = (
        lax.all_gather(moved_texts, "grp", axis=0, tiled=True),
        lax.all_gather(moved_tids, "grp", axis=0, tiled=True),
    )
    weight = pair_weights(
        picture_vectors, picture_match_label, block_texts, block_tids, score_factor, logit_bias
    )
    image_grad = (
        score_factor * jnp.dot(weight, block_texts, preferred_element_type=jnp.float32)
    ).astype(jnp.bfloat16)
    received = lax.all_to_all(weight, "grp", split_axis=1, concat_axis=0, tiled=True)
    summed = fold_rows(received, lax.all_gather(picture_vectors, "grp", axis=0, tiled=True))
    visiting_grad = score_factor * summed
    text_grad = shifted(visiting_grad, "blk", -1)
    return (image_grad, text_grad)


def solution(mesh):
    placed = (
        P(("blk", "grp"), None),
        P(("blk", "grp"), None),
        P(("blk", "grp")),
        P(("blk", "grp")),
        P(),
        P(),
    )
    return jax.shard_map(
        body,
        mesh=mesh,
        in_specs=placed,
        out_specs=(P(("blk", "grp"), None), P(("blk", "grp"), None)),
        check_vma=False,
    )
```

profile of v0, /device:TPU:31, one launch (start us, length us, event | category | flops | bytes accessed | tf_op | source)
XLA Modules:
  0.0 661.8 jit_solution(9621937452583764391)
XLA Ops:
  7.2 0.0 all-gather.3.cloned.1.call-start
  7.2 15.9 %collective-permute-start = (bf16[192,640]{1,0:T(8,128)(2,1)}, bf16[192,640]{1,0:T(8,128)(2,1)S(1)}, u32[]{:S(2)}, u32[]{:S(2)}) collective-permute-start(bf16[192,640]{1,0:T(8,128)(2,1)} %param.7), channel_id=1, source_target_pairs={{480,0},{0,32},{32,64},{64,96},{96,128},{128,160},{160,192},{192,2... | collective-permute-start | bytes 737288 | tf_op jit(solution)/shard_map/ppermute | solution.py:10
  23.1 10.0 %collective-permute-done = bf16[192,640]{1,0:T(8,128)(2,1)S(1)} collective-permute-done((bf16[192,640]{1,0:T(8,128)(2,1)}, bf16[192,640]{1,0:T(8,128)(2,1)S(1)}, u32[]{:S(2)}, u32[]{:S(2)}) %collective-permute-start) | collective-permute-done | bytes 245792 | tf_op jit(solution)/shard_map/ppermute | solution.py:10
  33.2 0.0 copy-start.1
  33.2 0.7 copy-done.1
  33.9 0.0 all-gather.3.cloned.1.call-update
  33.9 0.0 all-gather.5.cloned.1.call-start
  33.9 0.7 all-gather.5.cloned.1.call-update
  34.6 15.2 %collective-permute-start.1 = (s32[192]{0:T(256)}, s32[192]{0:T(256)S(1)}, u32[]{:S(2)}, u32[]{:S(2)}) collective-permute-start(s32[192]{0:T(256)} %param.9), channel_id=1, source_target_pairs={{480,0},{0,32},{32,64},{64,96},{96,128},{128,160},{160,192},{192,2... | collective-permute-start | bytes 2312 | tf_op jit(solution)/shard_map/ppermute | solution.py:10
  51.2 1.3 dynamic-slice
  53.1 0.0 collective-permute-done.1
  53.1 0.3 dynamic-update-slice
  53.4 186.4 %all-reduce = s32[6144]{0:T(1024)S(1)} all-reduce(s32[6144]{0:T(1024)S(1)} %dynamic-update-slice), channel_id=1, replica_groups=mesh['blk'=16,'grp'=32] {'grp'}, use_global_device_ids=true, to_apply=%add | all-reduce | flops 6144 | bytes 49152
  239.8 14.8 %all-gather.3.cloned.1.call-done = bf16[6144,640]{1,0:T(8,128)(2,1)} async-done(((bf16[192,640]{1,0:T(8,128)(2,1)}), bf16[6144,640]{1,0:T(8,128)(2,1)}) %all-gather.3.cloned.1.call-update) | async-done | bytes 7864336 | tf_op jit(solution)/shard_map/all_gather | solution.py:40
  254.7 7.6 %fusion.7 = bf16[192,6144]{1,0:T(8,128)(2,1)} fusion(bf16[192,640]{1,0:T(8,128)(2,1)} %param.6, bf16[6144,640]{1,0:T(8,128)(2,1)} %all-gather.3.cloned.1.call-done, s32[6144]{0:T(1024)S(1)} %all-reduce, f32[]{:T(128)} %bitcast.16, f32[]{:T(128)} %bitcast.14, s32[192]{0:T(256)} %param.8), kind=kOutput, calls=%fused_computation.8 | convolution fusion | flops 1521745920 | bytes 10494728 | tf_op jit(solution)/shard_map/dot_general | solution.py:15
  262.3 3.0 copy.11
  265.3 218.0 %all_to_all.19 = bf16[192,32,192]{0,2,1:T(8,128)(2,1)S(1)} all-to-all(bf16[192,32,192]{0,2,1:T(8,128)(2,1)S(1)} %bitcast.18), channel_id=1, replica_groups=mesh['blk'=16,'grp'=32] {'grp'}, dimensions={1} | all-to-all | bytes 4718592 | tf_op jit(solution)/shard_map/all_to_all | solution.py:49
  483.3 1.8 copy.10
  485.1 4.2 all_to_all.17
  489.3 116.8 %all-gather.5.cloned.1.call-done = bf16[6144,640]{1,0:T(8,128)(2,1)} async-done(((bf16[192,640]{1,0:T(8,128)(2,1)}), bf16[6144,640]{1,0:T(8,128)(2,1)}) %all-gather.5.cloned.1.call-update) | async-done | bytes 7864336 | tf_op jit(solution)/shard_map/all_gather | solution.py:50
  606.1 0.0 copy-start
  606.1 6.1 convolution_multiply_fusion.1
  612.2 14.9 %collective-permute-start.2 = (f32[192,640]{1,0:T(8,128)S(1)}, f32[192,640]{1,0:T(8,128)S(1)}, u32[]{:S(2)}, u32[]{:S(2)}) collective-permute-start(f32[192,640]{1,0:T(8,128)S(1)} %convolution_multiply_fusion.1), channel_id=1, source_target_pairs={{32,0},{64,32},{96,64},{128,96},{160,128},{192,160},{224,192},{256... | collective-permute-start | bytes 1474568 | tf_op jit(solution)/shard_map/ppermute | solution.py:10
  627.1 0.0 copy-done
  627.1 6.0 fusion.8
  633.1 21.0 %collective-permute-done.2 = f32[192,640]{1,0:T(8,128)S(1)} collective-permute-done((f32[192,640]{1,0:T(8,128)S(1)}, f32[192,640]{1,0:T(8,128)S(1)}, u32[]{:S(2)}, u32[]{:S(2)}) %collective-permute-start.2) | collective-permute-done | bytes 491552 | tf_op jit(solution)/shard_map/ppermute | solution.py:10
  654.2 0.8 copy.16
  (1 shorter events, 0.0 us)
Async XLA Ops:
  7.2 247.5 %all-gather.3.cloned.1.call-start = ((), (), s32[]{:S(2)}) async-start(), calls=%async_computation.1 | async-start | bytes 8110080 | tf_op jit(solution)/shard_map/all_gather | solution.py:40
  7.2 26.0 %collective-permute-start = (bf16[192,640]{1,0:T(8,128)(2,1)}, bf16[192,640]{1,0:T(8,128)(2,1)S(1)}, u32[]{:S(2)}, u32[]{:S(2)}) collective-permute-start(bf16[192,640]{1,0:T(8,128)(2,1)} %param.7), channel_id=1, source_target_pairs={{480,0},{0,32},{32,64},{64,96},{96,128},{128,160},{160,192},{192,2... | collective-permute-start | bytes 737288 | tf_op jit(solution)/shard_map/ppermute | solution.py:10
  33.2 0.7 copy-start.1
  33.9 572.2 %all-gather.5.cloned.1.call-start = ((), (), s32[]{:S(2)}) async-start(), calls=%async_computation.2 | async-start | bytes 8110080 | tf_op jit(solution)/shard_map/all_gather | solution.py:50
  34.6 18.5 %collective-permute-start.1 = (s32[192]{0:T(256)}, s32[192]{0:T(256)S(1)}, u32[]{:S(2)}, u32[]{:S(2)}) collective-permute-start(s32[192]{0:T(256)} %param.9), channel_id=1, source_target_pairs={{480,0},{0,32},{32,64},{64,96},{96,128},{128,160},{160,192},{192,2... | collective-permute-start | bytes 2312 | tf_op jit(solution)/shard_map/ppermute | solution.py:10
  606.1 21.0 %copy-start = (bf16[192,6144]{1,0:T(8,128)(2,1)S(1)}, bf16[192,6144]{1,0:T(8,128)(2,1)}, u32[]{:S(2)}) copy-start(bf16[192,6144]{1,0:T(8,128)(2,1)} %fusion.7) | copy-start | bytes 7077892
  612.2 42.0 %collective-permute-start.2 = (f32[192,640]{1,0:T(8,128)S(1)}, f32[192,640]{1,0:T(8,128)S(1)}, u32[]{:S(2)}, u32[]{:S(2)}) collective-permute-start(f32[192,640]{1,0:T(8,128)S(1)} %convolution_multiply_fusion.1), channel_id=1, source_target_pairs={{32,0},{64,32},{96,64},{128,96},{160,128},{192,160},{224,192},{256... | collective-permute-start | bytes 1474568 | tf_op jit(solution)/shard_map/ppermute | solution.py:10
Sparse Core Ops, SparseCore 0:
  34.0 220.5 all-gather.2
  256.7 349.3 all-gather.4
where the time goes:
time: 662 us
  blocking collectives  404 us (61%)
  waiting for transfers between devices  163 us (25%)
  starting transfers between devices  46.1 us (7%)
  matrix products  19.7 us (3%)
  between operations  16.1 us (2%)
  local copies, waits for them, and re-layouts  12 us (2%)
    all_to_all x1, blocking collectives, body(): lax.all_to_all(weight, 'grp', split_axis=1, concat_axis=0, tiled=True)  218 us
    unnamed x1, blocking collectives  186 us
    all_gather x1, waiting for transfers between devices, body(): lax.all_gather(picture_vectors, 'grp', axis=0, tiled=True)  117 us
    ppermute x3, starting transfers between devices, shifted(): return lax.ppermute(block, axis, route)  46.1 us
    ppermute x3, waiting for transfers between devices, shifted(): return lax.ppermute(block, axis, route)  31.1 us
    all_gather x1, waiting for transfers between devices, body(): lax.all_gather(moved_texts, 'grp', axis=0, tiled=True)  14.8 us
  transfers between devices with their start and end apart: 5, of which 4 were waited for; matrix products, arithmetic and copies ran while one was open for 3% of the time, Pallas kernels for 0%

commit v1 on v0

v1 whole, which is shorter than its diff:
```python
import itertools

import jax
import jax.numpy as jnp
import numpy as np
from jax import lax
from jax.experimental import pallas as pl
from jax.experimental.pallas import tpu as pltpu
from jax.sharding import Mesh, PartitionSpec as P

AXES = ("h", "x", "c", "y", "z")
SIZES = dict(h=2, x=4, c=2, y=4, z=8)
MOVE_AXES = ("h", "x", "c", "z")
ROWS = 192
EXTRA = 16
PACKED = ROWS + EXTRA
D = 640
GROUP = 4 * ROWS
CHUNK = 256

PLANE = (7, 3, 0, 5, 2, 6, 1, 4)
IMAGE_PLACE = ((0, 3, 5, 6, 4, 7, 2, 1), (6, 7, 0, 1, 3, 4, 2, 5), (1, 0, 5, 3, 6, 7, 2, 4), (1, 5, 3, 6, 2, 7, 4, 0), (4, 2, 0, 3, 6, 1, 5, 7), (6, 2, 7, 0, 3, 5, 1, 4), (7, 1, 6, 5, 4, 3, 0, 2), (6, 5, 4, 3, 2, 0, 7, 1))
TEXT_PLACE = ((3, 2, 4, 1, 6, 0, 7, 5), (3, 7, 4, 6, 2, 5, 1, 0), (5, 4, 6, 1, 0, 2, 3, 7), (5, 2, 0, 1, 7, 4, 6, 3), (3, 7, 0, 4, 1, 2, 5, 6), (0, 3, 4, 7, 1, 5, 2, 6), (6, 2, 5, 3, 1, 4, 0, 7), (6, 1, 2, 4, 0, 7, 5, 3))


def routes(place, shift):
    extent = tuple(SIZES[a] for a in MOVE_AXES)
    out = []
    for h, x, c, z in itertools.product(*map(range, extent)):
        pair = (8 * h + 2 * x + c + shift) % 16
        half, p = divmod(pair, 8)
        spot = place[p][z]
        to = (half, spot // 2, spot % 2, PLANE[p])
        out.append((int(np.ravel_multi_index((h, x, c, z), extent)), int(np.ravel_multi_index(to, extent))))
    return out


IMAGE_ROUTE = routes(IMAGE_PLACE, 0)
TEXT_ROUTE = routes(TEXT_PLACE, 1)


def back(route):
    return [(b, a) for a, b in route]


def pack(rows, ids, slot):
    flat = lax.dynamic_update_slice(jnp.zeros((EXTRA * D,), jnp.bfloat16), ids.astype(jnp.bfloat16), (slot * ROWS,))
    return jnp.concatenate([rows, flat.reshape(EXTRA, D)], axis=0)


def id_row(ref):
    parts = ref[0, ROWS:, :].astype(jnp.float32)
    for k in range(1, 4):
        parts = parts + ref[k, ROWS:, :].astype(jnp.float32)
    return jnp.concatenate([parts[0:1, :], parts[1:2, : GROUP - D]], axis=1)


def pair_kernel(scale_ref, own_ref, other_ref, text_ref, own_grad_ref, other_grad_ref, text_grad_ref, images, texts, weights, id_columns, sums):
    factor = scale_ref[0]
    offset = scale_ref[1]
    out_factor = factor * 0.125
    for k in range(4):
        texts[k * ROWS : (k + 1) * ROWS, :] = text_ref[k, :ROWS, :]
        images[k * ROWS : (k + 1) * ROWS, :] = own_ref[k, :ROWS, :]
        images[GROUP + k * ROWS : GROUP + (k + 1) * ROWS, :] = other_ref[k, :ROWS, :]
    text_ids = id_row(text_ref)
    for half, ref in enumerate((own_ref, other_ref)):
        ids = id_row(ref)
        for j in range(GROUP // 128):
            tile = jnp.broadcast_to(ids[:, j * 128 : (j + 1) * 128], (128, 128))
            id_columns[half * GROUP + j * 128 : half * GROUP + (j + 1) * 128, :] = tile.T

    def step(i, _):
        start = pl.multiple_of(i * CHUNK, CHUNK)
        block = images[pl.ds(start, CHUNK), :]
        scores = lax.dot_general(block, texts[...], (((1,), (1,)), ((), ())), preferred_element_type=jnp.float32)
        scores = scores * factor + offset
        columns = id_columns[pl.ds(start, CHUNK), :]
        positive = (jnp.concatenate([columns] * (GROUP // 128), axis=1) == text_ids).astype(jnp.float32)
        weight = (jax.nn.sigmoid(scores) - positive).astype(jnp.bfloat16)
        weights[pl.ds(start, CHUNK), :] = weight
        sums[pl.ds(start, CHUNK), :] = out_factor * jnp.dot(weight, texts[...], preferred_element_type=jnp.float32)
        return 0

    lax.fori_loop(0, 2 * GROUP // CHUNK, step, 0)
    for k in range(4):
        own_grad_ref[k] = sums[k * ROWS : (k + 1) * ROWS, :].astype(own_grad_ref.dtype)
        other_grad_ref[k] = sums[GROUP + k * ROWS : GROUP + (k + 1) * ROWS, :].astype(other_grad_ref.dtype)

    def text_step(j, _):
        start = pl.multiple_of(j * CHUNK, CHUNK)
        sums[pl.ds(start, CHUNK), :] = out_factor * lax.dot_general(
            weights[:, pl.ds(start, CHUNK)], images[...], (((0,), (0,)), ((), ())), preferred_element_type=jnp.float32
        )
        return 0

    for j in range(GROUP // CHUNK):
        text_step(j, 0)
    for k in range(4):
        text_grad_ref[k] = sums[k * ROWS : (k + 1) * ROWS, :].astype(text_grad_ref.dtype)


def pair_grads(scale, own, other, text):
    vmem = pl.BlockSpec(memory_space=pltpu.VMEM)
    grad = lambda kind: jax.ShapeDtypeStruct((4, ROWS, D), kind)
    return pl.pallas_call(
        pair_kernel,
        out_shape=(grad(jnp.float32), grad(jnp.bfloat16), grad(jnp.bfloat16)),
        in_specs=[pl.BlockSpec(memory_space=pltpu.SMEM), vmem, vmem, vmem],
        out_specs=(vmem, vmem, vmem),
        scratch_shapes=[
            pltpu.VMEM((2 * GROUP, D), jnp.bfloat16),
            pltpu.VMEM((GROUP, D), jnp.bfloat16),
            pltpu.VMEM((2 * GROUP, GROUP), jnp.bfloat16),
            pltpu.VMEM((2 * GROUP, 128), jnp.float32),
            pltpu.VMEM((2 * GROUP, D), jnp.float32),
        ],
        compiler_params=pltpu.CompilerParams(vmem_limit_bytes=48 * 1024 * 1024),
        cost_estimate=pl.CostEstimate(flops=6 * 2 * GROUP * GROUP * D, bytes_accessed=10 << 20, transcendentals=2 * GROUP * GROUP),
        name="pair_grads",
    )(scale, own, other, text)


def body(picture_vectors, caption_vectors, picture_match_label, caption_match_label, inverse_softness, score_offset):
    scale = jnp.concatenate([inverse_softness, score_offset])
    place = jnp.asarray(np.asarray(IMAGE_PLACE, np.int32))
    image_slot = place[2 * lax.axis_index("x") + lax.axis_index("c"), lax.axis_index("z")] // 2
    packed_images = pack(picture_vectors, picture_match_label, image_slot)
    packed_texts = pack(caption_vectors, caption_match_label, lax.axis_index("y"))
    images = lax.ppermute(packed_images, MOVE_AXES, IMAGE_ROUTE)
    texts = lax.ppermute(packed_texts, MOVE_AXES, TEXT_ROUTE)
    own = lax.all_gather(images, "x", axis=0)
    other = lax.ppermute(own, "c", [(0, 1), (1, 0)])
    text = lax.all_gather(texts, "y", axis=0)
    own_grad, other_grad, text_part = pair_grads(scale, own, other, text)
    other_grad = lax.ppermute(other_grad, "c", [(0, 1), (1, 0)])
    image_part = (own_grad + other_grad.astype(jnp.float32)).astype(jnp.bfloat16)
    text_parts = lax.all_to_all(text_part, "y", split_axis=0, concat_axis=0, tiled=True)
    text_sum = jnp.sum(text_parts.astype(jnp.float32), axis=0).astype(jnp.bfloat16)
    text_home = lax.ppermute(text_sum, MOVE_AXES, back(TEXT_ROUTE))
    image_parts = lax.all_to_all(image_part, "x", split_axis=0, concat_axis=0, tiled=True)
    image_sum = jnp.sum(image_parts.astype(jnp.float32), axis=0).astype(jnp.bfloat16)
    image_home = lax.ppermute(image_sum, MOVE_AXES, back(IMAGE_ROUTE))
    return image_home, text_home.astype(jnp.float32)


def solution(mesh):
    fine = Mesh(mesh.devices.reshape(tuple(SIZES.values())), AXES)
    rows, ids = P(AXES, None), P(AXES)
    return jax.shard_map(
        body,
        mesh=fine,
        in_specs=(rows, rows, ids, ids, P(), P()),
        out_specs=(rows, rows),
        check_vma=False,
    )
```

time: 662 us -> 193 us (0.29)
  the two profiles are of different devices: /device:TPU:31 before, /device:TPU:7 now
where the time goes in v1:
time: 193 us
  waiting for transfers between devices  92.9 us (48%)
  starting transfers between devices  57.8 us (30%)
  between operations  18 us (9%)
  Pallas kernels  10.3 us (5%)
  other arithmetic  7.31 us (4%)
  local copies, waits for them, and re-layouts  6.35 us (3%)
    all_gather x1, waiting for transfers between devices, body(): text = lax.all_gather(texts, 'y', axis=0)  30.9 us
    ppermute x1, waiting for transfers between devices, body(): texts = lax.ppermute(packed_texts, MOVE_AXES, TEXT_ROUTE)  19.7 us
    ppermute x1, starting transfers between devices, body(): texts = lax.ppermute(packed_texts, MOVE_AXES, TEXT_ROUTE)  16.9 us
    ppermute x1, waiting for transfers between devices, body(): image_home = lax.ppermute(image_sum, MOVE_AXES, back(IMAGE_ROUTE))  14.5 us
    all_to_all x1, waiting for transfers between devices, body(): lax.all_to_all(text_part, 'y', split_axis=0, concat_axis=0, tiled=True)  11.8 us
    pallas_call x1, Pallas kernels, pair_grads(): pl.pallas_call(pair_kernel, out_shape=(grad(jnp.float32), grad(jnp.bfloat...  10.3 us
    ppermute x1, starting transfers between devices, body(): text_home = lax.ppermute(text_sum, MOVE_AXES, back(TEXT_ROUTE))  10.1 us
    ppermute x1, starting transfers between devices, body(): images = lax.ppermute(packed_images, MOVE_AXES, IMAGE_ROUTE)  9.38 us
  transfers between devices with their start and end apart: 10, of which 7 were waited for; matrix products, arithmetic and copies ran while one was open for 3% of the time, Pallas kernels for 0%

profile of v1, /device:TPU:7, one launch (start us, length us, event | category | flops | bytes accessed | tf_op | source)
XLA Modules:
  0.0 192.7 jit_solution(7267864955663355080)
XLA Ops:
  7.2 0.0 all-gather.5.cloned.1.call-start
  7.2 1.3 dynamic_slice.3
  11.1 0.7 convert_element_type.19
  11.8 0.2 dynamic_update_slice.6
  12.0 1.0 pad_maximum_fusion
  13.0 9.4 %collective-permute-start = (bf16[208,640]{1,0:T(8,128)(2,1)S(1)}, bf16[208,640]{1,0:T(8,128)(2,1)S(1)}, u32[]{:S(2)}, u32[]{:S(2)}) collective-permute-start(bf16[208,640]{1,0:T(8,128)(2,1)S(1)} %pad_maximum_fusion), channel_id=1, source_target_pairs={{0,7},{1,103},{2,167},{3,199},{4,135},{5,231},{6,71},{7,39},{32,19... | collective-permute-start | bytes 798728 | tf_op jit(solution)/shard_map/ppermute | solution.py:130
  22.4 7.7 %collective-permute-done = bf16[208,640]{1,0:T(8,128)(2,1)S(1)} collective-permute-done((bf16[208,640]{1,0:T(8,128)(2,1)S(1)}, bf16[208,640]{1,0:T(8,128)(2,1)S(1)}, u32[]{:S(2)}, u32[]{:S(2)}) %collective-permute-start) | collective-permute-done | bytes 266272 | tf_op jit(solution)/shard_map/ppermute | solution.py:130
  30.1 0.0 copy-start.2
  30.1 0.7 copy-done.2
  30.8 0.0 all-gather.5.cloned.1.call-update
  30.8 0.0 all-gather.7.cloned.1.call-start
  30.8 0.7 convert_element_type.20
  31.5 0.2 dynamic_update_slice.7
  31.8 1.0 pad_maximum_fusion.1
  32.8 16.9 %collective-permute-start.2 = (bf16[208,640]{1,0:T(8,128)(2,1)S(1)}, bf16[208,640]{1,0:T(8,128)(2,1)S(1)}, u32[]{:S(2)}, u32[]{:S(2)}) collective-permute-start(bf16[208,640]{1,0:T(8,128)(2,1)S(1)} %pad_maximum_fusion.1), channel_id=1, source_target_pairs={{0,99},{1,227},{2,131},{3,195},{4,67},{5,163},{6,35},{7,3},{32,160... | collective-permute-start | bytes 798728 | tf_op jit(solution)/shard_map/ppermute | solution.py:131
  49.6 19.7 %collective-permute-done.2 = bf16[208,640]{1,0:T(8,128)(2,1)S(1)} collective-permute-done((bf16[208,640]{1,0:T(8,128)(2,1)S(1)}, bf16[208,640]{1,0:T(8,128)(2,1)S(1)}, u32[]{:S(2)}, u32[]{:S(2)}) %collective-permute-start.2) | collective-permute-done | bytes 266272 | tf_op jit(solution)/shard_map/ppermute | solution.py:131
  69.3 0.0 copy-start.3
  69.3 0.7 copy-done.3
  70.1 0.0 all-gather.7.cloned.1.call-update
  70.1 1.8 all-gather.5.cloned.1.call-done
  71.8 3.6 %collective-permute-start.1 = (bf16[4,208,640]{2,1,0:T(8,128)(2,1)}, bf16[4,208,640]{2,1,0:T(8,128)(2,1)S(1)}, u32[]{:S(2)}, u32[]{:S(2)}) collective-permute-start(bf16[4,208,640]{2,1,0:T(8,128)(2,1)} %bitcast.3), channel_id=1, source_target_pairs={{0,32},{32,0},{1,33},{33,1},{2,34},{34,2},{3,35},{35,3},{4,36},{36... | collective-permute-start | bytes 3194888 | tf_op jit(solution)/shard_map/ppermute | solution.py:133
  76.8 0.1 pad_maximum_fusion.2.scale_ref
  76.8 30.9 %all-gather.7.cloned.1.call-done = bf16[832,640]{1,0:T(8,128)(2,1)} async-done(((bf16[208,640]{1,0:T(8,128)(2,1)}), bf16[832,640]{1,0:T(8,128)(2,1)}) %all-gather.7.cloned.1.call-update) | async-done | bytes 1064976 | tf_op jit(solution)/shard_map/all_gather | solution.py:134
  107.7 0.0 collective-permute-done.1.other_ref
  107.7 0.0 copy-start
  107.7 1.2 copy-done
  108.9 0.0 copy-start.1
  108.9 1.2 copy-done.1
  110.2 10.3 %pair_grads.1 = (f32[4,192,640]{2,1,0:T(8,128)}, bf16[4,192,640]{2,1,0:T(8,128)(2,1)S(1)}, bf16[4,192,640]{2,1,0:T(8,128)(2,1)}) custom-call(f32[2]{0:T(128)S(1)} %pad_maximum_fusion.2.scale_ref, bf16[4,208,640]{2,1,0:T(8,128)(2,1)S(1)} %bitcast.4, bf16[4,208,640]{2,1,0:T(8,128)(2,1)S(1)} %collective-permute-done.1.other_ref, bf16[4,208,640]{2,1,0:T(8,128)(2,1)S(1)} %bitcast.5), custom_call_target="tpu_custom_call" | custom-call | flops 4529848320 | bytes 10485760 | tf_op jit(solution)/shard_map/pair_grads/pallas_call | solution.py:106
  120.4 3.5 %collective-permute-start.3 = (bf16[4,192,640]{2,1,0:T(8,128)(2,1)S(1)}, bf16[4,192,640]{2,1,0:T(8,128)(2,1)S(1)}, u32[]{:S(2)}, u32[]{:S(2)}) collective-permute-start(bf16[4,192,640]{2,1,0:T(8,128)(2,1)S(1)} %get-tuple-element.6), channel_id=1, source_target_pairs={{0,32},{32,0},{1,33},{33,1},{2,34},{34,2},{3,35},{35,3},{4,36},{36... | collective-permute-start | bytes 2949128 | tf_op jit(solution)/shard_map/ppermute | solution.py:136
  123.9 3.5 %all-to-all-start.1 = ((bf16[4,192,640]{2,1,0:T(8,128)(2,1)}), bf16[4,192,640]{2,1,0:T(8,128)(2,1)S(1)}, u32[]{:S(2)}, u32[]{:S(2)}) async-start(bf16[4,192,640]{2,1,0:T(8,128)(2,1)} %get-tuple-element.7), calls=%async_computation.1 | async-start | bytes 1966080 | tf_op jit(solution)/shard_map/all_to_all | solution.py:138
  127.4 0.0 collective-permute-done.3
  127.5 2.7 %add_convert_fusion = bf16[4,192,640]{2,1,0:T(8,128)(2,1)} fusion(f32[4,192,640]{2,1,0:T(8,128)} %get-tuple-element.5, bf16[4,192,640]{2,1,0:T(8,128)(2,1)S(1)} %collective-permute-done.3), kind=kLoop, calls=%fused_computation | loop fusion | flops 1474560 | bytes 3932160 | tf_op jit(solution)/shard_map/convert_element_type | solution.py:137
  130.2 11.8 %all-to-all-done.1 = bf16[4,192,640]{2,1,0:T(8,128)(2,1)S(1)} async-done(((bf16[4,192,640]{2,1,0:T(8,128)(2,1)}), bf16[4,192,640]{2,1,0:T(8,128)(2,1)S(1)}, u32[]{:S(2)}, u32[]{:S(2)}) %all-to-all-start.1) | async-done | bytes 983072 | tf_op jit(solution)/shard_map/all_to_all | solution.py:138
  142.0 4.2 %all-to-all-start = ((bf16[4,192,640]{2,1,0:T(8,128)(2,1)}), bf16[4,192,640]{2,1,0:T(8,128)(2,1)S(1)}, u32[]{:S(2)}, u32[]{:S(2)}) async-start(bf16[4,192,640]{2,1,0:T(8,128)(2,1)} %add_convert_fusion), calls=%async_computation | async-start | bytes 1966080 | tf_op jit(solution)/shard_map/all_to_all | solution.py:141
  146.2 0.2 reduce_sum.25
  146.4 10.1 %collective-permute-start.5 = (bf16[192,640]{1,0:T(8,128)(2,1)S(1)}, bf16[192,640]{1,0:T(8,128)(2,1)S(1)}, u32[]{:S(2)}, u32[]{:S(2)}) collective-permute-start(bf16[192,640]{1,0:T(8,128)(2,1)S(1)} %reduce_sum.25), channel_id=1, source_target_pairs={{99,0},{227,1},{131,2},{195,3},{67,4},{163,5},{35,6},{3,7},{160,32... | collective-permute-start | bytes 737288 | tf_op jit(solution)/shard_map/ppermute | solution.py:140
  156.5 6.6 %all-to-all-done = bf16[4,192,640]{2,1,0:T(8,128)(2,1)S(1)} async-done(((bf16[4,192,640]{2,1,0:T(8,128)(2,1)}), bf16[4,192,640]{2,1,0:T(8,128)(2,1)S(1)}, u32[]{:S(2)}, u32[]{:S(2)}) %all-to-all-start) | async-done | bytes 983072 | tf_op jit(solution)/shard_map/all_to_all | solution.py:141
  163.0 0.2 reduce_sum.24
  163.2 6.6 %collective-permute-start.4 = (bf16[192,640]{1,0:T(8,128)(2,1)S(1)}, bf16[192,640]{1,0:T(8,128)(2,1)S(1)}, u32[]{:S(2)}, u32[]{:S(2)}) collective-permute-start(bf16[192,640]{1,0:T(8,128)(2,1)S(1)} %reduce_sum.24), channel_id=1, source_target_pairs={{7,0},{103,1},{167,2},{199,3},{135,4},{231,5},{71,6},{39,7},{195,3... | collective-permute-start | bytes 737288 | tf_op jit(solution)/shard_map/ppermute | solution.py:143
  169.8 0.0 collective-permute-done.5
  169.8 0.8 convert_element_type.23
  170.7 14.5 %collective-permute-done.4 = bf16[192,640]{1,0:T(8,128)(2,1)S(1)} collective-permute-done((bf16[192,640]{1,0:T(8,128)(2,1)S(1)}, bf16[192,640]{1,0:T(8,128)(2,1)S(1)}, u32[]{:S(2)}, u32[]{:S(2)}) %collective-permute-start.4) | collective-permute-done | bytes 245792 | tf_op jit(solution)/shard_map/ppermute | solution.py:143
  185.2 0.7 copy.16
  (4 shorter events, 0.1 us)
Async XLA Ops:
  7.2 64.7 %all-gather.5.cloned.1.call-start = ((), (), s32[]{:S(2)}) async-start(), calls=%async_computation.2 | async-start | bytes 1331200 | tf_op jit(solution)/shard_map/all_gather | solution.py:132
  13.0 17.0 %collective-permute-start = (bf16[208,640]{1,0:T(8,128)(2,1)S(1)}, bf16[208,640]{1,0:T(8,128)(2,1)S(1)}, u32[]{:S(2)}, u32[]{:S(2)}) collective-permute-start(bf16[208,640]{1,0:T(8,128)(2,1)S(1)} %pad_maximum_fusion), channel_id=1, source_target_pairs={{0,7},{1,103},{2,167},{3,199},{4,135},{5,231},{6,71},{7,39},{32,19... | collective-permute-start | bytes 798728 | tf_op jit(solution)/shard_map/ppermute | solution.py:130
  30.1 0.7 copy-start.2
  30.8 76.9 %all-gather.7.cloned.1.call-start = ((), (), s32[]{:S(2)}) async-start(), calls=%async_computation.3 | async-start | bytes 1331200 | tf_op jit(solution)/shard_map/all_gather | solution.py:134
  32.8 36.6 %collective-permute-start.2 = (bf16[208,640]{1,0:T(8,128)(2,1)S(1)}, bf16[208,640]{1,0:T(8,128)(2,1)S(1)}, u32[]{:S(2)}, u32[]{:S(2)}) collective-permute-start(bf16[208,640]{1,0:T(8,128)(2,1)S(1)} %pad_maximum_fusion.1), channel_id=1, source_target_pairs={{0,99},{1,227},{2,131},{3,195},{4,67},{5,163},{6,35},{7,3},{32,160... | collective-permute-start | bytes 798728 | tf_op jit(solution)/shard_map/ppermute | solution.py:131
  69.3 0.7 copy-start.3
  71.8 35.9 %collective-permute-start.1 = (bf16[4,208,640]{2,1,0:T(8,128)(2,1)}, bf16[4,208,640]{2,1,0:T(8,128)(2,1)S(1)}, u32[]{:S(2)}, u32[]{:S(2)}) collective-permute-start(bf16[4,208,640]{2,1,0:T(8,128)(2,1)} %bitcast.3), channel_id=1, source_target_pairs={{0,32},{32,0},{1,33},{33,1},{2,34},{34,2},{3,35},{35,3},{4,36},{36... | collective-permute-start | bytes 3194888 | tf_op jit(solution)/shard_map/ppermute | solution.py:133
  107.7 1.2 copy-start
  108.9 1.2 copy-start.1
  120.4 7.0 %collective-permute-start.3 = (bf16[4,192,640]{2,1,0:T(8,128)(2,1)S(1)}, bf16[4,192,640]{2,1,0:T(8,128)(2,1)S(1)}, u32[]{:S(2)}, u32[]{:S(2)}) collective-permute-start(bf16[4,192,640]{2,1,0:T(8,128)(2,1)S(1)} %get-tuple-element.6), channel_id=1, source_target_pairs={{0,32},{32,0},{1,33},{33,1},{2,34},{34,2},{3,35},{35,3},{4,36},{36... | collective-permute-start | bytes 2949128 | tf_op jit(solution)/shard_map/ppermute | solution.py:136
  123.9 18.0 %all-to-all-start.1 = ((bf16[4,192,640]{2,1,0:T(8,128)(2,1)}), bf16[4,192,640]{2,1,0:T(8,128)(2,1)S(1)}, u32[]{:S(2)}, u32[]{:S(2)}) async-start(bf16[4,192,640]{2,1,0:T(8,128)(2,1)} %get-tuple-element.7), calls=%async_computation.1 | async-start | bytes 1966080 | tf_op jit(solution)/shard_map/all_to_all | solution.py:138
  142.0 21.1 %all-to-all-start = ((bf16[4,192,640]{2,1,0:T(8,128)(2,1)}), bf16[4,192,640]{2,1,0:T(8,128)(2,1)S(1)}, u32[]{:S(2)}, u32[]{:S(2)}) async-start(bf16[4,192,640]{2,1,0:T(8,128)(2,1)} %add_convert_fusion), calls=%async_computation | async-start | bytes 1966080 | tf_op jit(solution)/shard_map/all_to_all | solution.py:141
  146.4 23.4 %collective-permute-start.5 = (bf16[192,640]{1,0:T(8,128)(2,1)S(1)}, bf16[192,640]{1,0:T(8,128)(2,1)S(1)}, u32[]{:S(2)}, u32[]{:S(2)}) collective-permute-start(bf16[192,640]{1,0:T(8,128)(2,1)S(1)} %reduce_sum.25), channel_id=1, source_target_pairs={{99,0},{227,1},{131,2},{195,3},{67,4},{163,5},{35,6},{3,7},{160,32... | collective-permute-start | bytes 737288 | tf_op jit(solution)/shard_map/ppermute | solution.py:140
  163.2 22.0 %collective-permute-start.4 = (bf16[192,640]{1,0:T(8,128)(2,1)S(1)}, bf16[192,640]{1,0:T(8,128)(2,1)S(1)}, u32[]{:S(2)}, u32[]{:S(2)}) collective-permute-start(bf16[192,640]{1,0:T(8,128)(2,1)S(1)} %reduce_sum.24), channel_id=1, source_target_pairs={{7,0},{103,1},{167,2},{199,3},{135,4},{231,5},{71,6},{39,7},{195,3... | collective-permute-start | bytes 737288 | tf_op jit(solution)/shard_map/ppermute | solution.py:143
Sparse Core Ops, SparseCore 0:
  30.9 40.8 all-gather.4
  73.9 33.7 all-gather.6

commit v2 on v1

v2 whole, which is shorter than its diff:
```python
import itertools

import jax
import jax.numpy as jnp
import numpy as np
from jax import lax
from jax.experimental import pallas as pl
from jax.experimental.pallas import tpu as pltpu
from jax.sharding import Mesh, PartitionSpec as P

AXES = ("h", "x", "c", "y", "z")
SIZES = dict(h=2, x=4, c=2, y=4, z=8)
MOVE_AXES = ("h", "x", "c", "z")
ROWS = 192
EXTRA = 8
PACKED = ROWS + EXTRA
D = 640
GROUP = 4 * ROWS
CHUNK = 256

PLANE = (7, 3, 0, 5, 2, 6, 1, 4)
IMAGE_PLACE = ((0, 2, 4, 6, 1, 3, 5, 7), (0, 2, 4, 6, 1, 3, 5, 7), (2, 0, 6, 4, 3, 1, 7, 5), (2, 0, 6, 4, 3, 1, 7, 5), (4, 6, 0, 2, 5, 7, 1, 3), (4, 6, 0, 2, 5, 7, 1, 3), (6, 4, 2, 0, 7, 5, 3, 1), (6, 4, 2, 0, 7, 5, 3, 1))
TEXT_PLACE = ((6, 4, 2, 0, 7, 5, 3, 1), (0, 2, 4, 6, 1, 3, 5, 7), (0, 2, 4, 6, 1, 3, 5, 7), (2, 0, 6, 4, 3, 1, 7, 5), (2, 0, 6, 4, 3, 1, 7, 5), (4, 6, 0, 2, 5, 7, 1, 3), (4, 6, 0, 2, 5, 7, 1, 3), (6, 4, 2, 0, 7, 5, 3, 1))


def routes(place, shift):
    extent = tuple(SIZES[a] for a in MOVE_AXES)
    out = []
    for h, x, c, z in itertools.product(*map(range, extent)):
        pair = (8 * h + 2 * x + c + shift) % 16
        half, p = divmod(pair, 8)
        spot = place[p][z]
        to = (half, spot // 2, spot % 2, PLANE[p])
        out.append((int(np.ravel_multi_index((h, x, c, z), extent)), int(np.ravel_multi_index(to, extent))))
    return out


IMAGE_ROUTE = routes(IMAGE_PLACE, 0)
TEXT_ROUTE = routes(TEXT_PLACE, 1)


def back(route):
    return [(b, a) for a, b in route]


def pack(rows, ids):
    below = jnp.pad(ids.astype(jnp.bfloat16)[None, :], ((0, EXTRA - 1), (0, D - ROWS)))
    return jnp.concatenate([rows, below], axis=0)


def id_row(ref):
    total = None
    for k in range(4):
        part = ref[k, ROWS:, :].astype(jnp.float32)
        part = jnp.concatenate([part, jnp.zeros((EXTRA, GROUP - D), jnp.float32)], axis=1)
        part = part if k == 0 else pltpu.roll(part, k * ROWS, 1)
        total = part if total is None else total + part
    return total[0:1, :]


VMEM = pl.BlockSpec(memory_space=pltpu.VMEM)
SMEM = pl.BlockSpec(memory_space=pltpu.SMEM)


def call(kernel, name, out, in_specs, flops, *args):
    return pl.pallas_call(
        kernel,
        out_shape=tuple(jax.ShapeDtypeStruct(shape, kind) for shape, kind in out),
        in_specs=in_specs,
        out_specs=(VMEM,) * len(out),
        compiler_params=pltpu.CompilerParams(vmem_limit_bytes=24 * 1024 * 1024),
        cost_estimate=pl.CostEstimate(flops=flops, bytes_accessed=4 << 20, transcendentals=0),
        name=name,
    )(*args)


def pair_weights(scale_ref, block, texts, ids, text_ids):
    scores = lax.dot_general(block, texts, (((1,), (1,)), ((), ())), preferred_element_type=jnp.float32)
    scores = scores * scale_ref[0] + scale_ref[1]
    positive = (jnp.concatenate([ids] * (GROUP // 128), axis=1) == text_ids).astype(jnp.float32)
    return (jax.nn.sigmoid(scores) - positive).astype(jnp.bfloat16)


def unpack_rows(ref, rows):
    for k in range(4):
        rows[k * ROWS : (k + 1) * ROWS, :] = ref[k, :ROWS, :]


def id_tile(ids, j):
    return jnp.broadcast_to(ids[:, j * 128 : (j + 1) * 128], (128, 128)).T


def own_kernel(scale_ref, image_ref, text_ref, weights, images, texts, text_ids):
    unpack_rows(text_ref, texts)
    unpack_rows(image_ref, images)
    text_row = id_row(text_ref)
    text_ids[...] = jnp.broadcast_to(text_row, text_ids.shape)
    ids = id_row(image_ref)
    for j in range(GROUP // CHUNK):
        rows = pl.ds(j * CHUNK, CHUNK)
        columns = jnp.concatenate([id_tile(ids, 2 * j), id_tile(ids, 2 * j + 1)], axis=0)
        weights[rows, :] = pair_weights(scale_ref, images[rows, :], texts[...], columns, text_row)


def other_kernel(scale_ref, image_ref, texts, text_ids, weights, images):
    unpack_rows(image_ref, images)
    text_row = text_ids[0:1, :]
    ids = id_row(image_ref)
    for j in range(GROUP // CHUNK):
        rows = pl.ds(j * CHUNK, CHUNK)
        columns = jnp.concatenate([id_tile(ids, 2 * j), id_tile(ids, 2 * j + 1)], axis=0)
        weights[rows, :] = pair_weights(scale_ref, images[rows, :], texts[...], columns, text_row)


def other_grad_kernel(scale_ref, weights, texts, grads):
    for j in range(GROUP // CHUNK):
        rows = pl.ds(j * CHUNK, CHUNK)
        grad = jnp.dot(weights[rows, :], texts[...], preferred_element_type=jnp.float32)
        grads[rows, :] = (scale_ref[0] * 0.125 * grad).astype(grads.dtype)


def text_kernel(scale_ref, own_weights, own_images, other_weights, other_images, grads):
    fold = (((0,), (0,)), ((), ()))
    for j in range(GROUP // CHUNK):
        rows = pl.ds(j * CHUNK, CHUNK)
        grad = lax.dot_general(own_weights[:, rows], own_images[...], fold, preferred_element_type=jnp.float32)
        grad = grad + lax.dot_general(other_weights[:, rows], other_images[...], fold, preferred_element_type=jnp.float32)
        grads[rows, :] = (scale_ref[0] * 0.125 * grad).astype(grads.dtype)


def image_kernel(scale_ref, place_ref, weights, texts, received, kept, *sent):
    for k, out in enumerate((kept, *sent)):
        shard = lax.rem(place_ref[0] + k, 4)
        rows = pl.ds(pl.multiple_of(shard * ROWS, ROWS), ROWS)
        grad = jnp.dot(weights[rows, :], texts[...], preferred_element_type=jnp.float32)
        out[...] = (scale_ref[0] * 0.125 * grad + received[rows, :].astype(jnp.float32)).astype(out.dtype)


def body(picture_vectors, caption_vectors, picture_match_label, caption_match_label, inverse_softness, score_offset):
    scale = jnp.concatenate([inverse_softness, score_offset])
    place = lax.axis_index("x").astype(jnp.int32).reshape(1)
    packed_images = pack(picture_vectors, picture_match_label)
    packed_texts = pack(caption_vectors, caption_match_label)
    packed_images, packed_texts = lax.optimization_barrier((packed_images, packed_texts))
    images = lax.ppermute(packed_images, MOVE_AXES, IMAGE_ROUTE)
    texts = lax.ppermute(packed_texts, MOVE_AXES, TEXT_ROUTE)
    images, texts = lax.optimization_barrier((images, texts))
    own = lax.all_to_all(jnp.broadcast_to(images[None], (4, PACKED, D)), "x", split_axis=0, concat_axis=0, tiled=True)
    other = lax.ppermute(own, "c", [(0, 1), (1, 0)])
    text = lax.all_gather(texts, "y", axis=0)
    half, flops = (GROUP, GROUP), 2 * GROUP * GROUP * D
    rows = (GROUP, D)
    bf16, f32 = jnp.bfloat16, jnp.float32
    own_weights, own_images, all_texts, text_ids = call(
        own_kernel, "own_weights", ((half, bf16), (rows, bf16), (rows, bf16), ((8, GROUP), f32)), [SMEM, VMEM, VMEM], 40 * flops, scale, own, text
    )
    other_weights, other_images = call(
        other_kernel, "other_weights", ((half, bf16), (rows, bf16)), [SMEM, VMEM, VMEM, VMEM], flops, scale, other, all_texts, text_ids
    )
    (text_part,) = call(
        text_kernel, "text_grads", ((rows, bf16),), [SMEM] + [VMEM] * 4, 2 * flops, scale, own_weights, own_images, other_weights, other_images
    )
    text_parts = lax.all_to_all(text_part, "y", split_axis=0, concat_axis=0, tiled=True)
    (other_grad,) = call(other_grad_kernel, "other_grads", ((rows, bf16),), [SMEM, VMEM, VMEM], flops, scale, other_weights, all_texts)
    received = lax.ppermute(other_grad, "c", [(0, 1), (1, 0)])
    shard = (ROWS, D)
    kept, *sent = call(
        image_kernel, "image_grads", ((shard, f32),) + ((shard, bf16),) * 3, [SMEM, SMEM] + [VMEM] * 3, flops, scale, place, own_weights, all_texts, received
    )
    for k, part in enumerate(sent, 1):
        kept = kept + lax.ppermute(part, "x", [(i, (i + k) % 4) for i in range(4)]).astype(f32)
    image_home = lax.ppermute(kept.astype(bf16), MOVE_AXES, back(IMAGE_ROUTE))
    text_sum = jnp.sum(text_parts.reshape(4, ROWS, D).astype(f32), axis=0).astype(bf16)
    text_home = lax.ppermute(text_sum, MOVE_AXES, back(TEXT_ROUTE))
    return image_home, text_home.astype(f32)


def solution(mesh):
    fine = Mesh(mesh.devices.reshape(tuple(SIZES.values())), AXES)
    rows, ids = P(AXES, None), P(AXES)
    return jax.shard_map(
        body,
        mesh=fine,
        in_specs=(rows, rows, ids, ids, P(), P()),
        out_specs=(rows, rows),
        check_vma=False,
    )
```

time: 193 us -> 133 us (0.69)
  the two profiles are of different devices: /device:TPU:7 before, /device:TPU:43 now
where the time goes in v2:
time: 133 us; the launch traced here: 132 us
  starting transfers between devices  72.1 us (54%)
  waiting for transfers between devices  25.2 us (19%)
  blocking collectives  12.8 us (10%)
  Pallas kernels  12.6 us (9%)
  other arithmetic  4.87 us (4%)
  local copies, waits for them, and re-layouts  2.55 us (2%)
  between operations  2.07 us (2%)
    ppermute x1, starting transfers between devices, body(): text_home = lax.ppermute(text_sum, MOVE_AXES, back(TEXT_ROUTE))  18.3 us
    all_to_all x1, starting transfers between devices, body(): lax.all_to_all(jnp.broadcast_to(images[None], (4, PACKED, D)), 'x', split...  16.4 us
    all_gather x1, blocking collectives, body(): text = lax.all_gather(texts, 'y', axis=0)  12.8 us
    pallas_call x5, Pallas kernels, call(): pl.pallas_call(kernel, out_shape=tuple((jax.ShapeDtypeStruct(shape, kind)...  12.6 us
    ppermute x1, waiting for transfers between devices, body(): images = lax.ppermute(packed_images, MOVE_AXES, IMAGE_ROUTE)  10.4 us
    ppermute x3, starting transfers between devices, body(): lax.ppermute(part, 'x', [(i, (i + k) % 4) for i in range(4)]).astype(f32)  9.56 us
    ppermute x1, starting transfers between devices, body(): images = lax.ppermute(packed_images, MOVE_AXES, IMAGE_ROUTE)  9.35 us
    ppermute x1, waiting for transfers between devices, body(): image_home = lax.ppermute(kept.astype(bf16), MOVE_AXES, back(IMAGE_ROUTE))  7.9 us
  transfers between devices with their start and end apart: 11, of which 5 were waited for; matrix products, arithmetic and copies ran while one was open for 2% of the time, Pallas kernels for 6%

profile of v2, /device:TPU:43, one launch (start us, length us, event | category | flops | bytes accessed | tf_op | source)
XLA Modules:
  0.0 132.2 jit_solution(9119688216069596923)
XLA Ops:
  0.6 0.7 convert_element_type.26
  1.3 0.7 convert_element_type.27
  2.0 1.1 fusion.2
  3.1 9.3 %collective-permute-start = (bf16[200,640]{1,0:T(8,128)(2,1)S(1)}, bf16[200,640]{1,0:T(8,128)(2,1)S(1)}, u32[]{:S(2)}, u32[]{:S(2)}) collective-permute-start(bf16[200,640]{1,0:T(8,128)(2,1)S(1)} %get-tuple-element.16), channel_id=1, source_target_pairs={{0,7},{1,71},{2,135},{3,199},{4,39},{5,103},{6,167},{7,231},{32,3}... | collective-permute-start | bytes 768008 | tf_op jit(solution)/shard_map/ppermute | solution.py:145
  12.5 7.6 %collective-permute-start.1 = (bf16[200,640]{1,0:T(8,128)(2,1)S(1)}, bf16[200,640]{1,0:T(8,128)(2,1)S(1)}, u32[]{:S(2)}, u32[]{:S(2)}) collective-permute-start(bf16[200,640]{1,0:T(8,128)(2,1)S(1)} %get-tuple-element.17), channel_id=1, source_target_pairs={{0,3},{1,67},{2,131},{3,195},{4,35},{5,99},{6,163},{7,227},{32,0},... | collective-permute-start | bytes 768008 | tf_op jit(solution)/shard_map/ppermute | solution.py:146
  20.1 10.4 %collective-permute-done = bf16[200,640]{1,0:T(8,128)(2,1)S(1)} collective-permute-done((bf16[200,640]{1,0:T(8,128)(2,1)S(1)}, bf16[200,640]{1,0:T(8,128)(2,1)S(1)}, u32[]{:S(2)}, u32[]{:S(2)}) %collective-permute-start) | collective-permute-done | bytes 256032 | tf_op jit(solution)/shard_map/ppermute | solution.py:145
  30.5 0.0 collective-permute-done.1
  30.5 1.1 broadcast_in_dim.14
  31.5 16.4 %all-to-all-start = ((bf16[4,200,640]{2,1,0:T(8,128)(2,1)}), bf16[4,200,640]{2,1,0:T(8,128)(2,1)}, u32[]{:S(2)}, u32[]{:S(2)}) async-start(bf16[4,200,640]{2,1,0:T(8,128)(2,1)} %broadcast_in_dim.14), calls=%async_computation | async-start | bytes 2048000 | tf_op jit(solution)/shard_map/all_to_all | solution.py:148
  49.2 0.1 pad_maximum_fusion.scale_ref
  49.3 12.8 %all-gather = bf16[800,640]{1,0:T(8,128)(2,1)S(1)} all-gather(bf16[200,640]{1,0:T(8,128)(2,1)S(1)} %collective-permute-done.1), channel_id=2, replica_groups=mesh['h'=2,'x'=4,'c'=2,'y'=4,'z'=8] {'y'}, dimensions={0}, use_global_device_ids=true | all-gather | bytes 1280000 | tf_op jit(solution)/shard_map/all_gather | solution.py:150
  62.1 0.0 all-to-all-done.image_ref
  62.1 1.9 %collective-permute-start.2 = (bf16[4,200,640]{2,1,0:T(8,128)(2,1)}, bf16[4,200,640]{2,1,0:T(8,128)(2,1)S(1)}, u32[]{:S(2)}, u32[]{:S(2)}) collective-permute-start(bf16[4,200,640]{2,1,0:T(8,128)(2,1)} %all-to-all-done.image_ref), channel_id=1, source_target_pairs={{0,32},{32,0},{1,33},{33,1},{2,34},{34,2},{3,35},{35,3},{4,36},{36... | collective-permute-start | bytes 3072008 | tf_op jit(solution)/shard_map/ppermute | solution.py:149
  64.0 2.4 %own_weights.1 = (bf16[768,768]{1,0:T(8,128)(2,1)S(1)}, bf16[768,640]{1,0:T(8,128)(2,1)S(1)}, bf16[768,640]{1,0:T(8,128)(2,1)S(1)}, f32[8,768]{1,0:T(8,128)S(1)}) custom-call(f32[2]{0:T(128)S(1)} %pad_maximum_fusion.scale_ref, bf16[4,200,640]{2,1,0:T(8,128)(2,1)} %all-to-all-done.image_ref, bf16[4,200,640]{2,1,0:T(8,128)(2,1)S(1)} %bitcast.3), custom_call_target="tpu_custom_call" | custom-call | flops 30198988800 | bytes 4194304 | tf_op jit(solution)/shard_map/own_weights/pallas_call | solution.py:66
  66.4 0.4 collective-permute-done.2.image_ref
  66.8 1.7 %other_weights.1 = (bf16[768,768]{1,0:T(8,128)(2,1)S(1)}, bf16[768,640]{1,0:T(8,128)(2,1)S(1)}) custom-call(f32[2]{0:T(128)S(1)} %pad_maximum_fusion.scale_ref, bf16[4,200,640]{2,1,0:T(8,128)(2,1)S(1)} %collective-permute-done.2.image_ref, bf16[768,640]{1,0:T(8,128)(2,1)S(1)} %get-tuple-element.21.texts, f32[8,768]{1,0:T(8,128)S(1)} %get-tuple-element.22.text_ids), custom_call_target="tpu_custom_call" | custom-call | flops 754974720 | bytes 4194304 | tf_op jit(solution)/shard_map/other_weights/pallas_call | solution.py:66
  68.5 2.6 %other_grads.1 = bf16[768,640]{1,0:T(8,128)(2,1)} custom-call(f32[2]{0:T(128)S(1)} %pad_maximum_fusion.scale_ref, bf16[768,768]{1,0:T(8,128)(2,1)S(1)} %get-tuple-element.23.weights.other_weights, bf16[768,640]{1,0:T(8,128)(2,1)S(1)} %get-tuple-element.21.texts), custom_call_target="tpu_custom_call" | custom-call | flops 754974720 | bytes 4194304 | tf_op jit(solution)/shard_map/other_grads/pallas_call | solution.py:66
  71.1 2.0 %collective-permute-start.3 = (bf16[768,640]{1,0:T(8,128)(2,1)}, bf16[768,640]{1,0:T(8,128)(2,1)S(1)}, u32[]{:S(2)}, u32[]{:S(2)}) collective-permute-start(bf16[768,640]{1,0:T(8,128)(2,1)} %other_grads.1), channel_id=1, source_target_pairs={{0,32},{32,0},{1,33},{33,1},{2,34},{34,2},{3,35},{35,3},{4,36},{36... | collective-permute-start | bytes 2949128 | tf_op jit(solution)/shard_map/ppermute | solution.py:165
  73.2 3.6 %text_grads.1 = bf16[768,640]{1,0:T(8,128)(2,1)} custom-call(f32[2]{0:T(128)S(1)} %pad_maximum_fusion.scale_ref, bf16[768,768]{1,0:T(8,128)(2,1)S(1)} %get-tuple-element.20.weights.own_weights, bf16[768,640]{1,0:T(8,128)(2,1)S(1)} %get-tuple-element.28.own_images, bf16[768,768]{1,0:T(8,128)(2,1)S(1)} %get-tuple-element.23.weights.other_weights, ...), custom_call_target="tpu_custom_call" | custom-call | flops 1509949440 | bytes 4194304 | tf_op jit(solution)/shard_map/text_grads/pallas_call | solution.py:66
  76.8 4.8 %all-to-all-start.1 = ((bf16[4,192,640]{2,1,0:T(8,128)(2,1)}), bf16[4,192,640]{2,1,0:T(8,128)(2,1)}, u32[]{:S(2)}, u32[]{:S(2)}) async-start(bf16[4,192,640]{2,1,0:T(8,128)(2,1)} %bitcast.2), calls=%async_computation.1 | async-start | bytes 1966080 | tf_op jit(solution)/shard_map/all_to_all | solution.py:163
  81.6 0.0 collective-permute-done.3.received
  81.6 2.3 %image_grads.1 = (f32[192,640]{1,0:T(8,128)S(1)}, bf16[192,640]{1,0:T(8,128)(2,1)}, bf16[192,640]{1,0:T(8,128)(2,1)}, bf16[192,640]{1,0:T(8,128)(2,1)S(1)}) custom-call(f32[2]{0:T(128)S(1)} %pad_maximum_fusion.scale_ref, s32[1]{0:T(128)} %bitcast.place_ref, bf16[768,768]{1,0:T(8,128)(2,1)S(1)} %get-tuple-element.20.weights.own_weights, ...), custom_call_target="tpu_custom_call" | custom-call | flops 754974720 | bytes 4194304 | tf_op jit(solution)/shard_map/image_grads/pallas_call | solution.py:66
  83.9 0.0 copy-start
  83.9 0.8 copy-done
  84.7 0.0 copy-start.1
  84.7 3.1 %collective-permute-start.4 = (bf16[192,640]{1,0:T(8,128)(2,1)}, bf16[192,640]{1,0:T(8,128)(2,1)S(1)}, u32[]{:S(2)}, u32[]{:S(2)}) collective-permute-start(bf16[192,640]{1,0:T(8,128)(2,1)} %get-tuple-element.25), channel_id=1, source_target_pairs={{0,64},{64,128},{128,192},{192,0},{1,65},{65,129},{129,193},{193,1... | collective-permute-start | bytes 737288 | tf_op jit(solution)/shard_map/ppermute | solution.py:171
  87.8 2.5 %collective-permute-start.5 = (bf16[192,640]{1,0:T(8,128)(2,1)}, bf16[192,640]{1,0:T(8,128)(2,1)S(1)}, u32[]{:S(2)}, u32[]{:S(2)}) collective-permute-start(bf16[192,640]{1,0:T(8,128)(2,1)} %get-tuple-element.26), channel_id=1, source_target_pairs={{0,128},{64,192},{128,0},{192,64},{1,129},{65,193},{129,1},{193,65... | collective-permute-start | bytes 737288 | tf_op jit(solution)/shard_map/ppermute | solution.py:171
  90.3 4.0 %collective-permute-start.6 = (bf16[192,640]{1,0:T(8,128)(2,1)S(1)}, bf16[192,640]{1,0:T(8,128)(2,1)S(1)}, u32[]{:S(2)}, u32[]{:S(2)}) collective-permute-start(bf16[192,640]{1,0:T(8,128)(2,1)S(1)} %get-tuple-element.27), channel_id=1, source_target_pairs={{0,192},{64,0},{128,64},{192,128},{1,193},{65,1},{129,65},{193,129... | collective-permute-start | bytes 737288 | tf_op jit(solution)/shard_map/ppermute | solution.py:171
  94.3 0.4 all-to-all-done.1
  94.6 1.4 %reduce_sum.12 = bf16[192,640]{1,0:T(8,128)(2,1)S(1)} reduce(bf16[4,192,640]{2,1,0:T(8,128)(2,1)} %all-to-all-done.1, bf16[]{:T(256)} %constant.10.clone.1), dimensions={0}, to_apply=%region_0.1 | reduce | flops 368640 | bytes 1228802 | tf_op jit(solution)/shard_map/reduce_sum | solution.py:173
  96.0 18.3 %collective-permute-start.8 = (bf16[192,640]{1,0:T(8,128)(2,1)S(1)}, bf16[192,640]{1,0:T(8,128)(2,1)S(1)}, u32[]{:S(2)}, u32[]{:S(2)}) collective-permute-start(bf16[192,640]{1,0:T(8,128)(2,1)S(1)} %reduce_sum.12), channel_id=1, source_target_pairs={{3,0},{67,1},{131,2},{195,3},{35,4},{99,5},{163,6},{227,7},{0,32},... | collective-permute-start | bytes 737288 | tf_op jit(solution)/shard_map/ppermute | solution.py:174
  114.3 0.0 collective-permute-done.4
  114.4 0.0 collective-permute-done.5
  114.4 0.0 collective-permute-done.6
  114.4 0.0 copy-done.1
  114.4 0.1 add_convert_fusion
  114.5 2.2 %collective-permute-start.7 = (bf16[192,640]{1,0:T(8,128)(2,1)S(1)}, bf16[192,640]{1,0:T(8,128)(2,1)S(1)}, u32[]{:S(2)}, u32[]{:S(2)}) collective-permute-start(bf16[192,640]{1,0:T(8,128)(2,1)S(1)} %add_convert_fusion), channel_id=1, source_target_pairs={{7,0},{71,1},{135,2},{199,3},{39,4},{103,5},{167,6},{231,7},{3,32}... | collective-permute-start | bytes 737288 | tf_op jit(solution)/shard_map/ppermute | solution.py:172
  116.7 6.2 %collective-permute-done.8 = bf16[192,640]{1,0:T(8,128)(2,1)S(1)} collective-permute-done((bf16[192,640]{1,0:T(8,128)(2,1)S(1)}, bf16[192,640]{1,0:T(8,128)(2,1)S(1)}, u32[]{:S(2)}, u32[]{:S(2)}) %collective-permute-start.8) | collective-permute-done | bytes 245792 | tf_op jit(solution)/shard_map/ppermute | solution.py:174
  122.8 0.8 convert_element_type.32
  123.7 7.9 %collective-permute-done.7 = bf16[192,640]{1,0:T(8,128)(2,1)S(1)} collective-permute-done((bf16[192,640]{1,0:T(8,128)(2,1)S(1)}, bf16[192,640]{1,0:T(8,128)(2,1)S(1)}, u32[]{:S(2)}, u32[]{:S(2)}) %collective-permute-start.7) | collective-permute-done | bytes 245792 | tf_op jit(solution)/shard_map/ppermute | solution.py:172
  131.6 0.7 copy.11
  (2 shorter events, 0.0 us)
Async XLA Ops:
  3.1 27.4 %collective-permute-start = (bf16[200,640]{1,0:T(8,128)(2,1)S(1)}, bf16[200,640]{1,0:T(8,128)(2,1)S(1)}, u32[]{:S(2)}, u32[]{:S(2)}) collective-permute-start(bf16[200,640]{1,0:T(8,128)(2,1)S(1)} %get-tuple-element.16), channel_id=1, source_target_pairs={{0,7},{1,71},{2,135},{3,199},{4,39},{5,103},{6,167},{7,231},{32,3}... | collective-permute-start | bytes 768008 | tf_op jit(solution)/shard_map/ppermute | solution.py:145
  12.5 18.0 %collective-permute-start.1 = (bf16[200,640]{1,0:T(8,128)(2,1)S(1)}, bf16[200,640]{1,0:T(8,128)(2,1)S(1)}, u32[]{:S(2)}, u32[]{:S(2)}) collective-permute-start(bf16[200,640]{1,0:T(8,128)(2,1)S(1)} %get-tuple-element.17), channel_id=1, source_target_pairs={{0,3},{1,67},{2,131},{3,195},{4,35},{5,99},{6,163},{7,227},{32,0},... | collective-permute-start | bytes 768008 | tf_op jit(solution)/shard_map/ppermute | solution.py:146
  31.5 30.5 %all-to-all-start = ((bf16[4,200,640]{2,1,0:T(8,128)(2,1)}), bf16[4,200,640]{2,1,0:T(8,128)(2,1)}, u32[]{:S(2)}, u32[]{:S(2)}) async-start(bf16[4,200,640]{2,1,0:T(8,128)(2,1)} %broadcast_in_dim.14), calls=%async_computation | async-start | bytes 2048000 | tf_op jit(solution)/shard_map/all_to_all | solution.py:148
  62.1 4.7 %collective-permute-start.2 = (bf16[4,200,640]{2,1,0:T(8,128)(2,1)}, bf16[4,200,640]{2,1,0:T(8,128)(2,1)S(1)}, u32[]{:S(2)}, u32[]{:S(2)}) collective-permute-start(bf16[4,200,640]{2,1,0:T(8,128)(2,1)} %all-to-all-done.image_ref), channel_id=1, source_target_pairs={{0,32},{32,0},{1,33},{33,1},{2,34},{34,2},{3,35},{35,3},{4,36},{36... | collective-permute-start | bytes 3072008 | tf_op jit(solution)/shard_map/ppermute | solution.py:149
  71.1 10.5 %collective-permute-start.3 = (bf16[768,640]{1,0:T(8,128)(2,1)}, bf16[768,640]{1,0:T(8,128)(2,1)S(1)}, u32[]{:S(2)}, u32[]{:S(2)}) collective-permute-start(bf16[768,640]{1,0:T(8,128)(2,1)} %other_grads.1), channel_id=1, source_target_pairs={{0,32},{32,0},{1,33},{33,1},{2,34},{34,2},{3,35},{35,3},{4,36},{36... | collective-permute-start | bytes 2949128 | tf_op jit(solution)/shard_map/ppermute | solution.py:165
  76.8 17.9 %all-to-all-start.1 = ((bf16[4,192,640]{2,1,0:T(8,128)(2,1)}), bf16[4,192,640]{2,1,0:T(8,128)(2,1)}, u32[]{:S(2)}, u32[]{:S(2)}) async-start(bf16[4,192,640]{2,1,0:T(8,128)(2,1)} %bitcast.2), calls=%async_computation.1 | async-start | bytes 1966080 | tf_op jit(solution)/shard_map/all_to_all | solution.py:163
  83.9 0.8 copy-start
  84.7 29.7 %copy-start.1 = (f32[192,640]{1,0:T(8,128)S(1)}, f32[192,640]{1,0:T(8,128)}, u32[]{:S(2)}) copy-start(f32[192,640]{1,0:T(8,128)} %copy-done) | copy-start | bytes 1474564
  84.7 29.7 %collective-permute-start.4 = (bf16[192,640]{1,0:T(8,128)(2,1)}, bf16[192,640]{1,0:T(8,128)(2,1)S(1)}, u32[]{:S(2)}, u32[]{:S(2)}) collective-permute-start(bf16[192,640]{1,0:T(8,128)(2,1)} %get-tuple-element.25), channel_id=1, source_target_pairs={{0,64},{64,128},{128,192},{192,0},{1,65},{65,129},{129,193},{193,1... | collective-permute-start | bytes 737288 | tf_op jit(solution)/shard_map/ppermute | solution.py:171
  87.8 26.6 %collective-permute-start.5 = (bf16[192,640]{1,0:T(8,128)(2,1)}, bf16[192,640]{1,0:T(8,128)(2,1)S(1)}, u32[]{:S(2)}, u32[]{:S(2)}) collective-permute-start(bf16[192,640]{1,0:T(8,128)(2,1)} %get-tuple-element.26), channel_id=1, source_target_pairs={{0,128},{64,192},{128,0},{192,64},{1,129},{65,193},{129,1},{193,65... | collective-permute-start | bytes 737288 | tf_op jit(solution)/shard_map/ppermute | solution.py:171
  90.3 24.1 %collective-permute-start.6 = (bf16[192,640]{1,0:T(8,128)(2,1)S(1)}, bf16[192,640]{1,0:T(8,128)(2,1)S(1)}, u32[]{:S(2)}, u32[]{:S(2)}) collective-permute-start(bf16[192,640]{1,0:T(8,128)(2,1)S(1)} %get-tuple-element.27), channel_id=1, source_target_pairs={{0,192},{64,0},{128,64},{192,128},{1,193},{65,1},{129,65},{193,129... | collective-permute-start | bytes 737288 | tf_op jit(solution)/shard_map/ppermute | solution.py:171
  96.0 26.8 %collective-permute-start.8 = (bf16[192,640]{1,0:T(8,128)(2,1)S(1)}, bf16[192,640]{1,0:T(8,128)(2,1)S(1)}, u32[]{:S(2)}, u32[]{:S(2)}) collective-permute-start(bf16[192,640]{1,0:T(8,128)(2,1)S(1)} %reduce_sum.12), channel_id=1, source_target_pairs={{3,0},{67,1},{131,2},{195,3},{35,4},{99,5},{163,6},{227,7},{0,32},... | collective-permute-start | bytes 737288 | tf_op jit(solution)/shard_map/ppermute | solution.py:174
  114.5 17.0 %collective-permute-start.7 = (bf16[192,640]{1,0:T(8,128)(2,1)S(1)}, bf16[192,640]{1,0:T(8,128)(2,1)S(1)}, u32[]{:S(2)}, u32[]{:S(2)}) collective-permute-start(bf16[192,640]{1,0:T(8,128)(2,1)S(1)} %add_convert_fusion), channel_id=1, source_target_pairs={{7,0},{71,1},{135,2},{199,3},{39,4},{103,5},{167,6},{231,7},{3,32}... | collective-permute-start | bytes 737288 | tf_op jit(solution)/shard_map/ppermute | solution.py:172

commit v3 on v2

--- a/solution.py
+++ b/solution.py
@@ -44,8 +44,7 @@
 
 
 def pack(rows, ids):
-    below = jnp.pad(ids.astype(jnp.bfloat16)[None, :], ((0, EXTRA - 1), (0, D - ROWS)))
-    return jnp.concatenate([rows, below], axis=0)
+    return jnp.concatenate([rows, jnp.pad(ids[None, :], ((0, EXTRA - 1), (0, D - ROWS)))], axis=0)
 
 
 def id_row(ref):
@@ -62,13 +61,14 @@
 SMEM = pl.BlockSpec(memory_space=pltpu.SMEM)
 
 
-def call(kernel, name, out, in_specs, flops, *args):
+def call(kernel, name, out, in_specs, flops, *args, scratch=()):
     return pl.pallas_call(
         kernel,
         out_shape=tuple(jax.ShapeDtypeStruct(shape, kind) for shape, kind in out),
         in_specs=in_specs,
         out_specs=(VMEM,) * len(out),
-        compiler_params=pltpu.CompilerParams(vmem_limit_bytes=24 * 1024 * 1024),
+        scratch_shapes=list(scratch),
+        compiler_params=pltpu.CompilerParams(vmem_limit_bytes=16 * 1024 * 1024),
         cost_estimate=pl.CostEstimate(flops=flops, bytes_accessed=4 << 20, transcendentals=0),
         name=name,
     )(*args)
@@ -102,45 +102,51 @@
         weights[rows, :] = pair_weights(scale_ref, images[rows, :], texts[...], columns, text_row)
 
 
-def other_kernel(scale_ref, image_ref, texts, text_ids, weights, images):
+def other_kernel(scale_ref, image_ref, texts, text_ids, own_weights, own_images, image_grads, text_grads, images, weights):
     unpack_rows(image_ref, images)
+    factor = scale_ref[0] * 0.125
     text_row = text_ids[0:1, :]
     ids = id_row(image_ref)
     for j in range(GROUP // CHUNK):
         rows = pl.ds(j * CHUNK, CHUNK)
         columns = jnp.concatenate([id_tile(ids, 2 * j), id_tile(ids, 2 * j + 1)], axis=0)
-        weights[rows, :] = pair_weights(scale_ref, images[rows, :], texts[...], columns, text_row)
-
-
-def other_grad_kernel(scale_ref, weights, texts, grads):
-    for j in range(GROUP // CHUNK):
-        rows = pl.ds(j * CHUNK, CHUNK)
-        grad = jnp.dot(weights[rows, :], texts[...], preferred_element_type=jnp.float32)
-        grads[rows, :] = (scale_ref[0] * 0.125 * grad).astype(grads.dtype)
-
-
-def text_kernel(scale_ref, own_weights, own_images, other_weights, other_images, grads):
+        weight = pair_weights(scale_ref, images[rows, :], texts[...], columns, text_row)
+        weights[rows, :] = weight
+        grad = jnp.dot(weight, texts[...], preferred_element_type=jnp.float32)
+        image_grads[rows, :] = (factor * grad).astype(image_grads.dtype)
     fold = (((0,), (0,)), ((), ()))
     for j in range(GROUP // CHUNK):
         rows = pl.ds(j * CHUNK, CHUNK)
         grad = lax.dot_general(own_weights[:, rows], own_images[...], fold, preferred_element_type=jnp.float32)
-        grad = grad + lax.dot_general(other_weights[:, rows], other_images[...], fold, preferred_element_type=jnp.float32)
-        grads[rows, :] = (scale_ref[0] * 0.125 * grad).astype(grads.dtype)
+        grad = grad + lax.dot_general(weights[:, rows], images[...], fold, preferred_element_type=jnp.float32)
+        text_grads[rows, :] = (factor * grad).astype(text_grads.dtype)
 
 
-def image_kernel(scale_ref, place_ref, weights, texts, received, kept, *sent):
-    for k, out in enumerate((kept, *sent)):
-        shard = lax.rem(place_ref[0] + k, 4)
-        rows = pl.ds(pl.multiple_of(shard * ROWS, ROWS), ROWS)
-        grad = jnp.dot(weights[rows, :], texts[...], preferred_element_type=jnp.float32)
-        out[...] = (scale_ref[0] * 0.125 * grad + received[rows, :].astype(jnp.float32)).astype(out.dtype)
+def image_shard(scale_ref, shard, weights, texts, received):
+    rows = pl.ds(pl.multiple_of(shard * ROWS, ROWS), ROWS)
+    grad = jnp.dot(weights[rows, :], texts[...], preferred_element_type=jnp.float32)
+    return scale_ref[0] * 0.125 * grad + received[rows, :].astype(jnp.float32)
+
+
+def image_kernel(scale_ref, place_ref, weights, texts, received, *sent):
+    for k, out in enumerate(sent, 1):
+        out[...] = image_shard(scale_ref, lax.rem(place_ref[0] + k, 4), weights, texts, received).astype(out.dtype)
+
+
+def image_sum_kernel(scale_ref, place_ref, weights, texts, received, *rest):
+    *parts, out = rest
+    total = image_shard(scale_ref, place_ref[0], weights, texts, received)
+    for part in parts:
+        total = total + part[...].astype(jnp.float32)
+    out[...] = total.astype(out.dtype)
 
 
 def body(picture_vectors, caption_vectors, picture_match_label, caption_match_label, inverse_softness, score_offset):
     scale = jnp.concatenate([inverse_softness, score_offset])
     place = lax.axis_index("x").astype(jnp.int32).reshape(1)
-    packed_images = pack(picture_vectors, picture_match_label)
-    packed_texts = pack(caption_vectors, caption_match_label)
+    labels = lax.optimization_barrier(jnp.stack([picture_match_label, caption_match_label]).astype(jnp.bfloat16))
+    packed_images = pack(picture_vectors, labels[0])
+    packed_texts = pack(caption_vectors, labels[1])
     packed_images, packed_texts = lax.optimization_barrier((packed_images, packed_texts))
     images = lax.ppermute(packed_images, MOVE_AXES, IMAGE_ROUTE)
     texts = lax.ppermute(packed_texts, MOVE_AXES, TEXT_ROUTE)
@@ -154,23 +160,18 @@
     own_weights, own_images, all_texts, text_ids = call(
         own_kernel, "own_weights", ((half, bf16), (rows, bf16), (rows, bf16), ((8, GROUP), f32)), [SMEM, VMEM, VMEM], 40 * flops, scale, own, text
     )
-    other_weights, other_images = call(
-        other_kernel, "other_weights", ((half, bf16), (rows, bf16)), [SMEM, VMEM, VMEM, VMEM], flops, scale, other, all_texts, text_ids
+    other_grad, text_part = call(
+        other_kernel, "other_grads", ((rows, bf16), (rows, bf16)), [SMEM] + [VMEM] * 5, 4 * flops, scale, other, all_texts, text_ids, own_weights, own_images,
+        scratch=[pltpu.VMEM(rows, bf16), pltpu.VMEM(half, bf16)],
     )
-    (text_part,) = call(
-        text_kernel, "text_grads", ((rows, bf16),), [SMEM] + [VMEM] * 4, 2 * flops, scale, own_weights, own_images, other_weights, other_images
-    )
+    received = lax.ppermute(other_grad, "c", [(0, 1), (1, 0)])
     text_parts = lax.all_to_all(text_part, "y", split_axis=0, concat_axis=0, tiled=True)
-    (other_grad,) = call(other_grad_kernel, "other_grads", ((rows, bf16),), [SMEM, VMEM, VMEM], flops, scale, other_weights, all_texts)
-    received = lax.ppermute(other_grad, "c", [(0, 1), (1, 0)])
-    shard = (ROWS, D)
-    kept, *sent = call(
-        image_kernel, "image_grads", ((shard, f32),) + ((shard, bf16),) * 3, [SMEM, SMEM] + [VMEM] * 3, flops, scale, place, own_weights, all_texts, received
-    )
-    for k, part in enumerate(sent, 1):
-        kept = kept + lax.ppermute(part, "x", [(i, (i + k) % 4) for i in range(4)]).astype(f32)
-    image_home = lax.ppermute(kept.astype(bf16), MOVE_AXES, back(IMAGE_ROUTE))
-    text_sum = jnp.sum(text_parts.reshape(4, ROWS, D).astype(f32), axis=0).astype(bf16)
+    shard = ((ROWS, D), bf16)
+    sent = call(image_kernel, "image_grads", (shard,) * 3, [SMEM, SMEM] + [VMEM] * 3, 0, scale, place, own_weights, all_texts, received)
+    parts = [lax.ppermute(part, "x", [(i, (i + k) % 4) for i in range(4)]) for k, part in enumerate(sent, 1)]
+    (kept,) = call(image_sum_kernel, "image_sum", (shard,), [SMEM, SMEM] + [VMEM] * 6, 0, scale, place, own_weights, all_texts, received, *parts)
+    image_home = lax.ppermute(kept, MOVE_AXES, back(IMAGE_ROUTE))
+    text_sum = sum(text_parts[k * ROWS : (k + 1) * ROWS].astype(f32) for k in range(4)).astype(bf16)
     text_home = lax.ppermute(text_sum, MOVE_AXES, back(TEXT_ROUTE))
     return image_home, text_home.astype(f32)
 

time: 133 us -> 131 us (0.985)
  Pallas kernels: 12.6 us -> 10.7 us
    pallas_call x5 -> x4, Pallas kernels: 12.6 us -> 10.7 us  [call(): pl.pallas_call(kernel, out_shape=tuple((jax.ShapeDtypeStruct(shape, kind)...]
    convert_element_type x3 -> x0, other arithmetic: 1.48 us -> none  [the longest x2 1.36 us: pack(): ids.astype(jnp.bfloat16)[None, :]]
    add x0 -> x1, other arithmetic: none -> 1.43 us  [body(): sum((text_parts[k * ROWS:(k + 1) * ROWS].astype(f32) for k in range(4)))]
    reduce_sum x1 -> x0, other arithmetic: 1.4 us -> none  [body(): jnp.sum(text_parts.reshape(4, ROWS, D).astype(f32), axis=0).astype(bf16)]
    another operation x0 -> x3, other arithmetic: none -> 1.38 us
    ppermute x1, waiting for transfers between devices: 6.16 us -> 4.8 us  [body(): text_home = lax.ppermute(text_sum, MOVE_AXES, back(TEXT_ROUTE))]
  transfers between devices with their start and end apart: 11 -> 11, of which waited for: 5 -> 5; matrix products, arithmetic and copies ran while one was open for 2% -> 2% of each run, Pallas kernels for 6% -> 5%
where the time goes in v3:
time: 131 us; the launch traced here: 130 us
  starting transfers between devices  71.7 us (55%)
  waiting for transfers between devices  25.6 us (20%)
  blocking collectives  12.8 us (10%)
  Pallas kernels  10.7 us (8%)
  other arithmetic  4.81 us (4%)
  local copies, waits for them, and re-layouts  2.75 us (2%)
  between operations  2.07 us (2%)
    ppermute x1, starting transfers between devices, body(): text_home = lax.ppermute(text_sum, MOVE_AXES, back(TEXT_ROUTE))  18.3 us
    all_to_all x1, starting transfers between devices, body(): lax.all_to_all(jnp.broadcast_to(images[None], (4, PACKED, D)), 'x', split...  16.4 us
    all_gather x1, blocking collectives, body(): text = lax.all_gather(texts, 'y', axis=0)  12.8 us
    pallas_call x4, Pallas kernels, call(): pl.pallas_call(kernel, out_shape=tuple((jax.ShapeDtypeStruct(shape, kind)...  10.7 us
    ppermute x1, waiting for transfers between devices, body(): images = lax.ppermute(packed_images, MOVE_AXES, IMAGE_ROUTE)  10.4 us
    ppermute x3, starting transfers between devices, body(): lax.ppermute(part, 'x', [(i, (i + k) % 4) for i in range(4)])  9.39 us
    ppermute x1, starting transfers between devices, body(): images = lax.ppermute(packed_images, MOVE_AXES, IMAGE_ROUTE)  9.35 us
    ppermute x1, waiting for transfers between devices, body(): image_home = lax.ppermute(kept, MOVE_AXES, back(IMAGE_ROUTE))  8.55 us
  transfers between devices with their start and end apart: 11, of which 5 were waited for; matrix products, arithmetic and copies ran while one was open for 2% of the time, Pallas kernels for 5%

profile of v3, /device:TPU:43, one launch (start us, length us, event | category | flops | bytes accessed | tf_op | source)
XLA Modules:
  0.0 130.4 jit_solution(6164234570264711642)
XLA Ops:
  0.6 0.7 convert.11
  1.3 0.7 convert.12
  2.0 1.1 fusion.2
  3.1 9.3 %collective-permute-start = (bf16[200,640]{1,0:T(8,128)(2,1)S(1)}, bf16[200,640]{1,0:T(8,128)(2,1)S(1)}, u32[]{:S(2)}, u32[]{:S(2)}) collective-permute-start(bf16[200,640]{1,0:T(8,128)(2,1)S(1)} %get-tuple-element.15), channel_id=1, source_target_pairs={{0,7},{1,71},{2,135},{3,199},{4,39},{5,103},{6,167},{7,231},{32,3}... | collective-permute-start | bytes 768008 | tf_op jit(solution)/shard_map/ppermute | solution.py:151
  12.5 7.6 %collective-permute-start.1 = (bf16[200,640]{1,0:T(8,128)(2,1)S(1)}, bf16[200,640]{1,0:T(8,128)(2,1)S(1)}, u32[]{:S(2)}, u32[]{:S(2)}) collective-permute-start(bf16[200,640]{1,0:T(8,128)(2,1)S(1)} %get-tuple-element.16), channel_id=1, source_target_pairs={{0,3},{1,67},{2,131},{3,195},{4,35},{5,99},{6,163},{7,227},{32,0},... | collective-permute-start | bytes 768008 | tf_op jit(solution)/shard_map/ppermute | solution.py:152
  20.2 10.4 %collective-permute-done = bf16[200,640]{1,0:T(8,128)(2,1)S(1)} collective-permute-done((bf16[200,640]{1,0:T(8,128)(2,1)S(1)}, bf16[200,640]{1,0:T(8,128)(2,1)S(1)}, u32[]{:S(2)}, u32[]{:S(2)}) %collective-permute-start) | collective-permute-done | bytes 256032 | tf_op jit(solution)/shard_map/ppermute | solution.py:151
  30.5 0.0 collective-permute-done.1
  30.5 1.1 broadcast_in_dim.2
  31.6 16.4 %all-to-all-start = ((bf16[4,200,640]{2,1,0:T(8,128)(2,1)}), bf16[4,200,640]{2,1,0:T(8,128)(2,1)}, u32[]{:S(2)}, u32[]{:S(2)}) async-start(bf16[4,200,640]{2,1,0:T(8,128)(2,1)} %broadcast_in_dim.2), calls=%async_computation | async-start | bytes 2048000 | tf_op jit(solution)/shard_map/all_to_all | solution.py:154
  49.2 0.1 pad_maximum_fusion.1.scale_ref
  49.3 12.8 %all-gather = bf16[800,640]{1,0:T(8,128)(2,1)S(1)} all-gather(bf16[200,640]{1,0:T(8,128)(2,1)S(1)} %collective-permute-done.1), channel_id=2, replica_groups=mesh['h'=2,'x'=4,'c'=2,'y'=4,'z'=8] {'y'}, dimensions={0}, use_global_device_ids=true | all-gather | bytes 1280000 | tf_op jit(solution)/shard_map/all_gather | solution.py:156
  62.1 0.0 all-to-all-done.image_ref
  62.1 1.9 %collective-permute-start.2 = (bf16[4,200,640]{2,1,0:T(8,128)(2,1)}, bf16[4,200,640]{2,1,0:T(8,128)(2,1)S(1)}, u32[]{:S(2)}, u32[]{:S(2)}) collective-permute-start(bf16[4,200,640]{2,1,0:T(8,128)(2,1)} %all-to-all-done.image_ref), channel_id=1, source_target_pairs={{0,32},{32,0},{1,33},{33,1},{2,34},{34,2},{3,35},{35,3},{4,36},{36... | collective-permute-start | bytes 3072008 | tf_op jit(solution)/shard_map/ppermute | solution.py:155
  64.0 2.4 %own_weights.1 = (bf16[768,768]{1,0:T(8,128)(2,1)S(1)}, bf16[768,640]{1,0:T(8,128)(2,1)S(1)}, bf16[768,640]{1,0:T(8,128)(2,1)S(1)}, f32[8,768]{1,0:T(8,128)S(1)}) custom-call(f32[2]{0:T(128)S(1)} %pad_maximum_fusion.1.scale_ref, bf16[4,200,640]{2,1,0:T(8,128)(2,1)} %all-to-all-done.image_ref, bf16[4,200,640]{2,1,0:T(8,128)(2,1)S(1)} %bitcast.5), custom_call_target="tpu_custom_call" | custom-call | flops 30198988800 | bytes 4194304 | tf_op jit(solution)/shard_map/own_weights/pallas_call | solution.py:65
  66.5 0.4 collective-permute-done.2.image_ref
  66.9 4.6 %other_grads.1 = (bf16[768,640]{1,0:T(8,128)(2,1)}, bf16[768,640]{1,0:T(8,128)(2,1)S(1)}) custom-call(f32[2]{0:T(128)S(1)} %pad_maximum_fusion.1.scale_ref, bf16[4,200,640]{2,1,0:T(8,128)(2,1)S(1)} %collective-permute-done.2.image_ref, bf16[768,640]{1,0:T(8,128)(2,1)S(1)} %get-tuple-element.20.texts, f32[8,768]{1,0:T(8,128)S(1)} %get-tuple-element.21.text_ids, ...), custom_call_target="tpu_custom_call" | custom-call | flops 3019898880 | bytes 4194304 | tf_op jit(solution)/shard_map/other_grads/pallas_call | solution.py:65
  71.4 0.0 copy-start
  71.5 1.0 copy-done
  72.4 2.0 %collective-permute-start.3 = (bf16[768,640]{1,0:T(8,128)(2,1)}, bf16[768,640]{1,0:T(8,128)(2,1)S(1)}, u32[]{:S(2)}, u32[]{:S(2)}) collective-permute-start(bf16[768,640]{1,0:T(8,128)(2,1)} %get-tuple-element.23), channel_id=1, source_target_pairs={{0,32},{32,0},{1,33},{33,1},{2,34},{34,2},{3,35},{35,3},{4,36},{36... | collective-permute-start | bytes 2949128 | tf_op jit(solution)/shard_map/ppermute | solution.py:167
  74.5 4.8 %all-to-all-start.1 = ((bf16[4,192,640]{2,1,0:T(8,128)(2,1)}), bf16[4,192,640]{2,1,0:T(8,128)(2,1)}, u32[]{:S(2)}, u32[]{:S(2)}) async-start(bf16[4,192,640]{2,1,0:T(8,128)(2,1)} %bitcast.6), calls=%async_computation.1 | async-start | bytes 1966080 | tf_op jit(solution)/shard_map/all_to_all | solution.py:168
  79.3 0.0 collective-permute-done.3.received
  79.3 2.1 %image_grads.1 = (bf16[192,640]{1,0:T(8,128)(2,1)}, bf16[192,640]{1,0:T(8,128)(2,1)}, bf16[192,640]{1,0:T(8,128)(2,1)}) custom-call(f32[2]{0:T(128)S(1)} %pad_maximum_fusion.1.scale_ref, s32[1]{0:T(128)} %bitcast.place_ref, bf16[768,768]{1,0:T(8,128)(2,1)S(1)} %get-tuple-element.19.own_weights.weights, bf16[768,640]{1,0:T(8,128)(2,1)S(1)} %get-tuple-element.20.texts, ...), custom_call_target="tpu_custom_call" | custom-call | bytes 4194304 | tf_op jit(solution)/shard_map/image_grads/pallas_call | solution.py:65
  81.4 2.9 %collective-permute-start.4 = (bf16[192,640]{1,0:T(8,128)(2,1)}, bf16[192,640]{1,0:T(8,128)(2,1)S(1)}, u32[]{:S(2)}, u32[]{:S(2)}) collective-permute-start(bf16[192,640]{1,0:T(8,128)(2,1)} %get-tuple-element.24), channel_id=1, source_target_pairs={{0,64},{64,128},{128,192},{192,0},{1,65},{65,129},{129,193},{193,1... | collective-permute-start | bytes 737288 | tf_op jit(solution)/shard_map/ppermute | solution.py:171
  84.3 2.5 %collective-permute-start.5 = (bf16[192,640]{1,0:T(8,128)(2,1)}, bf16[192,640]{1,0:T(8,128)(2,1)}, u32[]{:S(2)}, u32[]{:S(2)}) collective-permute-start(bf16[192,640]{1,0:T(8,128)(2,1)} %get-tuple-element.25), channel_id=1, source_target_pairs={{0,128},{64,192},{128,0},{192,64},{1,129},{65,193},{129,1},{193,65... | collective-permute-start | bytes 737288 | tf_op jit(solution)/shard_map/ppermute | solution.py:171
  86.8 4.0 %collective-permute-start.6 = (bf16[192,640]{1,0:T(8,128)(2,1)}, bf16[192,640]{1,0:T(8,128)(2,1)}, u32[]{:S(2)}, u32[]{:S(2)}) collective-permute-start(bf16[192,640]{1,0:T(8,128)(2,1)} %get-tuple-element.26), channel_id=1, source_target_pairs={{0,192},{64,0},{128,64},{192,128},{1,193},{65,1},{129,65},{193,129... | collective-permute-start | bytes 737288 | tf_op jit(solution)/shard_map/ppermute | solution.py:171
  90.8 1.5 %all-to-all-done.1 = bf16[4,192,640]{2,1,0:T(8,128)(2,1)} async-done(((bf16[4,192,640]{2,1,0:T(8,128)(2,1)}), bf16[4,192,640]{2,1,0:T(8,128)(2,1)}, u32[]{:S(2)}, u32[]{:S(2)}) %all-to-all-start.1) | async-done | bytes 983072 | tf_op jit(solution)/shard_map/all_to_all | solution.py:168
  92.4 1.4 %fusion.4 = bf16[192,640]{1,0:T(8,128)(2,1)S(1)} fusion(bf16[4,192,640]{2,1,0:T(8,128)(2,1)} %all-to-all-done.1), kind=kLoop, calls=%fused_computation.6 | loop fusion | flops 983040 | bytes 1228800 | tf_op jit(solution)/shard_map/add | solution.py:174
  93.8 18.3 %collective-permute-start.8 = (bf16[192,640]{1,0:T(8,128)(2,1)S(1)}, bf16[192,640]{1,0:T(8,128)(2,1)S(1)}, u32[]{:S(2)}, u32[]{:S(2)}) collective-permute-start(bf16[192,640]{1,0:T(8,128)(2,1)S(1)} %fusion.4), channel_id=1, source_target_pairs={{3,0},{67,1},{131,2},{195,3},{35,4},{99,5},{163,6},{227,7},{0,32},... | collective-permute-start | bytes 737288 | tf_op jit(solution)/shard_map/ppermute | solution.py:175
  112.1 0.0 collective-permute-done.4.rest_0_
  112.1 0.0 collective-permute-done.5.rest_1_
  112.1 0.0 collective-permute-done.6.rest_2_
  112.1 1.5 %image_sum.1 = bf16[192,640]{1,0:T(8,128)(2,1)S(1)} custom-call(f32[2]{0:T(128)S(1)} %pad_maximum_fusion.1.scale_ref, s32[1]{0:T(128)} %bitcast.place_ref, bf16[768,768]{1,0:T(8,128)(2,1)S(1)} %get-tuple-element.19.own_weights.weights, bf16[768,640]{1,0:T(8,128)(2,1)S(1)} %get-tuple-element.20.texts, bf16[768,640]{1,0:T(8,128)(2,1)S(1)} %collective-permute-done.3.received, ...), custom_call_target="tpu_custom_call" | custom-call | bytes 4194304 | tf_op jit(solution)/shard_map/image_sum/pallas_call | solution.py:65
  113.6 1.9 %collective-permute-start.7 = (bf16[192,640]{1,0:T(8,128)(2,1)S(1)}, bf16[192,640]{1,0:T(8,128)(2,1)S(1)}, u32[]{:S(2)}, u32[]{:S(2)}) collective-permute-start(bf16[192,640]{1,0:T(8,128)(2,1)S(1)} %image_sum.1), channel_id=1, source_target_pairs={{7,0},{71,1},{135,2},{199,3},{39,4},{103,5},{167,6},{231,7},{3,32}... | collective-permute-start | bytes 737288 | tf_op jit(solution)/shard_map/ppermute | solution.py:173
  115.6 4.8 %collective-permute-done.8 = bf16[192,640]{1,0:T(8,128)(2,1)S(1)} collective-permute-done((bf16[192,640]{1,0:T(8,128)(2,1)S(1)}, bf16[192,640]{1,0:T(8,128)(2,1)S(1)}, u32[]{:S(2)}, u32[]{:S(2)}) %collective-permute-start.8) | collective-permute-done | bytes 245792 | tf_op jit(solution)/shard_map/ppermute | solution.py:175
  120.4 0.8 convert_element_type.28
  121.2 8.5 %collective-permute-done.7 = bf16[192,640]{1,0:T(8,128)(2,1)S(1)} collective-permute-done((bf16[192,640]{1,0:T(8,128)(2,1)S(1)}, bf16[192,640]{1,0:T(8,128)(2,1)S(1)}, u32[]{:S(2)}, u32[]{:S(2)}) %collective-permute-start.7) | collective-permute-done | bytes 245792 | tf_op jit(solution)/shard_map/ppermute | solution.py:173
  129.7 0.7 copy.11
  (4 shorter events, 0.0 us)
Async XLA Ops:
  3.1 27.4 %collective-permute-start = (bf16[200,640]{1,0:T(8,128)(2,1)S(1)}, bf16[200,640]{1,0:T(8,128)(2,1)S(1)}, u32[]{:S(2)}, u32[]{:S(2)}) collective-permute-start(bf16[200,640]{1,0:T(8,128)(2,1)S(1)} %get-tuple-element.15), channel_id=1, source_target_pairs={{0,7},{1,71},{2,135},{3,199},{4,39},{5,103},{6,167},{7,231},{32,3}... | collective-permute-start | bytes 768008 | tf_op jit(solution)/shard_map/ppermute | solution.py:151
  12.5 18.0 %collective-permute-start.1 = (bf16[200,640]{1,0:T(8,128)(2,1)S(1)}, bf16[200,640]{1,0:T(8,128)(2,1)S(1)}, u32[]{:S(2)}, u32[]{:S(2)}) collective-permute-start(bf16[200,640]{1,0:T(8,128)(2,1)S(1)} %get-tuple-element.16), channel_id=1, source_target_pairs={{0,3},{1,67},{2,131},{3,195},{4,35},{5,99},{6,163},{7,227},{32,0},... | collective-permute-start | bytes 768008 | tf_op jit(solution)/shard_map/ppermute | solution.py:152
  31.6 30.6 %all-to-all-start = ((bf16[4,200,640]{2,1,0:T(8,128)(2,1)}), bf16[4,200,640]{2,1,0:T(8,128)(2,1)}, u32[]{:S(2)}, u32[]{:S(2)}) async-start(bf16[4,200,640]{2,1,0:T(8,128)(2,1)} %broadcast_in_dim.2), calls=%async_computation | async-start | bytes 2048000 | tf_op jit(solution)/shard_map/all_to_all | solution.py:154
  62.1 4.7 %collective-permute-start.2 = (bf16[4,200,640]{2,1,0:T(8,128)(2,1)}, bf16[4,200,640]{2,1,0:T(8,128)(2,1)S(1)}, u32[]{:S(2)}, u32[]{:S(2)}) collective-permute-start(bf16[4,200,640]{2,1,0:T(8,128)(2,1)} %all-to-all-done.image_ref), channel_id=1, source_target_pairs={{0,32},{32,0},{1,33},{33,1},{2,34},{34,2},{3,35},{35,3},{4,36},{36... | collective-permute-start | bytes 3072008 | tf_op jit(solution)/shard_map/ppermute | solution.py:155
  71.4 1.0 copy-start
  72.4 6.9 %collective-permute-start.3 = (bf16[768,640]{1,0:T(8,128)(2,1)}, bf16[768,640]{1,0:T(8,128)(2,1)S(1)}, u32[]{:S(2)}, u32[]{:S(2)}) collective-permute-start(bf16[768,640]{1,0:T(8,128)(2,1)} %get-tuple-element.23), channel_id=1, source_target_pairs={{0,32},{32,0},{1,33},{33,1},{2,34},{34,2},{3,35},{35,3},{4,36},{36... | collective-permute-start | bytes 2949128 | tf_op jit(solution)/shard_map/ppermute | solution.py:167
  74.5 17.9 %all-to-all-start.1 = ((bf16[4,192,640]{2,1,0:T(8,128)(2,1)}), bf16[4,192,640]{2,1,0:T(8,128)(2,1)}, u32[]{:S(2)}, u32[]{:S(2)}) async-start(bf16[4,192,640]{2,1,0:T(8,128)(2,1)} %bitcast.6), calls=%async_computation.1 | async-start | bytes 1966080 | tf_op jit(solution)/shard_map/all_to_all | solution.py:168
  81.4 30.7 %collective-permute-start.4 = (bf16[192,640]{1,0:T(8,128)(2,1)}, bf16[192,640]{1,0:T(8,128)(2,1)S(1)}, u32[]{:S(2)}, u32[]{:S(2)}) collective-permute-start(bf16[192,640]{1,0:T(8,128)(2,1)} %get-tuple-element.24), channel_id=1, source_target_pairs={{0,64},{64,128},{128,192},{192,0},{1,65},{65,129},{129,193},{193,1... | collective-permute-start | bytes 737288 | tf_op jit(solution)/shard_map/ppermute | solution.py:171
  84.3 27.8 %collective-permute-start.5 = (bf16[192,640]{1,0:T(8,128)(2,1)}, bf16[192,640]{1,0:T(8,128)(2,1)}, u32[]{:S(2)}, u32[]{:S(2)}) collective-permute-start(bf16[192,640]{1,0:T(8,128)(2,1)} %get-tuple-element.25), channel_id=1, source_target_pairs={{0,128},{64,192},{128,0},{192,64},{1,129},{65,193},{129,1},{193,65... | collective-permute-start | bytes 737288 | tf_op jit(solution)/shard_map/ppermute | solution.py:171
  86.8 25.2 %collective-permute-start.6 = (bf16[192,640]{1,0:T(8,128)(2,1)}, bf16[192,640]{1,0:T(8,128)(2,1)}, u32[]{:S(2)}, u32[]{:S(2)}) collective-permute-start(bf16[192,640]{1,0:T(8,128)(2,1)} %get-tuple-element.26), channel_id=1, source_target_pairs={{0,192},{64,0},{128,64},{192,128},{1,193},{65,1},{129,65},{193,129... | collective-permute-start | bytes 737288 | tf_op jit(solution)/shard_map/ppermute | solution.py:171
  93.8 26.6 %collective-permute-start.8 = (bf16[192,640]{1,0:T(8,128)(2,1)S(1)}, bf16[192,640]{1,0:T(8,128)(2,1)S(1)}, u32[]{:S(2)}, u32[]{:S(2)}) collective-permute-start(bf16[192,640]{1,0:T(8,128)(2,1)S(1)} %fusion.4), channel_id=1, source_target_pairs={{3,0},{67,1},{131,2},{195,3},{35,4},{99,5},{163,6},{227,7},{0,32},... | collective-permute-start | bytes 737288 | tf_op jit(solution)/shard_map/ppermute | solution.py:175
  113.6 16.1 %collective-permute-start.7 = (bf16[192,640]{1,0:T(8,128)(2,1)S(1)}, bf16[192,640]{1,0:T(8,128)(2,1)S(1)}, u32[]{:S(2)}, u32[]{:S(2)}) collective-permute-start(bf16[192,640]{1,0:T(8,128)(2,1)S(1)} %image_sum.1), channel_id=1, source_target_pairs={{7,0},{71,1},{135,2},{199,3},{39,4},{103,5},{167,6},{231,7},{3,32}... | collective-permute-start | bytes 737288 | tf_op jit(solution)/shard_map/ppermute | solution.py:173

commit v4 on v3

--- a/solution.py
+++ b/solution.py
@@ -44,7 +44,8 @@
 
 
 def pack(rows, ids):
-    return jnp.concatenate([rows, jnp.pad(ids[None, :], ((0, EXTRA - 1), (0, D - ROWS)))], axis=0)
+    below = jnp.broadcast_to(ids.astype(jnp.bfloat16)[None, :], (EXTRA, ROWS))
+    return jnp.concatenate([rows, jnp.pad(below, ((0, 0), (0, D - ROWS)))], axis=0)
 
 
 def id_row(ref):
@@ -90,11 +91,14 @@
     return jnp.broadcast_to(ids[:, j * 128 : (j + 1) * 128], (128, 128)).T
 
 
-def own_kernel(scale_ref, image_ref, text_ref, weights, images, texts, text_ids):
+def unpack_kernel(text_ref, texts, text_ids):
     unpack_rows(text_ref, texts)
+    text_ids[...] = jnp.broadcast_to(id_row(text_ref), text_ids.shape)
+
+
+def own_kernel(scale_ref, image_ref, texts, text_ids, weights, images):
     unpack_rows(image_ref, images)
-    text_row = id_row(text_ref)
-    text_ids[...] = jnp.broadcast_to(text_row, text_ids.shape)
+    text_row = text_ids[0:1, :]
     ids = id_row(image_ref)
     for j in range(GROUP // CHUNK):
         rows = pl.ds(j * CHUNK, CHUNK)
@@ -141,24 +145,30 @@
     out[...] = total.astype(out.dtype)
 
 
+def text_sum_kernel(parts, out):
+    total = parts[0:ROWS, :].astype(jnp.float32)
+    for k in range(1, 4):
+        total = total + parts[k * ROWS : (k + 1) * ROWS, :].astype(jnp.float32)
+    out[...] = total.astype(out.dtype)
+
+
 def body(picture_vectors, caption_vectors, picture_match_label, caption_match_label, inverse_softness, score_offset):
     scale = jnp.concatenate([inverse_softness, score_offset])
     place = lax.axis_index("x").astype(jnp.int32).reshape(1)
-    labels = lax.optimization_barrier(jnp.stack([picture_match_label, caption_match_label]).astype(jnp.bfloat16))
-    packed_images = pack(picture_vectors, labels[0])
-    packed_texts = pack(caption_vectors, labels[1])
+    packed_images = pack(picture_vectors, picture_match_label)
+    packed_texts = pack(caption_vectors, caption_match_label)
     packed_images, packed_texts = lax.optimization_barrier((packed_images, packed_texts))
     images = lax.ppermute(packed_images, MOVE_AXES, IMAGE_ROUTE)
     texts = lax.ppermute(packed_texts, MOVE_AXES, TEXT_ROUTE)
-    images, texts = lax.optimization_barrier((images, texts))
     own = lax.all_to_all(jnp.broadcast_to(images[None], (4, PACKED, D)), "x", split_axis=0, concat_axis=0, tiled=True)
     other = lax.ppermute(own, "c", [(0, 1), (1, 0)])
     text = lax.all_gather(texts, "y", axis=0)
     half, flops = (GROUP, GROUP), 2 * GROUP * GROUP * D
     rows = (GROUP, D)
     bf16, f32 = jnp.bfloat16, jnp.float32
-    own_weights, own_images, all_texts, text_ids = call(
-        own_kernel, "own_weights", ((half, bf16), (rows, bf16), (rows, bf16), ((8, GROUP), f32)), [SMEM, VMEM, VMEM], 40 * flops, scale, own, text
+    all_texts, text_ids = call(unpack_kernel, "unpack_texts", ((rows, bf16), ((8, GROUP), f32)), [VMEM], 40 * flops, text)
+    own_weights, own_images = call(
+        own_kernel, "own_weights", ((half, bf16), (rows, bf16)), [SMEM, VMEM, VMEM, VMEM], 40 * flops, scale, own, all_texts, text_ids
     )
     other_grad, text_part = call(
         other_kernel, "other_grads", ((rows, bf16), (rows, bf16)), [SMEM] + [VMEM] * 5, 4 * flops, scale, other, all_texts, text_ids, own_weights, own_images,
@@ -171,7 +181,7 @@
     parts = [lax.ppermute(part, "x", [(i, (i + k) % 4) for i in range(4)]) for k, part in enumerate(sent, 1)]
     (kept,) = call(image_sum_kernel, "image_sum", (shard,), [SMEM, SMEM] + [VMEM] * 6, 0, scale, place, own_weights, all_texts, received, *parts)
     image_home = lax.ppermute(kept, MOVE_AXES, back(IMAGE_ROUTE))
-    text_sum = sum(text_parts[k * ROWS : (k + 1) * ROWS].astype(f32) for k in range(4)).astype(bf16)
+    (text_sum,) = call(text_sum_kernel, "text_sum", (shard,), [VMEM], 0, text_parts)
     text_home = lax.ppermute(text_sum, MOVE_AXES, back(TEXT_ROUTE))
     return image_home, text_home.astype(f32)
 

time: 131 us -> 126 us (0.962)
  the two profiles are of different devices: /device:TPU:43 before, /device:TPU:225 now
where the time goes in v4:
time: 126 us; the launch traced here: 125 us
  starting transfers between devices  73.6 us (58%)
  waiting for transfers between devices  20.5 us (16%)
  blocking collectives  11.7 us (9%)
  Pallas kernels  11.4 us (9%)
  other arithmetic  3.36 us (3%)
  local copies, waits for them, and re-layouts  2.75 us (2%)
  between operations  2.12 us (2%)
    ppermute x3, starting transfers between devices, body(): lax.ppermute(part, 'x', [(i, (i + k) % 4) for i in range(4)])  19.1 us
    all_to_all x1, starting transfers between devices, body(): lax.all_to_all(jnp.broadcast_to(images[None], (4, PACKED, D)), 'x', split...  15.1 us
    ppermute x1, waiting for transfers between devices, body(): image_home = lax.ppermute(kept, MOVE_AXES, back(IMAGE_ROUTE))  14.6 us
    all_gather x1, blocking collectives, body(): text = lax.all_gather(texts, 'y', axis=0)  11.7 us
    pallas_call x6, Pallas kernels, call(): pl.pallas_call(kernel, out_shape=tuple((jax.ShapeDtypeStruct(shape, kind)...  11.4 us
    ppermute x1, starting transfers between devices, body(): other = lax.ppermute(own, 'c', [(0, 1), (1, 0)])  11.1 us
    ppermute x1, starting transfers between devices, body(): text_home = lax.ppermute(text_sum, MOVE_AXES, back(TEXT_ROUTE))  9.33 us
    ppermute x1, starting transfers between devices, body(): texts = lax.ppermute(packed_texts, MOVE_AXES, TEXT_ROUTE)  8.01 us
  transfers between devices with their start and end apart: 11, of which 3 were waited for; matrix products, arithmetic and copies ran while one was open for 2% of the time, Pallas kernels for 5%

profile of v4, /device:TPU:225, one launch (start us, length us, event | category | flops | bytes accessed | tf_op | source)
XLA Modules:
  0.0 125.5 jit_solution(3651882248282573494)
XLA Ops:
  0.6 0.7 convert_element_type.12
  1.3 0.7 convert_element_type.13
  2.0 1.1 pad_maximum_fusion
  3.1 2.6 %collective-permute-start = (bf16[200,640]{1,0:T(8,128)(2,1)S(1)}, bf16[200,640]{1,0:T(8,128)(2,1)S(1)}, u32[]{:S(2)}, u32[]{:S(2)}) collective-permute-start(bf16[200,640]{1,0:T(8,128)(2,1)S(1)} %get-tuple-element.13), channel_id=1, source_target_pairs={{0,7},{1,71},{2,135},{3,199},{4,39},{5,103},{6,167},{7,231},{32,3}... | collective-permute-start | bytes 768008 | tf_op jit(solution)/shard_map/ppermute | solution.py:161
  5.7 8.0 %collective-permute-start.1 = (bf16[200,640]{1,0:T(8,128)(2,1)S(1)}, bf16[200,640]{1,0:T(8,128)(2,1)S(1)}, u32[]{:S(2)}, u32[]{:S(2)}) collective-permute-start(bf16[200,640]{1,0:T(8,128)(2,1)S(1)} %get-tuple-element.14), channel_id=1, source_target_pairs={{0,3},{1,67},{2,131},{3,195},{4,35},{5,99},{6,163},{7,227},{32,0},... | collective-permute-start | bytes 768008 | tf_op jit(solution)/shard_map/ppermute | solution.py:162
  15.0 0.1 pad_maximum_fusion.2.scale_ref
  15.1 0.0 collective-permute-done
  15.1 1.1 broadcast_in_dim.2
  16.2 15.1 %all-to-all-start = ((bf16[4,200,640]{2,1,0:T(8,128)(2,1)}), bf16[4,200,640]{2,1,0:T(8,128)(2,1)S(1)}, u32[]{:S(2)}, u32[]{:S(2)}) async-start(bf16[4,200,640]{2,1,0:T(8,128)(2,1)} %broadcast_in_dim.2), calls=%async_computation | async-start | bytes 2048000 | tf_op jit(solution)/shard_map/all_to_all | solution.py:163
  31.3 0.0 collective-permute-done.1
  31.3 11.7 %all-gather = bf16[800,640]{1,0:T(8,128)(2,1)S(1)} all-gather(bf16[200,640]{1,0:T(8,128)(2,1)S(1)} %collective-permute-done.1), channel_id=2, replica_groups=mesh['h'=2,'x'=4,'c'=2,'y'=4,'z'=8] {'y'}, dimensions={0}, use_global_device_ids=true | all-gather | bytes 1280000 | tf_op jit(solution)/shard_map/all_gather | solution.py:165
  43.0 0.2 unpack_texts.1
  43.2 0.0 all-to-all-done.image_ref
  43.2 11.1 %collective-permute-start.2 = (bf16[4,200,640]{2,1,0:T(8,128)(2,1)S(1)}, bf16[4,200,640]{2,1,0:T(8,128)(2,1)S(1)}, u32[]{:S(2)}, u32[]{:S(2)}) collective-permute-start(bf16[4,200,640]{2,1,0:T(8,128)(2,1)S(1)} %all-to-all-done.image_ref), channel_id=1, source_target_pairs={{0,32},{32,0},{1,33},{33,1},{2,34},{34,2},{3,35},{35,3},{4,36},{36... | collective-permute-start | bytes 3072008 | tf_op jit(solution)/shard_map/ppermute | solution.py:164
  54.3 1.7 %own_weights.1 = (bf16[768,768]{1,0:T(8,128)(2,1)S(1)}, bf16[768,640]{1,0:T(8,128)(2,1)S(1)}) custom-call(f32[2]{0:T(128)S(1)} %pad_maximum_fusion.2.scale_ref, bf16[4,200,640]{2,1,0:T(8,128)(2,1)S(1)} %all-to-all-done.image_ref, bf16[768,640]{1,0:T(8,128)(2,1)S(1)} %get-tuple-element.15.texts, f32[8,768]{1,0:T(8,128)S(1)} %get-tuple-element.16.text_ids), custom_call_target="tpu_custom_call" | custom-call | flops 30198988800 | bytes 4194304 | tf_op jit(solution)/shard_map/own_weights/pallas_call | solution.py:66
  56.0 0.5 collective-permute-done.2.image_ref
  56.5 4.6 %other_grads.1 = (bf16[768,640]{1,0:T(8,128)(2,1)}, bf16[768,640]{1,0:T(8,128)(2,1)S(1)}) custom-call(f32[2]{0:T(128)S(1)} %pad_maximum_fusion.2.scale_ref, bf16[4,200,640]{2,1,0:T(8,128)(2,1)S(1)} %collective-permute-done.2.image_ref, bf16[768,640]{1,0:T(8,128)(2,1)S(1)} %get-tuple-element.15.texts, f32[8,768]{1,0:T(8,128)S(1)} %get-tuple-element.16.text_ids, ...), custom_call_target="tpu_custom_call" | custom-call | flops 3019898880 | bytes 4194304 | tf_op jit(solution)/shard_map/other_grads/pallas_call | solution.py:66
  61.1 0.0 copy-start
  61.1 1.0 copy-done
  62.0 2.3 %collective-permute-start.3 = (bf16[768,640]{1,0:T(8,128)(2,1)}, bf16[768,640]{1,0:T(8,128)(2,1)S(1)}, u32[]{:S(2)}, u32[]{:S(2)}) collective-permute-start(bf16[768,640]{1,0:T(8,128)(2,1)} %get-tuple-element.19), channel_id=1, source_target_pairs={{0,32},{32,0},{1,33},{33,1},{2,34},{34,2},{3,35},{35,3},{4,36},{36... | collective-permute-start | bytes 2949128 | tf_op jit(solution)/shard_map/ppermute | solution.py:177
  64.3 4.2 %all-to-all-start.1 = ((bf16[4,192,640]{2,1,0:T(8,128)(2,1)}), bf16[4,192,640]{2,1,0:T(8,128)(2,1)}, u32[]{:S(2)}, u32[]{:S(2)}) async-start(bf16[4,192,640]{2,1,0:T(8,128)(2,1)} %bitcast.5), calls=%async_computation.1 | async-start | bytes 1966080 | tf_op jit(solution)/shard_map/all_to_all | solution.py:178
  68.6 0.0 collective-permute-done.3.received
  68.6 2.1 %image_grads.1 = (bf16[192,640]{1,0:T(8,128)(2,1)}, bf16[192,640]{1,0:T(8,128)(2,1)}, bf16[192,640]{1,0:T(8,128)(2,1)}) custom-call(f32[2]{0:T(128)S(1)} %pad_maximum_fusion.2.scale_ref, s32[1]{0:T(128)} %bitcast.place_ref, bf16[768,768]{1,0:T(8,128)(2,1)S(1)} %get-tuple-element.17.own_weights.weights, bf16[768,640]{1,0:T(8,128)(2,1)S(1)} %get-tuple-element.15.texts, ...), custom_call_target="tpu_custom_call" | custom-call | bytes 4194304 | tf_op jit(solution)/shard_map/image_grads/pallas_call | solution.py:66
  70.7 12.8 %collective-permute-start.4 = (bf16[192,640]{1,0:T(8,128)(2,1)}, bf16[192,640]{1,0:T(8,128)(2,1)S(1)}, u32[]{:S(2)}, u32[]{:S(2)}) collective-permute-start(bf16[192,640]{1,0:T(8,128)(2,1)} %get-tuple-element.20), channel_id=1, source_target_pairs={{0,64},{64,128},{128,192},{192,0},{1,65},{65,129},{129,193},{193,1... | collective-permute-start | bytes 737288 | tf_op jit(solution)/shard_map/ppermute | solution.py:181
  83.6 1.9 %collective-permute-start.5 = (bf16[192,640]{1,0:T(8,128)(2,1)}, bf16[192,640]{1,0:T(8,128)(2,1)}, u32[]{:S(2)}, u32[]{:S(2)}) collective-permute-start(bf16[192,640]{1,0:T(8,128)(2,1)} %get-tuple-element.21), channel_id=1, source_target_pairs={{0,128},{64,192},{128,0},{192,64},{1,129},{65,193},{129,1},{193,65... | collective-permute-start | bytes 737288 | tf_op jit(solution)/shard_map/ppermute | solution.py:181
  85.5 4.3 %collective-permute-start.6 = (bf16[192,640]{1,0:T(8,128)(2,1)}, bf16[192,640]{1,0:T(8,128)(2,1)}, u32[]{:S(2)}, u32[]{:S(2)}) collective-permute-start(bf16[192,640]{1,0:T(8,128)(2,1)} %get-tuple-element.22), channel_id=1, source_target_pairs={{0,192},{64,0},{128,64},{192,128},{1,193},{65,1},{129,65},{193,129... | collective-permute-start | bytes 737288 | tf_op jit(solution)/shard_map/ppermute | solution.py:181
  89.8 0.0 all-to-all-done.1
  89.8 1.3 %text_sum.1 = bf16[192,640]{1,0:T(8,128)(2,1)S(1)} custom-call(bf16[768,640]{1,0:T(8,128)(2,1)} %bitcast.3.parts), custom_call_target="tpu_custom_call" | custom-call | bytes 4194304 | tf_op jit(solution)/shard_map/text_sum/pallas_call | solution.py:66
  91.1 9.3 %collective-permute-start.8 = (bf16[192,640]{1,0:T(8,128)(2,1)S(1)}, bf16[192,640]{1,0:T(8,128)(2,1)S(1)}, u32[]{:S(2)}, u32[]{:S(2)}) collective-permute-start(bf16[192,640]{1,0:T(8,128)(2,1)S(1)} %text_sum.1), channel_id=1, source_target_pairs={{3,0},{67,1},{131,2},{195,3},{35,4},{99,5},{163,6},{227,7},{0,32},... | collective-permute-start | bytes 737288 | tf_op jit(solution)/shard_map/ppermute | solution.py:185
  100.5 0.0 collective-permute-done.4.rest_0_
  100.5 0.0 collective-permute-done.5.rest_1_
  100.5 0.0 collective-permute-done.6.rest_2_
  100.5 1.5 %image_sum.1 = bf16[192,640]{1,0:T(8,128)(2,1)S(1)} custom-call(f32[2]{0:T(128)S(1)} %pad_maximum_fusion.2.scale_ref, s32[1]{0:T(128)} %bitcast.place_ref, bf16[768,768]{1,0:T(8,128)(2,1)S(1)} %get-tuple-element.17.own_weights.weights, bf16[768,640]{1,0:T(8,128)(2,1)S(1)} %get-tuple-element.15.texts, bf16[768,640]{1,0:T(8,128)(2,1)S(1)} %collective-permute-done.3.received, ...), custom_call_target="tpu_custom_call" | custom-call | bytes 4194304 | tf_op jit(solution)/shard_map/image_sum/pallas_call | solution.py:66
  102.0 1.9 %collective-permute-start.7 = (bf16[192,640]{1,0:T(8,128)(2,1)S(1)}, bf16[192,640]{1,0:T(8,128)(2,1)S(1)}, u32[]{:S(2)}, u32[]{:S(2)}) collective-permute-start(bf16[192,640]{1,0:T(8,128)(2,1)S(1)} %image_sum.1), channel_id=1, source_target_pairs={{7,0},{71,1},{135,2},{199,3},{39,4},{103,5},{167,6},{231,7},{3,32}... | collective-permute-start | bytes 737288 | tf_op jit(solution)/shard_map/ppermute | solution.py:183
  104.0 5.3 %collective-permute-done.8 = bf16[192,640]{1,0:T(8,128)(2,1)S(1)} collective-permute-done((bf16[192,640]{1,0:T(8,128)(2,1)S(1)}, bf16[192,640]{1,0:T(8,128)(2,1)S(1)}, u32[]{:S(2)}, u32[]{:S(2)}) %collective-permute-start.8) | collective-permute-done | bytes 245792 | tf_op jit(solution)/shard_map/ppermute | solution.py:185
  109.3 0.8 convert_element_type.14
  110.1 14.6 %collective-permute-done.7 = bf16[192,640]{1,0:T(8,128)(2,1)S(1)} collective-permute-done((bf16[192,640]{1,0:T(8,128)(2,1)S(1)}, bf16[192,640]{1,0:T(8,128)(2,1)S(1)}, u32[]{:S(2)}, u32[]{:S(2)}) %collective-permute-start.7) | collective-permute-done | bytes 245792 | tf_op jit(solution)/shard_map/ppermute | solution.py:183
  124.8 0.7 copy.11
  (4 shorter events, 0.0 us)
Async XLA Ops:
  3.1 12.0 %collective-permute-start = (bf16[200,640]{1,0:T(8,128)(2,1)S(1)}, bf16[200,640]{1,0:T(8,128)(2,1)S(1)}, u32[]{:S(2)}, u32[]{:S(2)}) collective-permute-start(bf16[200,640]{1,0:T(8,128)(2,1)S(1)} %get-tuple-element.13), channel_id=1, source_target_pairs={{0,7},{1,71},{2,135},{3,199},{4,39},{5,103},{6,167},{7,231},{32,3}... | collective-permute-start | bytes 768008 | tf_op jit(solution)/shard_map/ppermute | solution.py:161
  5.7 25.6 %collective-permute-start.1 = (bf16[200,640]{1,0:T(8,128)(2,1)S(1)}, bf16[200,640]{1,0:T(8,128)(2,1)S(1)}, u32[]{:S(2)}, u32[]{:S(2)}) collective-permute-start(bf16[200,640]{1,0:T(8,128)(2,1)S(1)} %get-tuple-element.14), channel_id=1, source_target_pairs={{0,3},{1,67},{2,131},{3,195},{4,35},{5,99},{6,163},{7,227},{32,0},... | collective-permute-start | bytes 768008 | tf_op jit(solution)/shard_map/ppermute | solution.py:162
  16.2 27.0 %all-to-all-start = ((bf16[4,200,640]{2,1,0:T(8,128)(2,1)}), bf16[4,200,640]{2,1,0:T(8,128)(2,1)S(1)}, u32[]{:S(2)}, u32[]{:S(2)}) async-start(bf16[4,200,640]{2,1,0:T(8,128)(2,1)} %broadcast_in_dim.2), calls=%async_computation | async-start | bytes 2048000 | tf_op jit(solution)/shard_map/all_to_all | solution.py:163
  43.2 13.3 %collective-permute-start.2 = (bf16[4,200,640]{2,1,0:T(8,128)(2,1)S(1)}, bf16[4,200,640]{2,1,0:T(8,128)(2,1)S(1)}, u32[]{:S(2)}, u32[]{:S(2)}) collective-permute-start(bf16[4,200,640]{2,1,0:T(8,128)(2,1)S(1)} %all-to-all-done.image_ref), channel_id=1, source_target_pairs={{0,32},{32,0},{1,33},{33,1},{2,34},{34,2},{3,35},{35,3},{4,36},{36... | collective-permute-start | bytes 3072008 | tf_op jit(solution)/shard_map/ppermute | solution.py:164
  61.1 1.0 copy-start
  62.0 6.5 %collective-permute-start.3 = (bf16[768,640]{1,0:T(8,128)(2,1)}, bf16[768,640]{1,0:T(8,128)(2,1)S(1)}, u32[]{:S(2)}, u32[]{:S(2)}) collective-permute-start(bf16[768,640]{1,0:T(8,128)(2,1)} %get-tuple-element.19), channel_id=1, source_target_pairs={{0,32},{32,0},{1,33},{33,1},{2,34},{34,2},{3,35},{35,3},{4,36},{36... | collective-permute-start | bytes 2949128 | tf_op jit(solution)/shard_map/ppermute | solution.py:177
  64.3 25.5 %all-to-all-start.1 = ((bf16[4,192,640]{2,1,0:T(8,128)(2,1)}), bf16[4,192,640]{2,1,0:T(8,128)(2,1)}, u32[]{:S(2)}, u32[]{:S(2)}) async-start(bf16[4,192,640]{2,1,0:T(8,128)(2,1)} %bitcast.5), calls=%async_computation.1 | async-start | bytes 1966080 | tf_op jit(solution)/shard_map/all_to_all | solution.py:178
  70.7 29.8 %collective-permute-start.4 = (bf16[192,640]{1,0:T(8,128)(2,1)}, bf16[192,640]{1,0:T(8,128)(2,1)S(1)}, u32[]{:S(2)}, u32[]{:S(2)}) collective-permute-start(bf16[192,640]{1,0:T(8,128)(2,1)} %get-tuple-element.20), channel_id=1, source_target_pairs={{0,64},{64,128},{128,192},{192,0},{1,65},{65,129},{129,193},{193,1... | collective-permute-start | bytes 737288 | tf_op jit(solution)/shard_map/ppermute | solution.py:181
  83.6 16.9 %collective-permute-start.5 = (bf16[192,640]{1,0:T(8,128)(2,1)}, bf16[192,640]{1,0:T(8,128)(2,1)}, u32[]{:S(2)}, u32[]{:S(2)}) collective-permute-start(bf16[192,640]{1,0:T(8,128)(2,1)} %get-tuple-element.21), channel_id=1, source_target_pairs={{0,128},{64,192},{128,0},{192,64},{1,129},{65,193},{129,1},{193,65... | collective-permute-start | bytes 737288 | tf_op jit(solution)/shard_map/ppermute | solution.py:181
  85.5 15.0 %collective-permute-start.6 = (bf16[192,640]{1,0:T(8,128)(2,1)}, bf16[192,640]{1,0:T(8,128)(2,1)}, u32[]{:S(2)}, u32[]{:S(2)}) collective-permute-start(bf16[192,640]{1,0:T(8,128)(2,1)} %get-tuple-element.22), channel_id=1, source_target_pairs={{0,192},{64,0},{128,64},{192,128},{1,193},{65,1},{129,65},{193,129... | collective-permute-start | bytes 737288 | tf_op jit(solution)/shard_map/ppermute | solution.py:181
  91.1 18.2 %collective-permute-start.8 = (bf16[192,640]{1,0:T(8,128)(2,1)S(1)}, bf16[192,640]{1,0:T(8,128)(2,1)S(1)}, u32[]{:S(2)}, u32[]{:S(2)}) collective-permute-start(bf16[192,640]{1,0:T(8,128)(2,1)S(1)} %text_sum.1), channel_id=1, source_target_pairs={{3,0},{67,1},{131,2},{195,3},{35,4},{99,5},{163,6},{227,7},{0,32},... | collective-permute-start | bytes 737288 | tf_op jit(solution)/shard_map/ppermute | solution.py:185
  102.0 22.7 %collective-permute-start.7 = (bf16[192,640]{1,0:T(8,128)(2,1)S(1)}, bf16[192,640]{1,0:T(8,128)(2,1)S(1)}, u32[]{:S(2)}, u32[]{:S(2)}) collective-permute-start(bf16[192,640]{1,0:T(8,128)(2,1)S(1)} %image_sum.1), channel_id=1, source_target_pairs={{7,0},{71,1},{135,2},{199,3},{39,4},{103,5},{167,6},{231,7},{3,32}... | collective-permute-start | bytes 737288 | tf_op jit(solution)/shard_map/ppermute | solution.py:183

commit v5 on v4

--- a/solution.py
+++ b/solution.py
@@ -96,7 +96,7 @@
     text_ids[...] = jnp.broadcast_to(id_row(text_ref), text_ids.shape)
 
 
-def own_kernel(scale_ref, image_ref, texts, text_ids, weights, images):
+def own_kernel(scale_ref, image_ref, texts, text_ids, weights, images, text_sum):
     unpack_rows(image_ref, images)
     text_row = text_ids[0:1, :]
     ids = id_row(image_ref)
@@ -104,9 +104,13 @@
         rows = pl.ds(j * CHUNK, CHUNK)
         columns = jnp.concatenate([id_tile(ids, 2 * j), id_tile(ids, 2 * j + 1)], axis=0)
         weights[rows, :] = pair_weights(scale_ref, images[rows, :], texts[...], columns, text_row)
-
-
-def other_kernel(scale_ref, image_ref, texts, text_ids, own_weights, own_images, image_grads, text_grads, images, weights):
+    fold = (((0,), (0,)), ((), ()))
+    for j in range(GROUP // CHUNK):
+        rows = pl.ds(j * CHUNK, CHUNK)
+        text_sum[rows, :] = lax.dot_general(weights[:, rows], images[...], fold, preferred_element_type=jnp.float32)
+
+
+def other_kernel(scale_ref, image_ref, texts, text_ids, text_sum, image_grads, text_grads, images, weights):
     unpack_rows(image_ref, images)
     factor = scale_ref[0] * 0.125
     text_row = text_ids[0:1, :]
@@ -121,8 +125,7 @@
     fold = (((0,), (0,)), ((), ()))
     for j in range(GROUP // CHUNK):
         rows = pl.ds(j * CHUNK, CHUNK)
-        grad = lax.dot_general(own_weights[:, rows], own_images[...], fold, preferred_element_type=jnp.float32)
-        grad = grad + lax.dot_general(weights[:, rows], images[...], fold, preferred_element_type=jnp.float32)
+        grad = text_sum[rows, :] + lax.dot_general(weights[:, rows], images[...], fold, preferred_element_type=jnp.float32)
         text_grads[rows, :] = (factor * grad).astype(text_grads.dtype)
 
 
@@ -157,7 +160,6 @@
     place = lax.axis_index("x").astype(jnp.int32).reshape(1)
     packed_images = pack(picture_vectors, picture_match_label)
     packed_texts = pack(caption_vectors, caption_match_label)
-    packed_images, packed_texts = lax.optimization_barrier((packed_images, packed_texts))
     images = lax.ppermute(packed_images, MOVE_AXES, IMAGE_ROUTE)
     texts = lax.ppermute(packed_texts, MOVE_AXES, TEXT_ROUTE)
     own = lax.all_to_all(jnp.broadcast_to(images[None], (4, PACKED, D)), "x", split_axis=0, concat_axis=0, tiled=True)
@@ -167,11 +169,11 @@
     rows = (GROUP, D)
     bf16, f32 = jnp.bfloat16, jnp.float32
     all_texts, text_ids = call(unpack_kernel, "unpack_texts", ((rows, bf16), ((8, GROUP), f32)), [VMEM], 40 * flops, text)
-    own_weights, own_images = call(
-        own_kernel, "own_weights", ((half, bf16), (rows, bf16)), [SMEM, VMEM, VMEM, VMEM], 40 * flops, scale, own, all_texts, text_ids
+    own_weights, _, own_text = call(
+        own_kernel, "own_weights", ((half, bf16), (rows, bf16), (rows, f32)), [SMEM, VMEM, VMEM, VMEM], 40 * flops, scale, own, all_texts, text_ids
     )
     other_grad, text_part = call(
-        other_kernel, "other_grads", ((rows, bf16), (rows, bf16)), [SMEM] + [VMEM] * 5, 4 * flops, scale, other, all_texts, text_ids, own_weights, own_images,
+        other_kernel, "other_grads", ((rows, bf16), (rows, bf16)), [SMEM] + [VMEM] * 4, 4 * flops, scale, other, all_texts, text_ids, own_text,
         scratch=[pltpu.VMEM(rows, bf16), pltpu.VMEM(half, bf16)],
     )
     received = lax.ppermute(other_grad, "c", [(0, 1), (1, 0)])

time: 126 us -> 124 us (0.984)
  the two profiles are of different devices: /device:TPU:225 before, /device:TPU:193 now
where the time goes in v5:
time: 124 us; the launch traced here: 123 us
  starting transfers between devices  68.2 us (55%)
  waiting for transfers between devices  22.6 us (18%)
  blocking collectives  12.1 us (10%)
  Pallas kernels  11.4 us (9%)
  other arithmetic  4.19 us (3%)
  local copies, waits for them, and re-layouts  2.77 us (2%)
  between operations  2.09 us (2%)
    all_to_all x1, starting transfers between devices, body(): lax.all_to_all(jnp.broadcast_to(images[None], (4, PACKED, D)), 'x', split...  24.7 us
    all_gather x1, blocking collectives, body(): text = lax.all_gather(texts, 'y', axis=0)  12.1 us
    pallas_call x6, Pallas kernels, call(): pl.pallas_call(kernel, out_shape=tuple((jax.ShapeDtypeStruct(shape, kind)...  11.4 us
    ppermute x1, waiting for transfers between devices, body(): text_home = lax.ppermute(text_sum, MOVE_AXES, back(TEXT_ROUTE))  11.4 us
    ppermute x3, starting transfers between devices, body(): lax.ppermute(part, 'x', [(i, (i + k) % 4) for i in range(4)])  11.1 us
    ppermute x1, starting transfers between devices, body(): texts = lax.ppermute(packed_texts, MOVE_AXES, TEXT_ROUTE)  10.7 us
    ppermute x1, waiting for transfers between devices, body(): image_home = lax.ppermute(kept, MOVE_AXES, back(IMAGE_ROUTE))  9.82 us
    ppermute x1, starting transfers between devices, body(): text_home = lax.ppermute(text_sum, MOVE_AXES, back(TEXT_ROUTE))  5.89 us
  transfers between devices with their start and end apart: 11, of which 3 were waited for; matrix products, arithmetic and copies ran while one was open for 3% of the time, Pallas kernels for 6%

profile of v5, /device:TPU:193, one launch (start us, length us, event | category | flops | bytes accessed | tf_op | source)
XLA Modules:
  0.0 123.3 jit_solution(15783443033733307482)
XLA Ops:
  0.6 0.7 convert_element_type.12
  1.3 1.0 pad_maximum_fusion
  2.3 3.3 %collective-permute-start = (bf16[200,640]{1,0:T(8,128)(2,1)S(1)}, bf16[200,640]{1,0:T(8,128)(2,1)S(1)}, u32[]{:S(2)}, u32[]{:S(2)}) collective-permute-start(bf16[200,640]{1,0:T(8,128)(2,1)S(1)} %pad_maximum_fusion), channel_id=1, source_target_pairs={{0,7},{1,71},{2,135},{3,199},{4,39},{5,103},{6,167},{7,231},{32,3}... | collective-permute-start | bytes 768008 | tf_op jit(solution)/shard_map/ppermute | solution.py:163
  5.6 0.7 convert_element_type.13
  6.3 1.0 pad_maximum_fusion.1
  7.3 10.7 %collective-permute-start.1 = (bf16[200,640]{1,0:T(8,128)(2,1)S(1)}, bf16[200,640]{1,0:T(8,128)(2,1)S(1)}, u32[]{:S(2)}, u32[]{:S(2)}) collective-permute-start(bf16[200,640]{1,0:T(8,128)(2,1)S(1)} %pad_maximum_fusion.1), channel_id=1, source_target_pairs={{0,3},{1,67},{2,131},{3,195},{4,35},{5,99},{6,163},{7,227},{32,0},... | collective-permute-start | bytes 768008 | tf_op jit(solution)/shard_map/ppermute | solution.py:164
  19.3 0.1 pad_maximum_fusion.2.scale_ref
  19.4 0.0 collective-permute-done
  19.4 1.1 broadcast_in_dim.2
  20.4 24.7 %all-to-all-start = ((bf16[4,200,640]{2,1,0:T(8,128)(2,1)}), bf16[4,200,640]{2,1,0:T(8,128)(2,1)S(1)}, u32[]{:S(2)}, u32[]{:S(2)}) async-start(bf16[4,200,640]{2,1,0:T(8,128)(2,1)} %broadcast_in_dim.2), calls=%async_computation | async-start | bytes 2048000 | tf_op jit(solution)/shard_map/all_to_all | solution.py:165
  45.1 0.0 collective-permute-done.1
  45.1 12.1 %all-gather = bf16[800,640]{1,0:T(8,128)(2,1)S(1)} all-gather(bf16[200,640]{1,0:T(8,128)(2,1)S(1)} %collective-permute-done.1), channel_id=2, replica_groups=mesh['h'=2,'x'=4,'c'=2,'y'=4,'z'=8] {'y'}, dimensions={0}, use_global_device_ids=true | all-gather | bytes 1280000 | tf_op jit(solution)/shard_map/all_gather | solution.py:167
  57.2 0.2 unpack_texts.1
  57.3 0.0 all-to-all-done.image_ref
  57.4 1.9 %collective-permute-start.2 = (bf16[4,200,640]{2,1,0:T(8,128)(2,1)S(1)}, bf16[4,200,640]{2,1,0:T(8,128)(2,1)S(1)}, u32[]{:S(2)}, u32[]{:S(2)}) collective-permute-start(bf16[4,200,640]{2,1,0:T(8,128)(2,1)S(1)} %all-to-all-done.image_ref), channel_id=1, source_target_pairs={{0,32},{32,0},{1,33},{33,1},{2,34},{34,2},{3,35},{35,3},{4,36},{36... | collective-permute-start | bytes 3072008 | tf_op jit(solution)/shard_map/ppermute | solution.py:166
  59.3 2.7 %own_weights.1 = (bf16[768,768]{1,0:T(8,128)(2,1)S(1)}, bf16[768,640]{1,0:T(8,128)(2,1)}, f32[768,640]{1,0:T(8,128)S(1)}) custom-call(f32[2]{0:T(128)S(1)} %pad_maximum_fusion.2.scale_ref, bf16[4,200,640]{2,1,0:T(8,128)(2,1)S(1)} %all-to-all-done.image_ref, bf16[768,640]{1,0:T(8,128)(2,1)S(1)} %get-tuple-element.11.texts, ...), custom_call_target="tpu_custom_call" | custom-call | flops 30198988800 | bytes 4194304 | tf_op jit(solution)/shard_map/own_weights/pallas_call | solution.py:66
  62.0 0.0 collective-permute-done.2.image_ref
  62.0 3.6 %other_grads.1 = (bf16[768,640]{1,0:T(8,128)(2,1)}, bf16[768,640]{1,0:T(8,128)(2,1)S(1)}) custom-call(f32[2]{0:T(128)S(1)} %pad_maximum_fusion.2.scale_ref, bf16[4,200,640]{2,1,0:T(8,128)(2,1)S(1)} %collective-permute-done.2.image_ref, bf16[768,640]{1,0:T(8,128)(2,1)S(1)} %get-tuple-element.11.texts, f32[8,768]{1,0:T(8,128)S(1)} %get-tuple-element.12.text_ids, ...), custom_call_target="tpu_custom_call" | custom-call | flops 3019898880 | bytes 4194304 | tf_op jit(solution)/shard_map/other_grads/pallas_call | solution.py:66
  65.6 0.0 copy-start
  65.6 1.0 copy-done
  66.6 2.4 %collective-permute-start.3 = (bf16[768,640]{1,0:T(8,128)(2,1)}, bf16[768,640]{1,0:T(8,128)(2,1)S(1)}, u32[]{:S(2)}, u32[]{:S(2)}) collective-permute-start(bf16[768,640]{1,0:T(8,128)(2,1)} %get-tuple-element.15), channel_id=1, source_target_pairs={{0,32},{32,0},{1,33},{33,1},{2,34},{34,2},{3,35},{35,3},{4,36},{36... | collective-permute-start | bytes 2949128 | tf_op jit(solution)/shard_map/ppermute | solution.py:179
  69.0 4.2 %all-to-all-start.1 = ((bf16[4,192,640]{2,1,0:T(8,128)(2,1)}), bf16[4,192,640]{2,1,0:T(8,128)(2,1)}, u32[]{:S(2)}, u32[]{:S(2)}) async-start(bf16[4,192,640]{2,1,0:T(8,128)(2,1)} %bitcast.5), calls=%async_computation.1 | async-start | bytes 1966080 | tf_op jit(solution)/shard_map/all_to_all | solution.py:180
  73.3 0.0 collective-permute-done.3.received
  73.3 2.1 %image_grads.1 = (bf16[192,640]{1,0:T(8,128)(2,1)}, bf16[192,640]{1,0:T(8,128)(2,1)}, bf16[192,640]{1,0:T(8,128)(2,1)}) custom-call(f32[2]{0:T(128)S(1)} %pad_maximum_fusion.2.scale_ref, s32[1]{0:T(128)} %bitcast.place_ref, bf16[768,768]{1,0:T(8,128)(2,1)S(1)} %get-tuple-element.13.weights, bf16[768,640]{1,0:T(8,128)(2,1)S(1)} %get-tuple-element.11.texts, ...), custom_call_target="tpu_custom_call" | custom-call | bytes 4194304 | tf_op jit(solution)/shard_map/image_grads/pallas_call | solution.py:66
  75.4 3.8 %collective-permute-start.4 = (bf16[192,640]{1,0:T(8,128)(2,1)}, bf16[192,640]{1,0:T(8,128)(2,1)S(1)}, u32[]{:S(2)}, u32[]{:S(2)}) collective-permute-start(bf16[192,640]{1,0:T(8,128)(2,1)} %get-tuple-element.16), channel_id=1, source_target_pairs={{0,64},{64,128},{128,192},{192,0},{1,65},{65,129},{129,193},{193,1... | collective-permute-start | bytes 737288 | tf_op jit(solution)/shard_map/ppermute | solution.py:183
  79.2 4.2 %collective-permute-start.5 = (bf16[192,640]{1,0:T(8,128)(2,1)}, bf16[192,640]{1,0:T(8,128)(2,1)}, u32[]{:S(2)}, u32[]{:S(2)}) collective-permute-start(bf16[192,640]{1,0:T(8,128)(2,1)} %get-tuple-element.17), channel_id=1, source_target_pairs={{0,128},{64,192},{128,0},{192,64},{1,129},{65,193},{129,1},{193,65... | collective-permute-start | bytes 737288 | tf_op jit(solution)/shard_map/ppermute | solution.py:183
  83.4 3.1 %collective-permute-start.6 = (bf16[192,640]{1,0:T(8,128)(2,1)}, bf16[192,640]{1,0:T(8,128)(2,1)}, u32[]{:S(2)}, u32[]{:S(2)}) collective-permute-start(bf16[192,640]{1,0:T(8,128)(2,1)} %get-tuple-element.18), channel_id=1, source_target_pairs={{0,192},{64,0},{128,64},{192,128},{1,193},{65,1},{129,65},{193,129... | collective-permute-start | bytes 737288 | tf_op jit(solution)/shard_map/ppermute | solution.py:183
  86.5 1.4 %all-to-all-done.1 = bf16[4,192,640]{2,1,0:T(8,128)(2,1)} async-done(((bf16[4,192,640]{2,1,0:T(8,128)(2,1)}), bf16[4,192,640]{2,1,0:T(8,128)(2,1)}, u32[]{:S(2)}, u32[]{:S(2)}) %all-to-all-start.1) | async-done | bytes 983072 | tf_op jit(solution)/shard_map/all_to_all | solution.py:180
  87.9 1.3 %text_sum.1 = bf16[192,640]{1,0:T(8,128)(2,1)S(1)} custom-call(bf16[768,640]{1,0:T(8,128)(2,1)} %bitcast.3.parts), custom_call_target="tpu_custom_call" | custom-call | bytes 4194304 | tf_op jit(solution)/shard_map/text_sum/pallas_call | solution.py:66
  89.2 5.9 %collective-permute-start.8 = (bf16[192,640]{1,0:T(8,128)(2,1)S(1)}, bf16[192,640]{1,0:T(8,128)(2,1)S(1)}, u32[]{:S(2)}, u32[]{:S(2)}) collective-permute-start(bf16[192,640]{1,0:T(8,128)(2,1)S(1)} %text_sum.1), channel_id=1, source_target_pairs={{3,0},{67,1},{131,2},{195,3},{35,4},{99,5},{163,6},{227,7},{0,32},... | collective-permute-start | bytes 737288 | tf_op jit(solution)/shard_map/ppermute | solution.py:187
  95.1 0.0 collective-permute-done.4.rest_0_
  95.1 0.0 collective-permute-done.5.rest_1_
  95.1 0.0 collective-permute-done.6.rest_2_
  95.1 1.5 %image_sum.1 = bf16[192,640]{1,0:T(8,128)(2,1)S(1)} custom-call(f32[2]{0:T(128)S(1)} %pad_maximum_fusion.2.scale_ref, s32[1]{0:T(128)} %bitcast.place_ref, bf16[768,768]{1,0:T(8,128)(2,1)S(1)} %get-tuple-element.13.weights, bf16[768,640]{1,0:T(8,128)(2,1)S(1)} %get-tuple-element.11.texts, bf16[768,640]{1,0:T(8,128)(2,1)S(1)} %collective-permute-done.3.received, ...), custom_call_target="tpu_custom_call" | custom-call | bytes 4194304 | tf_op jit(solution)/shard_map/image_sum/pallas_call | solution.py:66
  96.7 3.9 %collective-permute-start.7 = (bf16[192,640]{1,0:T(8,128)(2,1)S(1)}, bf16[192,640]{1,0:T(8,128)(2,1)S(1)}, u32[]{:S(2)}, u32[]{:S(2)}) collective-permute-start(bf16[192,640]{1,0:T(8,128)(2,1)S(1)} %image_sum.1), channel_id=1, source_target_pairs={{7,0},{71,1},{135,2},{199,3},{39,4},{103,5},{167,6},{231,7},{3,32}... | collective-permute-start | bytes 737288 | tf_op jit(solution)/shard_map/ppermute | solution.py:185
  100.6 11.4 %collective-permute-done.8 = bf16[192,640]{1,0:T(8,128)(2,1)S(1)} collective-permute-done((bf16[192,640]{1,0:T(8,128)(2,1)S(1)}, bf16[192,640]{1,0:T(8,128)(2,1)S(1)}, u32[]{:S(2)}, u32[]{:S(2)}) %collective-permute-start.8) | collective-permute-done | bytes 245792 | tf_op jit(solution)/shard_map/ppermute | solution.py:187
  112.0 0.8 convert_element_type.14
  112.8 9.8 %collective-permute-done.7 = bf16[192,640]{1,0:T(8,128)(2,1)S(1)} collective-permute-done((bf16[192,640]{1,0:T(8,128)(2,1)S(1)}, bf16[192,640]{1,0:T(8,128)(2,1)S(1)}, u32[]{:S(2)}, u32[]{:S(2)}) %collective-permute-start.7) | collective-permute-done | bytes 245792 | tf_op jit(solution)/shard_map/ppermute | solution.py:185
  122.6 0.7 copy.11
  (4 shorter events, 0.0 us)
Async XLA Ops:
  2.3 17.1 %collective-permute-start = (bf16[200,640]{1,0:T(8,128)(2,1)S(1)}, bf16[200,640]{1,0:T(8,128)(2,1)S(1)}, u32[]{:S(2)}, u32[]{:S(2)}) collective-permute-start(bf16[200,640]{1,0:T(8,128)(2,1)S(1)} %pad_maximum_fusion), channel_id=1, source_target_pairs={{0,7},{1,71},{2,135},{3,199},{4,39},{5,103},{6,167},{7,231},{32,3}... | collective-permute-start | bytes 768008 | tf_op jit(solution)/shard_map/ppermute | solution.py:163
  7.3 37.9 %collective-permute-start.1 = (bf16[200,640]{1,0:T(8,128)(2,1)S(1)}, bf16[200,640]{1,0:T(8,128)(2,1)S(1)}, u32[]{:S(2)}, u32[]{:S(2)}) collective-permute-start(bf16[200,640]{1,0:T(8,128)(2,1)S(1)} %pad_maximum_fusion.1), channel_id=1, source_target_pairs={{0,3},{1,67},{2,131},{3,195},{4,35},{5,99},{6,163},{7,227},{32,0},... | collective-permute-start | bytes 768008 | tf_op jit(solution)/shard_map/ppermute | solution.py:164
  20.4 36.9 %all-to-all-start = ((bf16[4,200,640]{2,1,0:T(8,128)(2,1)}), bf16[4,200,640]{2,1,0:T(8,128)(2,1)S(1)}, u32[]{:S(2)}, u32[]{:S(2)}) async-start(bf16[4,200,640]{2,1,0:T(8,128)(2,1)} %broadcast_in_dim.2), calls=%async_computation | async-start | bytes 2048000 | tf_op jit(solution)/shard_map/all_to_all | solution.py:165
  57.4 4.7 %collective-permute-start.2 = (bf16[4,200,640]{2,1,0:T(8,128)(2,1)S(1)}, bf16[4,200,640]{2,1,0:T(8,128)(2,1)S(1)}, u32[]{:S(2)}, u32[]{:S(2)}) collective-permute-start(bf16[4,200,640]{2,1,0:T(8,128)(2,1)S(1)} %all-to-all-done.image_ref), channel_id=1, source_target_pairs={{0,32},{32,0},{1,33},{33,1},{2,34},{34,2},{3,35},{35,3},{4,36},{36... | collective-permute-start | bytes 3072008 | tf_op jit(solution)/shard_map/ppermute | solution.py:166
  65.6 1.0 copy-start
  66.6 6.7 %collective-permute-start.3 = (bf16[768,640]{1,0:T(8,128)(2,1)}, bf16[768,640]{1,0:T(8,128)(2,1)S(1)}, u32[]{:S(2)}, u32[]{:S(2)}) collective-permute-start(bf16[768,640]{1,0:T(8,128)(2,1)} %get-tuple-element.15), channel_id=1, source_target_pairs={{0,32},{32,0},{1,33},{33,1},{2,34},{34,2},{3,35},{35,3},{4,36},{36... | collective-permute-start | bytes 2949128 | tf_op jit(solution)/shard_map/ppermute | solution.py:179
  69.0 18.9 %all-to-all-start.1 = ((bf16[4,192,640]{2,1,0:T(8,128)(2,1)}), bf16[4,192,640]{2,1,0:T(8,128)(2,1)}, u32[]{:S(2)}, u32[]{:S(2)}) async-start(bf16[4,192,640]{2,1,0:T(8,128)(2,1)} %bitcast.5), calls=%async_computation.1 | async-start | bytes 1966080 | tf_op jit(solution)/shard_map/all_to_all | solution.py:180
  75.4 19.7 %collective-permute-start.4 = (bf16[192,640]{1,0:T(8,128)(2,1)}, bf16[192,640]{1,0:T(8,128)(2,1)S(1)}, u32[]{:S(2)}, u32[]{:S(2)}) collective-permute-start(bf16[192,640]{1,0:T(8,128)(2,1)} %get-tuple-element.16), channel_id=1, source_target_pairs={{0,64},{64,128},{128,192},{192,0},{1,65},{65,129},{129,193},{193,1... | collective-permute-start | bytes 737288 | tf_op jit(solution)/shard_map/ppermute | solution.py:183
  79.2 15.9 %collective-permute-start.5 = (bf16[192,640]{1,0:T(8,128)(2,1)}, bf16[192,640]{1,0:T(8,128)(2,1)}, u32[]{:S(2)}, u32[]{:S(2)}) collective-permute-start(bf16[192,640]{1,0:T(8,128)(2,1)} %get-tuple-element.17), channel_id=1, source_target_pairs={{0,128},{64,192},{128,0},{192,64},{1,129},{65,193},{129,1},{193,65... | collective-permute-start | bytes 737288 | tf_op jit(solution)/shard_map/ppermute | solution.py:183
  83.4 11.7 %collective-permute-start.6 = (bf16[192,640]{1,0:T(8,128)(2,1)}, bf16[192,640]{1,0:T(8,128)(2,1)}, u32[]{:S(2)}, u32[]{:S(2)}) collective-permute-start(bf16[192,640]{1,0:T(8,128)(2,1)} %get-tuple-element.18), channel_id=1, source_target_pairs={{0,192},{64,0},{128,64},{192,128},{1,193},{65,1},{129,65},{193,129... | collective-permute-start | bytes 737288 | tf_op jit(solution)/shard_map/ppermute | solution.py:183
  89.2 22.8 %collective-permute-start.8 = (bf16[192,640]{1,0:T(8,128)(2,1)S(1)}, bf16[192,640]{1,0:T(8,128)(2,1)S(1)}, u32[]{:S(2)}, u32[]{:S(2)}) collective-permute-start(bf16[192,640]{1,0:T(8,128)(2,1)S(1)} %text_sum.1), channel_id=1, source_target_pairs={{3,0},{67,1},{131,2},{195,3},{35,4},{99,5},{163,6},{227,7},{0,32},... | collective-permute-start | bytes 737288 | tf_op jit(solution)/shard_map/ppermute | solution.py:187
  96.7 25.9 %collective-permute-start.7 = (bf16[192,640]{1,0:T(8,128)(2,1)S(1)}, bf16[192,640]{1,0:T(8,128)(2,1)S(1)}, u32[]{:S(2)}, u32[]{:S(2)}) collective-permute-start(bf16[192,640]{1,0:T(8,128)(2,1)S(1)} %image_sum.1), channel_id=1, source_target_pairs={{7,0},{71,1},{135,2},{199,3},{39,4},{103,5},{167,6},{231,7},{3,32}... | collective-permute-start | bytes 737288 | tf_op jit(solution)/shard_map/ppermute | solution.py:185

commit v6 on v5

--- a/solution.py
+++ b/solution.py
@@ -51,7 +51,7 @@
 def id_row(ref):
     total = None
     for k in range(4):
-        part = ref[k, ROWS:, :].astype(jnp.float32)
+        part = ref[k][ROWS:, :].astype(jnp.float32)
         part = jnp.concatenate([part, jnp.zeros((EXTRA, GROUP - D), jnp.float32)], axis=1)
         part = part if k == 0 else pltpu.roll(part, k * ROWS, 1)
         total = part if total is None else total + part

time: 124 us -> 124 us (level)
  no operation moved by 1% of the time
where the time goes in v6:
time: 124 us; the launch traced here: 123 us
  starting transfers between devices  68.2 us (55%)
  waiting for transfers between devices  22.6 us (18%)
  blocking collectives  12.1 us (10%)
  Pallas kernels  11.4 us (9%)
  other arithmetic  4.19 us (3%)
  local copies, waits for them, and re-layouts  2.77 us (2%)
  between operations  2.09 us (2%)
    all_to_all x1, starting transfers between devices, body(): lax.all_to_all(jnp.broadcast_to(images[None], (4, PACKED, D)), 'x', split...  24.7 us
    all_gather x1, blocking collectives, body(): text = lax.all_gather(texts, 'y', axis=0)  12.1 us
    pallas_call x6, Pallas kernels, call(): pl.pallas_call(kernel, out_shape=tuple((jax.ShapeDtypeStruct(shape, kind)...  11.4 us
    ppermute x1, waiting for transfers between devices, body(): text_home = lax.ppermute(text_sum, MOVE_AXES, back(TEXT_ROUTE))  11.4 us
    ppermute x3, starting transfers between devices, body(): lax.ppermute(part, 'x', [(i, (i + k) % 4) for i in range(4)])  11.1 us
    ppermute x1, starting transfers between devices, body(): texts = lax.ppermute(packed_texts, MOVE_AXES, TEXT_ROUTE)  10.7 us
    ppermute x1, waiting for transfers between devices, body(): image_home = lax.ppermute(kept, MOVE_AXES, back(IMAGE_ROUTE))  9.82 us
    ppermute x1, starting transfers between devices, body(): text_home = lax.ppermute(text_sum, MOVE_AXES, back(TEXT_ROUTE))  5.89 us
  transfers between devices with their start and end apart: 11, of which 3 were waited for; matrix products, arithmetic and copies ran while one was open for 3% of the time, Pallas kernels for 6%

profile of v6, /device:TPU:193, one launch (start us, length us, event | category | flops | bytes accessed | tf_op | source)
XLA Modules:
  0.0 123.3 jit_solution(15783443033733307482)
XLA Ops:
  0.6 0.7 convert_element_type.12
  1.3 1.0 pad_maximum_fusion
  2.3 3.3 %collective-permute-start = (bf16[200,640]{1,0:T(8,128)(2,1)S(1)}, bf16[200,640]{1,0:T(8,128)(2,1)S(1)}, u32[]{:S(2)}, u32[]{:S(2)}) collective-permute-start(bf16[200,640]{1,0:T(8,128)(2,1)S(1)} %pad_maximum_fusion), channel_id=1, source_target_pairs={{0,7},{1,71},{2,135},{3,199},{4,39},{5,103},{6,167},{7,231},{32,3}... | collective-permute-start | bytes 768008 | tf_op jit(solution)/shard_map/ppermute | solution.py:163
  5.6 0.7 convert_element_type.13
  6.3 1.0 pad_maximum_fusion.1
  7.3 10.7 %collective-permute-start.1 = (bf16[200,640]{1,0:T(8,128)(2,1)S(1)}, bf16[200,640]{1,0:T(8,128)(2,1)S(1)}, u32[]{:S(2)}, u32[]{:S(2)}) collective-permute-start(bf16[200,640]{1,0:T(8,128)(2,1)S(1)} %pad_maximum_fusion.1), channel_id=1, source_target_pairs={{0,3},{1,67},{2,131},{3,195},{4,35},{5,99},{6,163},{7,227},{32,0},... | collective-permute-start | bytes 768008 | tf_op jit(solution)/shard_map/ppermute | solution.py:164
  19.3 0.1 pad_maximum_fusion.2.scale_ref
  19.4 0.0 collective-permute-done
  19.4 1.1 broadcast_in_dim.2
  20.4 24.7 %all-to-all-start = ((bf16[4,200,640]{2,1,0:T(8,128)(2,1)}), bf16[4,200,640]{2,1,0:T(8,128)(2,1)S(1)}, u32[]{:S(2)}, u32[]{:S(2)}) async-start(bf16[4,200,640]{2,1,0:T(8,128)(2,1)} %broadcast_in_dim.2), calls=%async_computation | async-start | bytes 2048000 | tf_op jit(solution)/shard_map/all_to_all | solution.py:165
  45.1 0.0 collective-permute-done.1
  45.1 12.1 %all-gather = bf16[800,640]{1,0:T(8,128)(2,1)S(1)} all-gather(bf16[200,640]{1,0:T(8,128)(2,1)S(1)} %collective-permute-done.1), channel_id=2, replica_groups=mesh['h'=2,'x'=4,'c'=2,'y'=4,'z'=8] {'y'}, dimensions={0}, use_global_device_ids=true | all-gather | bytes 1280000 | tf_op jit(solution)/shard_map/all_gather | solution.py:167
  57.2 0.2 unpack_texts.1
  57.3 0.0 all-to-all-done.image_ref
  57.4 1.9 %collective-permute-start.2 = (bf16[4,200,640]{2,1,0:T(8,128)(2,1)S(1)}, bf16[4,200,640]{2,1,0:T(8,128)(2,1)S(1)}, u32[]{:S(2)}, u32[]{:S(2)}) collective-permute-start(bf16[4,200,640]{2,1,0:T(8,128)(2,1)S(1)} %all-to-all-done.image_ref), channel_id=1, source_target_pairs={{0,32},{32,0},{1,33},{33,1},{2,34},{34,2},{3,35},{35,3},{4,36},{36... | collective-permute-start | bytes 3072008 | tf_op jit(solution)/shard_map/ppermute | solution.py:166
  59.3 2.7 %own_weights.1 = (bf16[768,768]{1,0:T(8,128)(2,1)S(1)}, bf16[768,640]{1,0:T(8,128)(2,1)}, f32[768,640]{1,0:T(8,128)S(1)}) custom-call(f32[2]{0:T(128)S(1)} %pad_maximum_fusion.2.scale_ref, bf16[4,200,640]{2,1,0:T(8,128)(2,1)S(1)} %all-to-all-done.image_ref, bf16[768,640]{1,0:T(8,128)(2,1)S(1)} %get-tuple-element.11.texts, ...), custom_call_target="tpu_custom_call" | custom-call | flops 30198988800 | bytes 4194304 | tf_op jit(solution)/shard_map/own_weights/pallas_call | solution.py:66
  62.0 0.0 collective-permute-done.2.image_ref
  62.0 3.6 %other_grads.1 = (bf16[768,640]{1,0:T(8,128)(2,1)}, bf16[768,640]{1,0:T(8,128)(2,1)S(1)}) custom-call(f32[2]{0:T(128)S(1)} %pad_maximum_fusion.2.scale_ref, bf16[4,200,640]{2,1,0:T(8,128)(2,1)S(1)} %collective-permute-done.2.image_ref, bf16[768,640]{1,0:T(8,128)(2,1)S(1)} %get-tuple-element.11.texts, f32[8,768]{1,0:T(8,128)S(1)} %get-tuple-element.12.text_ids, ...), custom_call_target="tpu_custom_call" | custom-call | flops 3019898880 | bytes 4194304 | tf_op jit(solution)/shard_map/other_grads/pallas_call | solution.py:66
  65.6 0.0 copy-start
  65.6 1.0 copy-done
  66.6 2.4 %collective-permute-start.3 = (bf16[768,640]{1,0:T(8,128)(2,1)}, bf16[768,640]{1,0:T(8,128)(2,1)S(1)}, u32[]{:S(2)}, u32[]{:S(2)}) collective-permute-start(bf16[768,640]{1,0:T(8,128)(2,1)} %get-tuple-element.15), channel_id=1, source_target_pairs={{0,32},{32,0},{1,33},{33,1},{2,34},{34,2},{3,35},{35,3},{4,36},{36... | collective-permute-start | bytes 2949128 | tf_op jit(solution)/shard_map/ppermute | solution.py:179
  69.0 4.2 %all-to-all-start.1 = ((bf16[4,192,640]{2,1,0:T(8,128)(2,1)}), bf16[4,192,640]{2,1,0:T(8,128)(2,1)}, u32[]{:S(2)}, u32[]{:S(2)}) async-start(bf16[4,192,640]{2,1,0:T(8,128)(2,1)} %bitcast.5), calls=%async_computation.1 | async-start | bytes 1966080 | tf_op jit(solution)/shard_map/all_to_all | solution.py:180
  73.3 0.0 collective-permute-done.3.received
  73.3 2.1 %image_grads.1 = (bf16[192,640]{1,0:T(8,128)(2,1)}, bf16[192,640]{1,0:T(8,128)(2,1)}, bf16[192,640]{1,0:T(8,128)(2,1)}) custom-call(f32[2]{0:T(128)S(1)} %pad_maximum_fusion.2.scale_ref, s32[1]{0:T(128)} %bitcast.place_ref, bf16[768,768]{1,0:T(8,128)(2,1)S(1)} %get-tuple-element.13.weights, bf16[768,640]{1,0:T(8,128)(2,1)S(1)} %get-tuple-element.11.texts, ...), custom_call_target="tpu_custom_call" | custom-call | bytes 4194304 | tf_op jit(solution)/shard_map/image_grads/pallas_call | solution.py:66
  75.4 3.8 %collective-permute-start.4 = (bf16[192,640]{1,0:T(8,128)(2,1)}, bf16[192,640]{1,0:T(8,128)(2,1)S(1)}, u32[]{:S(2)}, u32[]{:S(2)}) collective-permute-start(bf16[192,640]{1,0:T(8,128)(2,1)} %get-tuple-element.16), channel_id=1, source_target_pairs={{0,64},{64,128},{128,192},{192,0},{1,65},{65,129},{129,193},{193,1... | collective-permute-start | bytes 737288 | tf_op jit(solution)/shard_map/ppermute | solution.py:183
  79.2 4.2 %collective-permute-start.5 = (bf16[192,640]{1,0:T(8,128)(2,1)}, bf16[192,640]{1,0:T(8,128)(2,1)}, u32[]{:S(2)}, u32[]{:S(2)}) collective-permute-start(bf16[192,640]{1,0:T(8,128)(2,1)} %get-tuple-element.17), channel_id=1, source_target_pairs={{0,128},{64,192},{128,0},{192,64},{1,129},{65,193},{129,1},{193,65... | collective-permute-start | bytes 737288 | tf_op jit(solution)/shard_map/ppermute | solution.py:183
  83.4 3.1 %collective-permute-start.6 = (bf16[192,640]{1,0:T(8,128)(2,1)}, bf16[192,640]{1,0:T(8,128)(2,1)}, u32[]{:S(2)}, u32[]{:S(2)}) collective-permute-start(bf16[192,640]{1,0:T(8,128)(2,1)} %get-tuple-element.18), channel_id=1, source_target_pairs={{0,192},{64,0},{128,64},{192,128},{1,193},{65,1},{129,65},{193,129... | collective-permute-start | bytes 737288 | tf_op jit(solution)/shard_map/ppermute | solution.py:183
  86.5 1.4 %all-to-all-done.1 = bf16[4,192,640]{2,1,0:T(8,128)(2,1)} async-done(((bf16[4,192,640]{2,1,0:T(8,128)(2,1)}), bf16[4,192,640]{2,1,0:T(8,128)(2,1)}, u32[]{:S(2)}, u32[]{:S(2)}) %all-to-all-start.1) | async-done | bytes 983072 | tf_op jit(solution)/shard_map/all_to_all | solution.py:180
  87.9 1.3 %text_sum.1 = bf16[192,640]{1,0:T(8,128)(2,1)S(1)} custom-call(bf16[768,640]{1,0:T(8,128)(2,1)} %bitcast.3.parts), custom_call_target="tpu_custom_call" | custom-call | bytes 4194304 | tf_op jit(solution)/shard_map/text_sum/pallas_call | solution.py:66
  89.2 5.9 %collective-permute-start.8 = (bf16[192,640]{1,0:T(8,128)(2,1)S(1)}, bf16[192,640]{1,0:T(8,128)(2,1)S(1)}, u32[]{:S(2)}, u32[]{:S(2)}) collective-permute-start(bf16[192,640]{1,0:T(8,128)(2,1)S(1)} %text_sum.1), channel_id=1, source_target_pairs={{3,0},{67,1},{131,2},{195,3},{35,4},{99,5},{163,6},{227,7},{0,32},... | collective-permute-start | bytes 737288 | tf_op jit(solution)/shard_map/ppermute | solution.py:187
  95.1 0.0 collective-permute-done.4.rest_0_
  95.1 0.0 collective-permute-done.5.rest_1_
  95.1 0.0 collective-permute-done.6.rest_2_
  95.1 1.5 %image_sum.1 = bf16[192,640]{1,0:T(8,128)(2,1)S(1)} custom-call(f32[2]{0:T(128)S(1)} %pad_maximum_fusion.2.scale_ref, s32[1]{0:T(128)} %bitcast.place_ref, bf16[768,768]{1,0:T(8,128)(2,1)S(1)} %get-tuple-element.13.weights, bf16[768,640]{1,0:T(8,128)(2,1)S(1)} %get-tuple-element.11.texts, bf16[768,640]{1,0:T(8,128)(2,1)S(1)} %collective-permute-done.3.received, ...), custom_call_target="tpu_custom_call" | custom-call | bytes 4194304 | tf_op jit(solution)/shard_map/image_sum/pallas_call | solution.py:66
  96.7 3.9 %collective-permute-start.7 = (bf16[192,640]{1,0:T(8,128)(2,1)S(1)}, bf16[192,640]{1,0:T(8,128)(2,1)S(1)}, u32[]{:S(2)}, u32[]{:S(2)}) collective-permute-start(bf16[192,640]{1,0:T(8,128)(2,1)S(1)} %image_sum.1), channel_id=1, source_target_pairs={{7,0},{71,1},{135,2},{199,3},{39,4},{103,5},{167,6},{231,7},{3,32}... | collective-permute-start | bytes 737288 | tf_op jit(solution)/shard_map/ppermute | solution.py:185
  100.6 11.4 %collective-permute-done.8 = bf16[192,640]{1,0:T(8,128)(2,1)S(1)} collective-permute-done((bf16[192,640]{1,0:T(8,128)(2,1)S(1)}, bf16[192,640]{1,0:T(8,128)(2,1)S(1)}, u32[]{:S(2)}, u32[]{:S(2)}) %collective-permute-start.8) | collective-permute-done | bytes 245792 | tf_op jit(solution)/shard_map/ppermute | solution.py:187
  112.0 0.8 convert_element_type.14
  112.8 9.8 %collective-permute-done.7 = bf16[192,640]{1,0:T(8,128)(2,1)S(1)} collective-permute-done((bf16[192,640]{1,0:T(8,128)(2,1)S(1)}, bf16[192,640]{1,0:T(8,128)(2,1)S(1)}, u32[]{:S(2)}, u32[]{:S(2)}) %collective-permute-start.7) | collective-permute-done | bytes 245792 | tf_op jit(solution)/shard_map/ppermute | solution.py:185
  122.6 0.7 copy.11
  (4 shorter events, 0.0 us)
Async XLA Ops:
  2.3 17.1 %collective-permute-start = (bf16[200,640]{1,0:T(8,128)(2,1)S(1)}, bf16[200,640]{1,0:T(8,128)(2,1)S(1)}, u32[]{:S(2)}, u32[]{:S(2)}) collective-permute-start(bf16[200,640]{1,0:T(8,128)(2,1)S(1)} %pad_maximum_fusion), channel_id=1, source_target_pairs={{0,7},{1,71},{2,135},{3,199},{4,39},{5,103},{6,167},{7,231},{32,3}... | collective-permute-start | bytes 768008 | tf_op jit(solution)/shard_map/ppermute | solution.py:163
  7.3 37.9 %collective-permute-start.1 = (bf16[200,640]{1,0:T(8,128)(2,1)S(1)}, bf16[200,640]{1,0:T(8,128)(2,1)S(1)}, u32[]{:S(2)}, u32[]{:S(2)}) collective-permute-start(bf16[200,640]{1,0:T(8,128)(2,1)S(1)} %pad_maximum_fusion.1), channel_id=1, source_target_pairs={{0,3},{1,67},{2,131},{3,195},{4,35},{5,99},{6,163},{7,227},{32,0},... | collective-permute-start | bytes 768008 | tf_op jit(solution)/shard_map/ppermute | solution.py:164
  20.4 36.9 %all-to-all-start = ((bf16[4,200,640]{2,1,0:T(8,128)(2,1)}), bf16[4,200,640]{2,1,0:T(8,128)(2,1)S(1)}, u32[]{:S(2)}, u32[]{:S(2)}) async-start(bf16[4,200,640]{2,1,0:T(8,128)(2,1)} %broadcast_in_dim.2), calls=%async_computation | async-start | bytes 2048000 | tf_op jit(solution)/shard_map/all_to_all | solution.py:165
  57.4 4.7 %collective-permute-start.2 = (bf16[4,200,640]{2,1,0:T(8,128)(2,1)S(1)}, bf16[4,200,640]{2,1,0:T(8,128)(2,1)S(1)}, u32[]{:S(2)}, u32[]{:S(2)}) collective-permute-start(bf16[4,200,640]{2,1,0:T(8,128)(2,1)S(1)} %all-to-all-done.image_ref), channel_id=1, source_target_pairs={{0,32},{32,0},{1,33},{33,1},{2,34},{34,2},{3,35},{35,3},{4,36},{36... | collective-permute-start | bytes 3072008 | tf_op jit(solution)/shard_map/ppermute | solution.py:166
  65.6 1.0 copy-start
  66.6 6.7 %collective-permute-start.3 = (bf16[768,640]{1,0:T(8,128)(2,1)}, bf16[768,640]{1,0:T(8,128)(2,1)S(1)}, u32[]{:S(2)}, u32[]{:S(2)}) collective-permute-start(bf16[768,640]{1,0:T(8,128)(2,1)} %get-tuple-element.15), channel_id=1, source_target_pairs={{0,32},{32,0},{1,33},{33,1},{2,34},{34,2},{3,35},{35,3},{4,36},{36... | collective-permute-start | bytes 2949128 | tf_op jit(solution)/shard_map/ppermute | solution.py:179
  69.0 18.9 %all-to-all-start.1 = ((bf16[4,192,640]{2,1,0:T(8,128)(2,1)}), bf16[4,192,640]{2,1,0:T(8,128)(2,1)}, u32[]{:S(2)}, u32[]{:S(2)}) async-start(bf16[4,192,640]{2,1,0:T(8,128)(2,1)} %bitcast.5), calls=%async_computation.1 | async-start | bytes 1966080 | tf_op jit(solution)/shard_map/all_to_all | solution.py:180
  75.4 19.7 %collective-permute-start.4 = (bf16[192,640]{1,0:T(8,128)(2,1)}, bf16[192,640]{1,0:T(8,128)(2,1)S(1)}, u32[]{:S(2)}, u32[]{:S(2)}) collective-permute-start(bf16[192,640]{1,0:T(8,128)(2,1)} %get-tuple-element.16), channel_id=1, source_target_pairs={{0,64},{64,128},{128,192},{192,0},{1,65},{65,129},{129,193},{193,1... | collective-permute-start | bytes 737288 | tf_op jit(solution)/shard_map/ppermute | solution.py:183
  79.2 15.9 %collective-permute-start.5 = (bf16[192,640]{1,0:T(8,128)(2,1)}, bf16[192,640]{1,0:T(8,128)(2,1)}, u32[]{:S(2)}, u32[]{:S(2)}) collective-permute-start(bf16[192,640]{1,0:T(8,128)(2,1)} %get-tuple-element.17), channel_id=1, source_target_pairs={{0,128},{64,192},{128,0},{192,64},{1,129},{65,193},{129,1},{193,65... | collective-permute-start | bytes 737288 | tf_op jit(solution)/shard_map/ppermute | solution.py:183
  83.4 11.7 %collective-permute-start.6 = (bf16[192,640]{1,0:T(8,128)(2,1)}, bf16[192,640]{1,0:T(8,128)(2,1)}, u32[]{:S(2)}, u32[]{:S(2)}) collective-permute-start(bf16[192,640]{1,0:T(8,128)(2,1)} %get-tuple-element.18), channel_id=1, source_target_pairs={{0,192},{64,0},{128,64},{192,128},{1,193},{65,1},{129,65},{193,129... | collective-permute-start | bytes 737288 | tf_op jit(solution)/shard_map/ppermute | solution.py:183
  89.2 22.8 %collective-permute-start.8 = (bf16[192,640]{1,0:T(8,128)(2,1)S(1)}, bf16[192,640]{1,0:T(8,128)(2,1)S(1)}, u32[]{:S(2)}, u32[]{:S(2)}) collective-permute-start(bf16[192,640]{1,0:T(8,128)(2,1)S(1)} %text_sum.1), channel_id=1, source_target_pairs={{3,0},{67,1},{131,2},{195,3},{35,4},{99,5},{163,6},{227,7},{0,32},... | collective-permute-start | bytes 737288 | tf_op jit(solution)/shard_map/ppermute | solution.py:187
  96.7 25.9 %collective-permute-start.7 = (bf16[192,640]{1,0:T(8,128)(2,1)S(1)}, bf16[192,640]{1,0:T(8,128)(2,1)S(1)}, u32[]{:S(2)}, u32[]{:S(2)}) collective-permute-start(bf16[192,640]{1,0:T(8,128)(2,1)S(1)} %image_sum.1), channel_id=1, source_target_pairs={{7,0},{71,1},{135,2},{199,3},{39,4},{103,5},{167,6},{231,7},{3,32}... | collective-permute-start | bytes 737288 | tf_op jit(solution)/shard_map/ppermute | solution.py:185

commit v7 on v6

--- a/solution.py
+++ b/solution.py
@@ -179,7 +179,7 @@
     received = lax.ppermute(other_grad, "c", [(0, 1), (1, 0)])
     text_parts = lax.all_to_all(text_part, "y", split_axis=0, concat_axis=0, tiled=True)
     shard = ((ROWS, D), bf16)
-    sent = call(image_kernel, "image_grads", (shard,) * 3, [SMEM, SMEM] + [VMEM] * 3, 0, scale, place, own_weights, all_texts, received)
+    sent = call(image_kernel, "image_grads", (shard,) * 3, [SMEM, SMEM] + [VMEM] * 3, 40 * flops, scale, place, own_weights, all_texts, received)
     parts = [lax.ppermute(part, "x", [(i, (i + k) % 4) for i in range(4)]) for k, part in enumerate(sent, 1)]
     (kept,) = call(image_sum_kernel, "image_sum", (shard,), [SMEM, SMEM] + [VMEM] * 6, 0, scale, place, own_weights, all_texts, received, *parts)
     image_home = lax.ppermute(kept, MOVE_AXES, back(IMAGE_ROUTE))

time: 124 us -> 124 us (level)
  the two profiles are of different devices: /device:TPU:193 before, /device:TPU:15 now
where the time goes in v7:
time: 124 us; the launch traced here: 123 us
  starting transfers between devices  68 us (55%)
  waiting for transfers between devices  21.4 us (17%)
  blocking collectives  13.3 us (11%)
  Pallas kernels  11.3 us (9%)
  other arithmetic  4.19 us (3%)
  local copies, waits for them, and re-layouts  2.75 us (2%)
  between operations  2.1 us (2%)
    ppermute x1, starting transfers between devices, body(): text_home = lax.ppermute(text_sum, MOVE_AXES, back(TEXT_ROUTE))  18.1 us
    all_gather x1, blocking collectives, body(): text = lax.all_gather(texts, 'y', axis=0)  13.3 us
    pallas_call x6, Pallas kernels, call(): pl.pallas_call(kernel, out_shape=tuple((jax.ShapeDtypeStruct(shape, kind)...  11.3 us
    ppermute x1, starting transfers between devices, body(): image_home = lax.ppermute(kept, MOVE_AXES, back(IMAGE_ROUTE))  10.3 us
    ppermute x1, waiting for transfers between devices, body(): images = lax.ppermute(packed_images, MOVE_AXES, IMAGE_ROUTE)  9.79 us
    ppermute x3, starting transfers between devices, body(): lax.ppermute(part, 'x', [(i, (i + k) % 4) for i in range(4)])  9.69 us
    ppermute x1, starting transfers between devices, body(): images = lax.ppermute(packed_images, MOVE_AXES, IMAGE_ROUTE)  9.38 us
    ppermute x1, starting transfers between devices, body(): texts = lax.ppermute(packed_texts, MOVE_AXES, TEXT_ROUTE)  8.01 us
  transfers between devices with their start and end apart: 11, of which 4 were waited for; matrix products, arithmetic and copies ran while one was open for 3% of the time, Pallas kernels for 6%

profile of v7, /device:TPU:15, one launch (start us, length us, event | category | flops | bytes accessed | tf_op | source)
XLA Modules:
  0.0 122.9 jit_solution(16433777344600993121)
XLA Ops:
  0.6 0.7 convert_element_type.12
  1.3 1.0 pad_maximum_fusion
  2.3 9.4 %collective-permute-start = (bf16[200,640]{1,0:T(8,128)(2,1)S(1)}, bf16[200,640]{1,0:T(8,128)(2,1)S(1)}, u32[]{:S(2)}, u32[]{:S(2)}) collective-permute-start(bf16[200,640]{1,0:T(8,128)(2,1)S(1)} %pad_maximum_fusion), channel_id=1, source_target_pairs={{0,7},{1,71},{2,135},{3,199},{4,39},{5,103},{6,167},{7,231},{32,3}... | collective-permute-start | bytes 768008 | tf_op jit(solution)/shard_map/ppermute | solution.py:163
  11.7 0.7 convert_element_type.13
  12.4 1.0 pad_maximum_fusion.1
  13.4 8.0 %collective-permute-start.1 = (bf16[200,640]{1,0:T(8,128)(2,1)S(1)}, bf16[200,640]{1,0:T(8,128)(2,1)S(1)}, u32[]{:S(2)}, u32[]{:S(2)}) collective-permute-start(bf16[200,640]{1,0:T(8,128)(2,1)S(1)} %pad_maximum_fusion.1), channel_id=1, source_target_pairs={{0,3},{1,67},{2,131},{3,195},{4,35},{5,99},{6,163},{7,227},{32,0},... | collective-permute-start | bytes 768008 | tf_op jit(solution)/shard_map/ppermute | solution.py:164
  22.7 0.1 pad_maximum_fusion.2.scale_ref
  22.7 9.8 %collective-permute-done = bf16[200,640]{1,0:T(8,128)(2,1)S(1)} collective-permute-done((bf16[200,640]{1,0:T(8,128)(2,1)S(1)}, bf16[200,640]{1,0:T(8,128)(2,1)S(1)}, u32[]{:S(2)}, u32[]{:S(2)}) %collective-permute-start) | collective-permute-done | bytes 256032 | tf_op jit(solution)/shard_map/ppermute | solution.py:163
  32.5 1.1 broadcast_in_dim.2
  33.6 3.9 %all-to-all-start = ((bf16[4,200,640]{2,1,0:T(8,128)(2,1)}), bf16[4,200,640]{2,1,0:T(8,128)(2,1)S(1)}, u32[]{:S(2)}, u32[]{:S(2)}) async-start(bf16[4,200,640]{2,1,0:T(8,128)(2,1)} %broadcast_in_dim.2), calls=%async_computation | async-start | bytes 2048000 | tf_op jit(solution)/shard_map/all_to_all | solution.py:165
  37.5 3.2 %collective-permute-done.1 = bf16[200,640]{1,0:T(8,128)(2,1)S(1)} collective-permute-done((bf16[200,640]{1,0:T(8,128)(2,1)S(1)}, bf16[200,640]{1,0:T(8,128)(2,1)S(1)}, u32[]{:S(2)}, u32[]{:S(2)}) %collective-permute-start.1) | collective-permute-done | bytes 256032 | tf_op jit(solution)/shard_map/ppermute | solution.py:164
  40.7 13.3 %all-gather = bf16[800,640]{1,0:T(8,128)(2,1)S(1)} all-gather(bf16[200,640]{1,0:T(8,128)(2,1)S(1)} %collective-permute-done.1), channel_id=2, replica_groups=mesh['h'=2,'x'=4,'c'=2,'y'=4,'z'=8] {'y'}, dimensions={0}, use_global_device_ids=true | all-gather | bytes 1280000 | tf_op jit(solution)/shard_map/all_gather | solution.py:167
  54.0 0.2 unpack_texts.1
  54.1 0.0 copy-start
  54.2 0.0 all-to-all-done.image_ref
  54.2 2.2 %collective-permute-start.2 = (bf16[4,200,640]{2,1,0:T(8,128)(2,1)S(1)}, bf16[4,200,640]{2,1,0:T(8,128)(2,1)S(1)}, u32[]{:S(2)}, u32[]{:S(2)}) collective-permute-start(bf16[4,200,640]{2,1,0:T(8,128)(2,1)S(1)} %all-to-all-done.image_ref), channel_id=1, source_target_pairs={{0,32},{32,0},{1,33},{33,1},{2,34},{34,2},{3,35},{35,3},{4,36},{36... | collective-permute-start | bytes 3072008 | tf_op jit(solution)/shard_map/ppermute | solution.py:166
  56.4 2.7 %own_weights.1 = (bf16[768,768]{1,0:T(8,128)(2,1)S(1)}, bf16[768,640]{1,0:T(8,128)(2,1)}, f32[768,640]{1,0:T(8,128)S(1)}) custom-call(f32[2]{0:T(128)S(1)} %pad_maximum_fusion.2.scale_ref, bf16[4,200,640]{2,1,0:T(8,128)(2,1)S(1)} %all-to-all-done.image_ref, bf16[768,640]{1,0:T(8,128)(2,1)S(1)} %get-tuple-element.11.texts, ...), custom_call_target="tpu_custom_call" | custom-call | flops 30198988800 | bytes 4194304 | tf_op jit(solution)/shard_map/own_weights/pallas_call | solution.py:66
  59.1 0.0 collective-permute-done.2.image_ref
  59.1 0.0 copy-done
  59.1 3.6 %other_grads.1 = (bf16[768,640]{1,0:T(8,128)(2,1)}, bf16[768,640]{1,0:T(8,128)(2,1)S(1)}) custom-call(f32[2]{0:T(128)S(1)} %pad_maximum_fusion.2.scale_ref, bf16[4,200,640]{2,1,0:T(8,128)(2,1)S(1)} %collective-permute-done.2.image_ref, bf16[768,640]{1,0:T(8,128)(2,1)S(1)} %get-tuple-element.11.texts, f32[8,768]{1,0:T(8,128)S(1)} %get-tuple-element.12.text_ids, ...), custom_call_target="tpu_custom_call" | custom-call | flops 3019898880 | bytes 4194304 | tf_op jit(solution)/shard_map/other_grads/pallas_call | solution.py:66
  62.8 0.0 copy-start.2
  62.8 1.0 copy-done.2
  63.7 0.0 copy-start.1
  63.7 2.3 %collective-permute-start.3 = (bf16[768,640]{1,0:T(8,128)(2,1)}, bf16[768,640]{1,0:T(8,128)(2,1)}, u32[]{:S(2)}, u32[]{:S(2)}) collective-permute-start(bf16[768,640]{1,0:T(8,128)(2,1)} %get-tuple-element.15), channel_id=1, source_target_pairs={{0,32},{32,0},{1,33},{33,1},{2,34},{34,2},{3,35},{35,3},{4,36},{36... | collective-permute-start | bytes 2949128 | tf_op jit(solution)/shard_map/ppermute | solution.py:179
  66.0 4.1 %all-to-all-start.1 = ((bf16[4,192,640]{2,1,0:T(8,128)(2,1)}), bf16[4,192,640]{2,1,0:T(8,128)(2,1)S(1)}, u32[]{:S(2)}, u32[]{:S(2)}) async-start(bf16[4,192,640]{2,1,0:T(8,128)(2,1)} %bitcast.6), calls=%async_computation.1 | async-start | bytes 1966080 | tf_op jit(solution)/shard_map/all_to_all | solution.py:180
  70.1 0.0 collective-permute-done.3.received
  70.1 0.0 copy-done.1
  70.1 2.8 %image_grads.1 = (bf16[192,640]{1,0:T(8,128)(2,1)}, bf16[192,640]{1,0:T(8,128)(2,1)}, bf16[192,640]{1,0:T(8,128)(2,1)}) custom-call(f32[2]{0:T(128)S(1)} %pad_maximum_fusion.2.scale_ref, s32[1]{0:T(128)} %bitcast.place_ref, bf16[768,768]{1,0:T(8,128)(2,1)S(1)} %get-tuple-element.13.weights, bf16[768,640]{1,0:T(8,128)(2,1)S(1)} %copy-done.1, ...), custom_call_target="tpu_custom_call" | custom-call | flops 30198988800 | bytes 4194304 | tf_op jit(solution)/shard_map/image_grads/pallas_call | solution.py:66
  72.9 5.3 %collective-permute-start.4 = (bf16[192,640]{1,0:T(8,128)(2,1)}, bf16[192,640]{1,0:T(8,128)(2,1)S(1)}, u32[]{:S(2)}, u32[]{:S(2)}) collective-permute-start(bf16[192,640]{1,0:T(8,128)(2,1)} %get-tuple-element.16), channel_id=1, source_target_pairs={{0,64},{64,128},{128,192},{192,0},{1,65},{65,129},{129,193},{193,1... | collective-permute-start | bytes 737288 | tf_op jit(solution)/shard_map/ppermute | solution.py:183
  78.2 1.9 %collective-permute-start.5 = (bf16[192,640]{1,0:T(8,128)(2,1)}, bf16[192,640]{1,0:T(8,128)(2,1)}, u32[]{:S(2)}, u32[]{:S(2)}) collective-permute-start(bf16[192,640]{1,0:T(8,128)(2,1)} %get-tuple-element.17), channel_id=1, source_target_pairs={{0,128},{64,192},{128,0},{192,64},{1,129},{65,193},{129,1},{193,65... | collective-permute-start | bytes 737288 | tf_op jit(solution)/shard_map/ppermute | solution.py:183
  80.1 2.5 %collective-permute-start.6 = (bf16[192,640]{1,0:T(8,128)(2,1)}, bf16[192,640]{1,0:T(8,128)(2,1)}, u32[]{:S(2)}, u32[]{:S(2)}) collective-permute-start(bf16[192,640]{1,0:T(8,128)(2,1)} %get-tuple-element.18), channel_id=1, source_target_pairs={{0,192},{64,0},{128,64},{192,128},{1,193},{65,1},{129,65},{193,129... | collective-permute-start | bytes 737288 | tf_op jit(solution)/shard_map/ppermute | solution.py:183
  82.6 0.4 all-to-all-done.1
  83.1 0.1 text_sum.1
  83.2 18.1 %collective-permute-start.8 = (bf16[192,640]{1,0:T(8,128)(2,1)S(1)}, bf16[192,640]{1,0:T(8,128)(2,1)S(1)}, u32[]{:S(2)}, u32[]{:S(2)}) collective-permute-start(bf16[192,640]{1,0:T(8,128)(2,1)S(1)} %text_sum.1), channel_id=1, source_target_pairs={{3,0},{67,1},{131,2},{195,3},{35,4},{99,5},{163,6},{227,7},{0,32},... | collective-permute-start | bytes 737288 | tf_op jit(solution)/shard_map/ppermute | solution.py:187
  101.3 0.0 collective-permute-done.4.rest_0_
  101.3 0.0 collective-permute-done.5.rest_1_
  101.3 0.0 collective-permute-done.6.rest_2_
  101.3 1.8 %image_sum.1 = bf16[192,640]{1,0:T(8,128)(2,1)S(1)} custom-call(f32[2]{0:T(128)S(1)} %pad_maximum_fusion.2.scale_ref, s32[1]{0:T(128)} %bitcast.place_ref, bf16[768,768]{1,0:T(8,128)(2,1)S(1)} %get-tuple-element.13.weights, bf16[768,640]{1,0:T(8,128)(2,1)S(1)} %copy-done.1, bf16[768,640]{1,0:T(8,128)(2,1)} %collective-permute-done.3.received, ...), custom_call_target="tpu_custom_call" | custom-call | bytes 4194304 | tf_op jit(solution)/shard_map/image_sum/pallas_call | solution.py:66
  103.2 10.3 %collective-permute-start.7 = (bf16[192,640]{1,0:T(8,128)(2,1)S(1)}, bf16[192,640]{1,0:T(8,128)(2,1)S(1)}, u32[]{:S(2)}, u32[]{:S(2)}) collective-permute-start(bf16[192,640]{1,0:T(8,128)(2,1)S(1)} %image_sum.1), channel_id=1, source_target_pairs={{7,0},{71,1},{135,2},{199,3},{39,4},{103,5},{167,6},{231,7},{3,32}... | collective-permute-start | bytes 737288 | tf_op jit(solution)/shard_map/ppermute | solution.py:185
  113.5 0.0 collective-permute-done.8
  113.5 0.8 convert_element_type.14
  114.3 7.9 %collective-permute-done.7 = bf16[192,640]{1,0:T(8,128)(2,1)S(1)} collective-permute-done((bf16[192,640]{1,0:T(8,128)(2,1)S(1)}, bf16[192,640]{1,0:T(8,128)(2,1)S(1)}, u32[]{:S(2)}, u32[]{:S(2)}) %collective-permute-start.7) | collective-permute-done | bytes 245792 | tf_op jit(solution)/shard_map/ppermute | solution.py:185
  122.3 0.7 copy.11
  (4 shorter events, 0.0 us)
Async XLA Ops:
  2.3 30.2 %collective-permute-start = (bf16[200,640]{1,0:T(8,128)(2,1)S(1)}, bf16[200,640]{1,0:T(8,128)(2,1)S(1)}, u32[]{:S(2)}, u32[]{:S(2)}) collective-permute-start(bf16[200,640]{1,0:T(8,128)(2,1)S(1)} %pad_maximum_fusion), channel_id=1, source_target_pairs={{0,7},{1,71},{2,135},{3,199},{4,39},{5,103},{6,167},{7,231},{32,3}... | collective-permute-start | bytes 768008 | tf_op jit(solution)/shard_map/ppermute | solution.py:163
  13.4 27.4 %collective-permute-start.1 = (bf16[200,640]{1,0:T(8,128)(2,1)S(1)}, bf16[200,640]{1,0:T(8,128)(2,1)S(1)}, u32[]{:S(2)}, u32[]{:S(2)}) collective-permute-start(bf16[200,640]{1,0:T(8,128)(2,1)S(1)} %pad_maximum_fusion.1), channel_id=1, source_target_pairs={{0,3},{1,67},{2,131},{3,195},{4,35},{5,99},{6,163},{7,227},{32,0},... | collective-permute-start | bytes 768008 | tf_op jit(solution)/shard_map/ppermute | solution.py:164
  33.6 20.6 %all-to-all-start = ((bf16[4,200,640]{2,1,0:T(8,128)(2,1)}), bf16[4,200,640]{2,1,0:T(8,128)(2,1)S(1)}, u32[]{:S(2)}, u32[]{:S(2)}) async-start(bf16[4,200,640]{2,1,0:T(8,128)(2,1)} %broadcast_in_dim.2), calls=%async_computation | async-start | bytes 2048000 | tf_op jit(solution)/shard_map/all_to_all | solution.py:165
  54.1 5.0 %copy-start = (bf16[768,640]{1,0:T(8,128)(2,1)}, bf16[768,640]{1,0:T(8,128)(2,1)S(1)}, u32[]{:S(2)}) copy-start(bf16[768,640]{1,0:T(8,128)(2,1)S(1)} %get-tuple-element.11.texts) | copy-start | bytes 2949124
  54.2 5.0 %collective-permute-start.2 = (bf16[4,200,640]{2,1,0:T(8,128)(2,1)S(1)}, bf16[4,200,640]{2,1,0:T(8,128)(2,1)S(1)}, u32[]{:S(2)}, u32[]{:S(2)}) collective-permute-start(bf16[4,200,640]{2,1,0:T(8,128)(2,1)S(1)} %all-to-all-done.image_ref), channel_id=1, source_target_pairs={{0,32},{32,0},{1,33},{33,1},{2,34},{34,2},{3,35},{35,3},{4,36},{36... | collective-permute-start | bytes 3072008 | tf_op jit(solution)/shard_map/ppermute | solution.py:166
  62.8 1.0 copy-start.2
  63.7 6.4 %copy-start.1 = (bf16[768,640]{1,0:T(8,128)(2,1)S(1)}, bf16[768,640]{1,0:T(8,128)(2,1)}, u32[]{:S(2)}) copy-start(bf16[768,640]{1,0:T(8,128)(2,1)} %copy-done) | copy-start | bytes 2949124
  63.7 6.4 %collective-permute-start.3 = (bf16[768,640]{1,0:T(8,128)(2,1)}, bf16[768,640]{1,0:T(8,128)(2,1)}, u32[]{:S(2)}, u32[]{:S(2)}) collective-permute-start(bf16[768,640]{1,0:T(8,128)(2,1)} %get-tuple-element.15), channel_id=1, source_target_pairs={{0,32},{32,0},{1,33},{33,1},{2,34},{34,2},{3,35},{35,3},{4,36},{36... | collective-permute-start | bytes 2949128 | tf_op jit(solution)/shard_map/ppermute | solution.py:179
  66.0 17.0 %all-to-all-start.1 = ((bf16[4,192,640]{2,1,0:T(8,128)(2,1)}), bf16[4,192,640]{2,1,0:T(8,128)(2,1)S(1)}, u32[]{:S(2)}, u32[]{:S(2)}) async-start(bf16[4,192,640]{2,1,0:T(8,128)(2,1)} %bitcast.6), calls=%async_computation.1 | async-start | bytes 1966080 | tf_op jit(solution)/shard_map/all_to_all | solution.py:180
  72.9 28.4 %collective-permute-start.4 = (bf16[192,640]{1,0:T(8,128)(2,1)}, bf16[192,640]{1,0:T(8,128)(2,1)S(1)}, u32[]{:S(2)}, u32[]{:S(2)}) collective-permute-start(bf16[192,640]{1,0:T(8,128)(2,1)} %get-tuple-element.16), channel_id=1, source_target_pairs={{0,64},{64,128},{128,192},{192,0},{1,65},{65,129},{129,193},{193,1... | collective-permute-start | bytes 737288 | tf_op jit(solution)/shard_map/ppermute | solution.py:183
  78.2 23.1 %collective-permute-start.5 = (bf16[192,640]{1,0:T(8,128)(2,1)}, bf16[192,640]{1,0:T(8,128)(2,1)}, u32[]{:S(2)}, u32[]{:S(2)}) collective-permute-start(bf16[192,640]{1,0:T(8,128)(2,1)} %get-tuple-element.17), channel_id=1, source_target_pairs={{0,128},{64,192},{128,0},{192,64},{1,129},{65,193},{129,1},{193,65... | collective-permute-start | bytes 737288 | tf_op jit(solution)/shard_map/ppermute | solution.py:183
  80.1 21.2 %collective-permute-start.6 = (bf16[192,640]{1,0:T(8,128)(2,1)}, bf16[192,640]{1,0:T(8,128)(2,1)}, u32[]{:S(2)}, u32[]{:S(2)}) collective-permute-start(bf16[192,640]{1,0:T(8,128)(2,1)} %get-tuple-element.18), channel_id=1, source_target_pairs={{0,192},{64,0},{128,64},{192,128},{1,193},{65,1},{129,65},{193,129... | collective-permute-start | bytes 737288 | tf_op jit(solution)/shard_map/ppermute | solution.py:183
  83.2 30.3 %collective-permute-start.8 = (bf16[192,640]{1,0:T(8,128)(2,1)S(1)}, bf16[192,640]{1,0:T(8,128)(2,1)S(1)}, u32[]{:S(2)}, u32[]{:S(2)}) collective-permute-start(bf16[192,640]{1,0:T(8,128)(2,1)S(1)} %text_sum.1), channel_id=1, source_target_pairs={{3,0},{67,1},{131,2},{195,3},{35,4},{99,5},{163,6},{227,7},{0,32},... | collective-permute-start | bytes 737288 | tf_op jit(solution)/shard_map/ppermute | solution.py:187
  103.2 19.1 %collective-permute-start.7 = (bf16[192,640]{1,0:T(8,128)(2,1)S(1)}, bf16[192,640]{1,0:T(8,128)(2,1)S(1)}, u32[]{:S(2)}, u32[]{:S(2)}) collective-permute-start(bf16[192,640]{1,0:T(8,128)(2,1)S(1)} %image_sum.1), channel_id=1, source_target_pairs={{7,0},{71,1},{135,2},{199,3},{39,4},{103,5},{167,6},{231,7},{3,32}... | collective-permute-start | bytes 737288 | tf_op jit(solution)/shard_map/ppermute | solution.py:185

commit v8 on v6

--- a/solution.py
+++ b/solution.py
@@ -17,6 +17,7 @@
 D = 640
 GROUP = 4 * ROWS
 CHUNK = 256
+STEPS = (2, 1, 3)
 
 PLANE = (7, 3, 0, 5, 2, 6, 1, 4)
 IMAGE_PLACE = ((0, 2, 4, 6, 1, 3, 5, 7), (0, 2, 4, 6, 1, 3, 5, 7), (2, 0, 6, 4, 3, 1, 7, 5), (2, 0, 6, 4, 3, 1, 7, 5), (4, 6, 0, 2, 5, 7, 1, 3), (4, 6, 0, 2, 5, 7, 1, 3), (6, 4, 2, 0, 7, 5, 3, 1), (6, 4, 2, 0, 7, 5, 3, 1))
@@ -44,7 +45,8 @@
 
 
 def pack(rows, ids):
-    below = jnp.broadcast_to(ids.astype(jnp.bfloat16)[None, :], (EXTRA, ROWS))
+    row = lax.optimization_barrier(ids[None, :])
+    below = jnp.broadcast_to(row.astype(jnp.bfloat16), (EXTRA, ROWS))
     return jnp.concatenate([rows, jnp.pad(below, ((0, 0), (0, D - ROWS)))], axis=0)
 
 
@@ -136,7 +138,7 @@
 
 
 def image_kernel(scale_ref, place_ref, weights, texts, received, *sent):
-    for k, out in enumerate(sent, 1):
+    for k, out in zip(STEPS, sent):
         out[...] = image_shard(scale_ref, lax.rem(place_ref[0] + k, 4), weights, texts, received).astype(out.dtype)
 
 
@@ -180,7 +182,7 @@
     text_parts = lax.all_to_all(text_part, "y", split_axis=0, concat_axis=0, tiled=True)
     shard = ((ROWS, D), bf16)
     sent = call(image_kernel, "image_grads", (shard,) * 3, [SMEM, SMEM] + [VMEM] * 3, 0, scale, place, own_weights, all_texts, received)
-    parts = [lax.ppermute(part, "x", [(i, (i + k) % 4) for i in range(4)]) for k, part in enumerate(sent, 1)]
+    parts = [lax.ppermute(part, "x", [(i, (i + k) % 4) for i in range(4)]) for k, part in zip(STEPS, sent)]
     (kept,) = call(image_sum_kernel, "image_sum", (shard,), [SMEM, SMEM] + [VMEM] * 6, 0, scale, place, own_weights, all_texts, received, *parts)
     image_home = lax.ppermute(kept, MOVE_AXES, back(IMAGE_ROUTE))
     (text_sum,) = call(text_sum_kernel, "text_sum", (shard,), [VMEM], 0, text_parts)

time: 124 us -> 124 us (level)
    ppermute x1, waiting for transfers between devices: 11.4 us -> 13 us  [body(): text_home = lax.ppermute(text_sum, MOVE_AXES, back(TEXT_ROUTE))]
    ppermute x1, starting transfers between devices: 3.93 us -> 2.38 us  [body(): image_home = lax.ppermute(kept, MOVE_AXES, back(IMAGE_ROUTE))]
where the time goes in v8:
time: 124 us; the launch traced here: 123 us
  starting transfers between devices  67.2 us (54%)
  waiting for transfers between devices  23.6 us (19%)
  blocking collectives  12.1 us (10%)
  Pallas kernels  11.5 us (9%)
  other arithmetic  4.23 us (3%)
  local copies, waits for them, and re-layouts  2.76 us (2%)
  between operations  2.11 us (2%)
    all_to_all x1, starting transfers between devices, body(): lax.all_to_all(jnp.broadcast_to(images[None], (4, PACKED, D)), 'x', split...  24.7 us
    ppermute x1, waiting for transfers between devices, body(): text_home = lax.ppermute(text_sum, MOVE_AXES, back(TEXT_ROUTE))  13 us
    all_gather x1, blocking collectives, body(): text = lax.all_gather(texts, 'y', axis=0)  12.1 us
    ppermute x3, starting transfers between devices, body(): lax.ppermute(part, 'x', [(i, (i + k) % 4) for i in range(4)])  11.7 us
    pallas_call x6, Pallas kernels, call(): pl.pallas_call(kernel, out_shape=tuple((jax.ShapeDtypeStruct(shape, kind)...  11.5 us
    ppermute x1, starting transfers between devices, body(): texts = lax.ppermute(packed_texts, MOVE_AXES, TEXT_ROUTE)  10.7 us
    ppermute x1, waiting for transfers between devices, body(): image_home = lax.ppermute(kept, MOVE_AXES, back(IMAGE_ROUTE))  9.83 us
    ppermute x1, starting transfers between devices, body(): text_home = lax.ppermute(text_sum, MOVE_AXES, back(TEXT_ROUTE))  5.89 us
  transfers between devices with their start and end apart: 11, of which 3 were waited for; matrix products, arithmetic and copies ran while one was open for 3% of the time, Pallas kernels for 6%

profile of v8, /device:TPU:193, one launch (start us, length us, event | category | flops | bytes accessed | tf_op | source)
XLA Modules:
  0.0 123.4 jit_solution(9704436875311981322)
XLA Ops:
  0.6 0.7 convert_reduce_fusion.1
  1.4 1.0 pad_maximum_fusion
  2.3 3.3 %collective-permute-start = (bf16[200,640]{1,0:T(8,128)(2,1)S(1)}, bf16[200,640]{1,0:T(8,128)(2,1)S(1)}, u32[]{:S(2)}, u32[]{:S(2)}) collective-permute-start(bf16[200,640]{1,0:T(8,128)(2,1)S(1)} %pad_maximum_fusion), channel_id=1, source_target_pairs={{0,7},{1,71},{2,135},{3,199},{4,39},{5,103},{6,167},{7,231},{32,3}... | collective-permute-start | bytes 768008 | tf_op jit(solution)/shard_map/ppermute | solution.py:165
  5.6 0.7 convert_reduce_fusion
  6.3 1.0 pad_maximum_fusion.1
  7.3 10.7 %collective-permute-start.1 = (bf16[200,640]{1,0:T(8,128)(2,1)S(1)}, bf16[200,640]{1,0:T(8,128)(2,1)S(1)}, u32[]{:S(2)}, u32[]{:S(2)}) collective-permute-start(bf16[200,640]{1,0:T(8,128)(2,1)S(1)} %pad_maximum_fusion.1), channel_id=1, source_target_pairs={{0,3},{1,67},{2,131},{3,195},{4,35},{5,99},{6,163},{7,227},{32,0},... | collective-permute-start | bytes 768008 | tf_op jit(solution)/shard_map/ppermute | solution.py:166
  19.3 0.1 pad_maximum_fusion.2.scale_ref
  19.4 0.0 collective-permute-done
  19.4 1.0 broadcast_in_dim.24
  20.5 24.7 %all-to-all-start = ((bf16[4,200,640]{2,1,0:T(8,128)(2,1)}), bf16[4,200,640]{2,1,0:T(8,128)(2,1)S(1)}, u32[]{:S(2)}, u32[]{:S(2)}) async-start(bf16[4,200,640]{2,1,0:T(8,128)(2,1)} %broadcast_in_dim.24), calls=%async_computation | async-start | bytes 2048000 | tf_op jit(solution)/shard_map/all_to_all | solution.py:167
  45.2 0.0 collective-permute-done.1
  45.2 12.1 %all-gather = bf16[800,640]{1,0:T(8,128)(2,1)S(1)} all-gather(bf16[200,640]{1,0:T(8,128)(2,1)S(1)} %collective-permute-done.1), channel_id=2, replica_groups=mesh['h'=2,'x'=4,'c'=2,'y'=4,'z'=8] {'y'}, dimensions={0}, use_global_device_ids=true | all-gather | bytes 1280000 | tf_op jit(solution)/shard_map/all_gather | solution.py:169
  57.2 0.2 unpack_texts.1
  57.4 0.0 all-to-all-done.image_ref
  57.4 1.9 %collective-permute-start.2 = (bf16[4,200,640]{2,1,0:T(8,128)(2,1)S(1)}, bf16[4,200,640]{2,1,0:T(8,128)(2,1)S(1)}, u32[]{:S(2)}, u32[]{:S(2)}) collective-permute-start(bf16[4,200,640]{2,1,0:T(8,128)(2,1)S(1)} %all-to-all-done.image_ref), channel_id=1, source_target_pairs={{0,32},{32,0},{1,33},{33,1},{2,34},{34,2},{3,35},{35,3},{4,36},{36... | collective-permute-start | bytes 3072008 | tf_op jit(solution)/shard_map/ppermute | solution.py:168
  59.3 2.7 %own_weights.1 = (bf16[768,768]{1,0:T(8,128)(2,1)S(1)}, bf16[768,640]{1,0:T(8,128)(2,1)}, f32[768,640]{1,0:T(8,128)S(1)}) custom-call(f32[2]{0:T(128)S(1)} %pad_maximum_fusion.2.scale_ref, bf16[4,200,640]{2,1,0:T(8,128)(2,1)S(1)} %all-to-all-done.image_ref, bf16[768,640]{1,0:T(8,128)(2,1)S(1)} %get-tuple-element.11.texts, ...), custom_call_target="tpu_custom_call" | custom-call | flops 30198988800 | bytes 4194304 | tf_op jit(solution)/shard_map/own_weights/pallas_call | solution.py:68
  62.0 0.0 collective-permute-done.2.image_ref
  62.0 3.6 %other_grads.1 = (bf16[768,640]{1,0:T(8,128)(2,1)}, bf16[768,640]{1,0:T(8,128)(2,1)S(1)}) custom-call(f32[2]{0:T(128)S(1)} %pad_maximum_fusion.2.scale_ref, bf16[4,200,640]{2,1,0:T(8,128)(2,1)S(1)} %collective-permute-done.2.image_ref, bf16[768,640]{1,0:T(8,128)(2,1)S(1)} %get-tuple-element.11.texts, f32[8,768]{1,0:T(8,128)S(1)} %get-tuple-element.12.text_ids, ...), custom_call_target="tpu_custom_call" | custom-call | flops 3019898880 | bytes 4194304 | tf_op jit(solution)/shard_map/other_grads/pallas_call | solution.py:68
  65.7 0.0 copy-start
  65.7 1.0 copy-done
  66.7 2.4 %collective-permute-start.3 = (bf16[768,640]{1,0:T(8,128)(2,1)}, bf16[768,640]{1,0:T(8,128)(2,1)S(1)}, u32[]{:S(2)}, u32[]{:S(2)}) collective-permute-start(bf16[768,640]{1,0:T(8,128)(2,1)} %get-tuple-element.15), channel_id=1, source_target_pairs={{0,32},{32,0},{1,33},{33,1},{2,34},{34,2},{3,35},{35,3},{4,36},{36... | collective-permute-start | bytes 2949128 | tf_op jit(solution)/shard_map/ppermute | solution.py:181
  69.1 4.3 %all-to-all-start.1 = ((bf16[4,192,640]{2,1,0:T(8,128)(2,1)}), bf16[4,192,640]{2,1,0:T(8,128)(2,1)}, u32[]{:S(2)}, u32[]{:S(2)}) async-start(bf16[4,192,640]{2,1,0:T(8,128)(2,1)} %bitcast.7), calls=%async_computation.1 | async-start | bytes 1966080 | tf_op jit(solution)/shard_map/all_to_all | solution.py:182
  73.3 0.0 collective-permute-done.3.received
  73.3 2.1 %image_grads.1 = (bf16[192,640]{1,0:T(8,128)(2,1)}, bf16[192,640]{1,0:T(8,128)(2,1)}, bf16[192,640]{1,0:T(8,128)(2,1)}) custom-call(f32[2]{0:T(128)S(1)} %pad_maximum_fusion.2.scale_ref, s32[1]{0:T(128)} %bitcast.place_ref, bf16[768,768]{1,0:T(8,128)(2,1)S(1)} %get-tuple-element.13.weights, bf16[768,640]{1,0:T(8,128)(2,1)S(1)} %get-tuple-element.11.texts, ...), custom_call_target="tpu_custom_call" | custom-call | bytes 4194304 | tf_op jit(solution)/shard_map/image_grads/pallas_call | solution.py:68
  75.5 5.2 %collective-permute-start.4 = (bf16[192,640]{1,0:T(8,128)(2,1)}, bf16[192,640]{1,0:T(8,128)(2,1)S(1)}, u32[]{:S(2)}, u32[]{:S(2)}) collective-permute-start(bf16[192,640]{1,0:T(8,128)(2,1)} %get-tuple-element.16), channel_id=1, source_target_pairs={{0,128},{64,192},{128,0},{192,64},{1,129},{65,193},{129,1},{193,65... | collective-permute-start | bytes 737288 | tf_op jit(solution)/shard_map/ppermute | solution.py:185
  80.7 2.2 %collective-permute-start.5 = (bf16[192,640]{1,0:T(8,128)(2,1)}, bf16[192,640]{1,0:T(8,128)(2,1)}, u32[]{:S(2)}, u32[]{:S(2)}) collective-permute-start(bf16[192,640]{1,0:T(8,128)(2,1)} %get-tuple-element.17), channel_id=1, source_target_pairs={{0,64},{64,128},{128,192},{192,0},{1,65},{65,129},{129,193},{193,1... | collective-permute-start | bytes 737288 | tf_op jit(solution)/shard_map/ppermute | solution.py:185
  82.9 4.3 %collective-permute-start.6 = (bf16[192,640]{1,0:T(8,128)(2,1)}, bf16[192,640]{1,0:T(8,128)(2,1)}, u32[]{:S(2)}, u32[]{:S(2)}) collective-permute-start(bf16[192,640]{1,0:T(8,128)(2,1)} %get-tuple-element.18), channel_id=1, source_target_pairs={{0,192},{64,0},{128,64},{192,128},{1,193},{65,1},{129,65},{193,129... | collective-permute-start | bytes 737288 | tf_op jit(solution)/shard_map/ppermute | solution.py:185
  87.2 0.8 all-to-all-done.1
  87.9 1.3 %text_sum.1 = bf16[192,640]{1,0:T(8,128)(2,1)S(1)} custom-call(bf16[768,640]{1,0:T(8,128)(2,1)} %bitcast.5.parts), custom_call_target="tpu_custom_call" | custom-call | bytes 4194304 | tf_op jit(solution)/shard_map/text_sum/pallas_call | solution.py:68
  89.3 5.9 %collective-permute-start.8 = (bf16[192,640]{1,0:T(8,128)(2,1)S(1)}, bf16[192,640]{1,0:T(8,128)(2,1)S(1)}, u32[]{:S(2)}, u32[]{:S(2)}) collective-permute-start(bf16[192,640]{1,0:T(8,128)(2,1)S(1)} %text_sum.1), channel_id=1, source_target_pairs={{3,0},{67,1},{131,2},{195,3},{35,4},{99,5},{163,6},{227,7},{0,32},... | collective-permute-start | bytes 737288 | tf_op jit(solution)/shard_map/ppermute | solution.py:189
  95.1 0.0 collective-permute-done.4.rest_0_
  95.2 0.0 collective-permute-done.5.rest_1_
  95.2 0.0 collective-permute-done.6.rest_2_
  95.2 1.5 %image_sum.1 = bf16[192,640]{1,0:T(8,128)(2,1)S(1)} custom-call(f32[2]{0:T(128)S(1)} %pad_maximum_fusion.2.scale_ref, s32[1]{0:T(128)} %bitcast.place_ref, bf16[768,768]{1,0:T(8,128)(2,1)S(1)} %get-tuple-element.13.weights, bf16[768,640]{1,0:T(8,128)(2,1)S(1)} %get-tuple-element.11.texts, bf16[768,640]{1,0:T(8,128)(2,1)S(1)} %collective-permute-done.3.received, ...), custom_call_target="tpu_custom_call" | custom-call | bytes 4194304 | tf_op jit(solution)/shard_map/image_sum/pallas_call | solution.py:68
  96.7 2.4 %collective-permute-start.7 = (bf16[192,640]{1,0:T(8,128)(2,1)S(1)}, bf16[192,640]{1,0:T(8,128)(2,1)S(1)}, u32[]{:S(2)}, u32[]{:S(2)}) collective-permute-start(bf16[192,640]{1,0:T(8,128)(2,1)S(1)} %image_sum.1), channel_id=1, source_target_pairs={{7,0},{71,1},{135,2},{199,3},{39,4},{103,5},{167,6},{231,7},{3,32}... | collective-permute-start | bytes 737288 | tf_op jit(solution)/shard_map/ppermute | solution.py:187
  99.1 13.0 %collective-permute-done.8 = bf16[192,640]{1,0:T(8,128)(2,1)S(1)} collective-permute-done((bf16[192,640]{1,0:T(8,128)(2,1)S(1)}, bf16[192,640]{1,0:T(8,128)(2,1)S(1)}, u32[]{:S(2)}, u32[]{:S(2)}) %collective-permute-start.8) | collective-permute-done | bytes 245792 | tf_op jit(solution)/shard_map/ppermute | solution.py:189
  112.1 0.8 convert_element_type.14
  112.9 9.8 %collective-permute-done.7 = bf16[192,640]{1,0:T(8,128)(2,1)S(1)} collective-permute-done((bf16[192,640]{1,0:T(8,128)(2,1)S(1)}, bf16[192,640]{1,0:T(8,128)(2,1)S(1)}, u32[]{:S(2)}, u32[]{:S(2)}) %collective-permute-start.7) | collective-permute-done | bytes 245792 | tf_op jit(solution)/shard_map/ppermute | solution.py:187
  122.7 0.7 copy.11
  (4 shorter events, 0.0 us)
Async XLA Ops:
  2.3 17.1 %collective-permute-start = (bf16[200,640]{1,0:T(8,128)(2,1)S(1)}, bf16[200,640]{1,0:T(8,128)(2,1)S(1)}, u32[]{:S(2)}, u32[]{:S(2)}) collective-permute-start(bf16[200,640]{1,0:T(8,128)(2,1)S(1)} %pad_maximum_fusion), channel_id=1, source_target_pairs={{0,7},{1,71},{2,135},{3,199},{4,39},{5,103},{6,167},{7,231},{32,3}... | collective-permute-start | bytes 768008 | tf_op jit(solution)/shard_map/ppermute | solution.py:165
  7.3 37.8 %collective-permute-start.1 = (bf16[200,640]{1,0:T(8,128)(2,1)S(1)}, bf16[200,640]{1,0:T(8,128)(2,1)S(1)}, u32[]{:S(2)}, u32[]{:S(2)}) collective-permute-start(bf16[200,640]{1,0:T(8,128)(2,1)S(1)} %pad_maximum_fusion.1), channel_id=1, source_target_pairs={{0,3},{1,67},{2,131},{3,195},{4,35},{5,99},{6,163},{7,227},{32,0},... | collective-permute-start | bytes 768008 | tf_op jit(solution)/shard_map/ppermute | solution.py:166
  20.5 36.9 %all-to-all-start = ((bf16[4,200,640]{2,1,0:T(8,128)(2,1)}), bf16[4,200,640]{2,1,0:T(8,128)(2,1)S(1)}, u32[]{:S(2)}, u32[]{:S(2)}) async-start(bf16[4,200,640]{2,1,0:T(8,128)(2,1)} %broadcast_in_dim.24), calls=%async_computation | async-start | bytes 2048000 | tf_op jit(solution)/shard_map/all_to_all | solution.py:167
  57.4 4.7 %collective-permute-start.2 = (bf16[4,200,640]{2,1,0:T(8,128)(2,1)S(1)}, bf16[4,200,640]{2,1,0:T(8,128)(2,1)S(1)}, u32[]{:S(2)}, u32[]{:S(2)}) collective-permute-start(bf16[4,200,640]{2,1,0:T(8,128)(2,1)S(1)} %all-to-all-done.image_ref), channel_id=1, source_target_pairs={{0,32},{32,0},{1,33},{33,1},{2,34},{34,2},{3,35},{35,3},{4,36},{36... | collective-permute-start | bytes 3072008 | tf_op jit(solution)/shard_map/ppermute | solution.py:168
  65.7 1.0 copy-start
  66.7 6.7 %collective-permute-start.3 = (bf16[768,640]{1,0:T(8,128)(2,1)}, bf16[768,640]{1,0:T(8,128)(2,1)S(1)}, u32[]{:S(2)}, u32[]{:S(2)}) collective-permute-start(bf16[768,640]{1,0:T(8,128)(2,1)} %get-tuple-element.15), channel_id=1, source_target_pairs={{0,32},{32,0},{1,33},{33,1},{2,34},{34,2},{3,35},{35,3},{4,36},{36... | collective-permute-start | bytes 2949128 | tf_op jit(solution)/shard_map/ppermute | solution.py:181
  69.1 18.9 %all-to-all-start.1 = ((bf16[4,192,640]{2,1,0:T(8,128)(2,1)}), bf16[4,192,640]{2,1,0:T(8,128)(2,1)}, u32[]{:S(2)}, u32[]{:S(2)}) async-start(bf16[4,192,640]{2,1,0:T(8,128)(2,1)} %bitcast.7), calls=%async_computation.1 | async-start | bytes 1966080 | tf_op jit(solution)/shard_map/all_to_all | solution.py:182
  75.5 19.7 %collective-permute-start.4 = (bf16[192,640]{1,0:T(8,128)(2,1)}, bf16[192,640]{1,0:T(8,128)(2,1)S(1)}, u32[]{:S(2)}, u32[]{:S(2)}) collective-permute-start(bf16[192,640]{1,0:T(8,128)(2,1)} %get-tuple-element.16), channel_id=1, source_target_pairs={{0,128},{64,192},{128,0},{192,64},{1,129},{65,193},{129,1},{193,65... | collective-permute-start | bytes 737288 | tf_op jit(solution)/shard_map/ppermute | solution.py:185
  80.7 14.5 %collective-permute-start.5 = (bf16[192,640]{1,0:T(8,128)(2,1)}, bf16[192,640]{1,0:T(8,128)(2,1)}, u32[]{:S(2)}, u32[]{:S(2)}) collective-permute-start(bf16[192,640]{1,0:T(8,128)(2,1)} %get-tuple-element.17), channel_id=1, source_target_pairs={{0,64},{64,128},{128,192},{192,0},{1,65},{65,129},{129,193},{193,1... | collective-permute-start | bytes 737288 | tf_op jit(solution)/shard_map/ppermute | solution.py:185
  82.9 12.3 %collective-permute-start.6 = (bf16[192,640]{1,0:T(8,128)(2,1)}, bf16[192,640]{1,0:T(8,128)(2,1)}, u32[]{:S(2)}, u32[]{:S(2)}) collective-permute-start(bf16[192,640]{1,0:T(8,128)(2,1)} %get-tuple-element.18), channel_id=1, source_target_pairs={{0,192},{64,0},{128,64},{192,128},{1,193},{65,1},{129,65},{193,129... | collective-permute-start | bytes 737288 | tf_op jit(solution)/shard_map/ppermute | solution.py:185
  89.3 22.9 %collective-permute-start.8 = (bf16[192,640]{1,0:T(8,128)(2,1)S(1)}, bf16[192,640]{1,0:T(8,128)(2,1)S(1)}, u32[]{:S(2)}, u32[]{:S(2)}) collective-permute-start(bf16[192,640]{1,0:T(8,128)(2,1)S(1)} %text_sum.1), channel_id=1, source_target_pairs={{3,0},{67,1},{131,2},{195,3},{35,4},{99,5},{163,6},{227,7},{0,32},... | collective-permute-start | bytes 737288 | tf_op jit(solution)/shard_map/ppermute | solution.py:189
  96.7 26.0 %collective-permute-start.7 = (bf16[192,640]{1,0:T(8,128)(2,1)S(1)}, bf16[192,640]{1,0:T(8,128)(2,1)S(1)}, u32[]{:S(2)}, u32[]{:S(2)}) collective-permute-start(bf16[192,640]{1,0:T(8,128)(2,1)S(1)} %image_sum.1), channel_id=1, source_target_pairs={{7,0},{71,1},{135,2},{199,3},{39,4},{103,5},{167,6},{231,7},{3,32}... | collective-permute-start | bytes 737288 | tf_op jit(solution)/shard_map/ppermute | solution.py:187
